TPU v7x, 512 devices: a whole 4x8x8 slice. The times are simulated.
512 devices in a mesh: mesh: 128 (over z, x, y_hi), field: 4 (over y_lo, core).
Axes of the slice: x: 4, y: 8 (y_hi: 4, y_lo: 2; y = y_hi * 2 + y_lo), z: 8, core: 2. Of those that a mesh axis runs over, the one named last changes fastest.
Arguments:
- velocity: float32 [3, 512, 1024], P(None, ('mesh', 'field')), may hold values from -4 to 4
- pressure: float32 [512, 1024], P(('mesh', 'field')), may hold values from -128 to 128
- fields: bfloat16 [3, 256, 512, 1024], P(None, 'field', 'mesh'), may hold values from -1.8 to 1.8
- brownian: bfloat16 [3, 256, 512, 1024], P(None, 'field', 'mesh'), may hold values from -4 to 4
Outputs:
- new_fields: bfloat16 [3, 256, 512, 1024], P(None, 'field', 'mesh')
- new_velocity: float32 [3, 512, 1024], P(None, ('mesh', 'field'))
All inputs are finite; a program needn't handle non-finite values.
Results may differ from a plain program's by a relative error of at most 0.001.
Values sent between devices are 32-bit elements; how exact they have to be, the bound alone decides.
No kernel may reach another device: no remote copies, remote signals or barrier semaphores. Data moves between devices by JAX's collectives and lax.ppermute only.
A program may use at most 64 MiB of HBM per device.

v0:
```python
import jax
import jax.numpy as jnp
from jax import lax
from jax.sharding import PartitionSpec as P

NF = 256
NY = 32
NZ = 32
SWEEPS = 4


time_step = 0.02
axial_weight = 400.0
transverse_weight = 40.0
weissenberg = 0.5
max_stretch = 50.0
polymer_viscosity = 40.0
noise_scale = (0.02 / 0.5) ** 0.5
diagonal_weight = 1.0 / 0.02 + 2.0 * 400.0 + 4.0 * 40.0
index_table = ((0, 1, 2), (1, 3, 4), (2, 4, 5))
component_pairs = ((0, 0), (0, 1), (0, 2), (1, 1), (1, 2), (2, 2))


def extended(array, sides, width):
    edges = {}
    for axis, dim in sides:
        count, length = (lax.axis_size(axis), array.shape[dim])
        up = [(i, (i + 1) % count) for i in range(count - 1)]
        last = lax.slice_in_dim(array, length - width, length, axis=dim)
        first = lax.slice_in_dim(array, 0, width, axis=dim)
        edges[dim] = (
            lax.ppermute(last, axis, up),
            lax.ppermute(first, axis, [(b, a) for a, b in up]),
        )
    done = []
    for _, dim in sides:
        low, high = edges[dim]
        around = [(width, width) if d in done else (0, 0) for d in range(array.ndim)]
        array = jnp.concatenate([jnp.pad(low, around), array, jnp.pad(high, around)], axis=dim)
        done.append(dim)
    return array


def cut_along(array, dim, count):
    lengths = array.shape
    pieces = array.reshape(*lengths[:dim], count, lengths[dim] // count, *lengths[dim + 1 :])
    return jnp.moveaxis(pieces, dim, 0)


def sum_at_owner(array, axis, dim):
    count = lax.axis_size(axis)
    pieces = lax.all_to_all(cut_along(array, dim, count), axis, 0, 0, tiled=True)
    return jnp.sum(pieces, axis=0)


def plane_shifts(values):
    extent = values.shape[-1]
    leading = [(0, 0)] * (values.ndim - 1)
    along_y = jnp.pad(values, leading + [(NZ, NZ)])
    along_z = jnp.pad(values, leading + [(1, 1)])
    column = lax.broadcasted_iota(jnp.int32, (extent,), 0) % NZ
    upper_keep = (column < NZ - 1).astype(values.dtype)
    lower_keep = (column > 0).astype(values.dtype)
    return (
        along_y[..., 2 * NZ :],
        along_y[..., :extent],
        along_z[..., 2:] * upper_keep,
        along_z[..., :extent] * lower_keep,
    )


def derivatives(padded):
    interior = padded[:, 1:-1]
    y_plus, y_minus, z_plus, z_minus = plane_shifts(interior)
    return (
        (padded[:, 2:] - padded[:, :-2]) * 0.5,
        (y_plus - y_minus) * 0.5,
        (z_plus - z_minus) * 0.5,
    )


def velocity_gradient(padded):
    stacked = jnp.stack(derivatives(padded), axis=1)
    return stacked.reshape(9, stacked.shape[2], stacked.shape[3])


def advance(fields, brownian, gradient):
    current = fields.astype(jnp.float32)
    increments = brownian.astype(jnp.float32)
    length_sq = current[0] * current[0] + current[1] * current[1] + current[2] * current[2]
    spring = 1.0 / (1.0 - length_sq / max_stretch)
    drift_terms = []
    for out_axis in range(3):
        stretch = (
            gradient[3 * out_axis][None] * current[0]
            + gradient[3 * out_axis + 1][None] * current[1]
            + gradient[3 * out_axis + 2][None] * current[2]
        )
        drift_terms.append(stretch - spring * current[out_axis] / (2.0 * weissenberg))
    advanced = current + time_step * jnp.stack(drift_terms) + noise_scale * increments
    new_sq = advanced[0] * advanced[0] + advanced[1] * advanced[1] + advanced[2] * advanced[2]
    new_spring = 1.0 / (1.0 - new_sq / max_stretch)
    partial_value = jnp.stack(
        [
            jnp.sum(new_spring * advanced[left_axis] * advanced[right_axis], axis=0)
            for left_axis, right_axis in component_pairs
        ]
    )
    return (advanced.astype(jnp.bfloat16), partial_value)


def to_stress(summed):
    identity = jnp.array([1.0, 0.0, 0.0, 1.0, 0.0, 1.0], dtype=summed.dtype)[:, None, None]
    return polymer_viscosity / weissenberg * (summed / NF - identity)


def momentum_source(velocity, padded_pressure, padded_stress):
    pressure_grad = jnp.concatenate(derivatives(padded_pressure), axis=0)
    slopes = derivatives(padded_stress)
    divergence = jnp.stack(
        [
            slopes[0][index_table[out_axis][0]]
            + slopes[1][index_table[out_axis][1]]
            + slopes[2][index_table[out_axis][2]]
            for out_axis in range(3)
        ]
    )
    return velocity / time_step - pressure_grad + divergence


def fluid_mask(offset, planes, total_planes, extent):
    position = offset + lax.broadcasted_iota(jnp.int32, (planes, extent), 0)
    across = lax.broadcasted_iota(jnp.int32, (planes, extent), 1) // NZ
    blocked = (position >= total_planes // 2) & ((across < NY // 4) | (across >= NY - NY // 4))
    return jnp.where(blocked, 0.0, 1.0).astype(jnp.float32)


def relax_step(padded, source, fluid):
    interior = padded[:, 1:-1]
    y_plus, y_minus, z_plus, z_minus = plane_shifts(interior)
    along_flow = padded[:, 2:] + padded[:, :-2]
    across_flow = y_plus + y_minus + z_plus + z_minus
    return (
        fluid
        * (source + axial_weight * along_flow + transverse_weight * across_flow)
        / diagonal_weight
    )


def body(velocity, pressure, fields, brownian):
    planes = velocity.shape[1]
    extent = velocity.shape[2]
    groups = lax.axis_size("field")
    total_planes = planes * groups * lax.axis_size("mesh")
    stacked = jnp.concatenate([velocity, pressure[None]], axis=0)
    padded = extended(stacked, ((("mesh", "field"), 1),), 1)
    gradient = lax.all_gather(velocity_gradient(padded[:3]), "field", axis=1, tiled=True)
    new_fields, partial_value = advance(fields, brownian, gradient)
    portion = sum_at_owner(partial_value, "field", 1)
    stress = to_stress(portion)
    padded_stress = extended(stress, ((("mesh", "field"), 1),), 1)
    source = momentum_source(velocity, padded[3:], padded_stress)
    offset = (lax.axis_index("mesh") * groups + lax.axis_index("field")) * planes
    fluid = fluid_mask(offset, planes, total_planes, extent)

    def sweep_slab(repeat, current):
        with_rim = extended(current, ((("mesh", "field"), 1),), 1)
        return relax_step(with_rim, source, fluid)

    new_velocity = lax.fori_loop(0, SWEEPS, sweep_slab, velocity)
    return (new_fields, new_velocity)


def solution(mesh):
    placed = (
        P(None, ("mesh", "field"), None),
        P(("mesh", "field"), None),
        P(None, "field", "mesh", None),
        P(None, "field", "mesh", None),
    )
    return jax.shard_map(
        body,
        mesh=mesh,
        in_specs=placed,
        out_specs=(P(None, "field", "mesh", None), P(None, ("mesh", "field"), None)),
        check_vma=False,
    )
```

profile of v0, /device:TPU:255, one launch (start us, length us, event | category | flops | bytes accessed | tf_op | source)
XLA Modules:
  0.0 105.8 jit_solution(16889571252351092093)
XLA Ops:
  0.6 0.7 copy.53
  1.3 0.7 pad_maximum_fusion.1
  2.0 4.9 %collective-permute-start.3 = (f32[4,1,1024]{2,1,0:T(1,128)S(1)}, f32[4,1,1024]{2,1,0:T(1,128)S(1)}, u32[]{:S(2)}, u32[]{:S(2)}) collective-permute-start(f32[4,1,1024]{2,1,0:T(1,128)S(1)} %pad_maximum_fusion.1), channel_id=1, source_target_pairs={{0,1},{1,2},{2,3},{3,4},{4,5},{5,6},{6,7},{7,8},{8,9},{9,10},{10,1... | collective-permute-start | bytes 49160 | tf_op jit(solution)/shard_map/ppermute | solution.py:32
  6.9 1.9 %collective-permute-start.2 = (f32[4,1,1024]{2,1,0:T(1,128)S(1)}, f32[4,1,1024]{2,1,0:T(1,128)S(1)}, u32[]{:S(2)}, u32[]{:S(2)}) collective-permute-start(f32[4,1,1024]{2,1,0:T(1,128)S(1)} %pad_maximum_fusion.1), channel_id=1, source_target_pairs={{1,0},{2,1},{3,2},{4,3},{5,4},{6,5},{7,6},{8,7},{9,8},{10,9},{11,1... | collective-permute-start | bytes 49160 | tf_op jit(solution)/shard_map/ppermute | solution.py:33
  8.9 0.2 multiply_bitcast_fusion.1
  9.1 0.9 subtract_multiply_fusion.3
  10.0 2.3 %convert_element_type.67 = f32[3,64,4,1024]{3,2,1,0:T(4,128)S(1)} convert(bf16[3,64,4,1024]{3,2,1,0:T(4,128)(2,1)} %param.9) | non-fusion elementwise | flops 786432 | bytes 4718592 | tf_op jit(solution)/shard_map/convert_element_type | solution.py:88
  12.4 5.1 %collective-permute-done.2 = f32[4,1,1024]{2,1,0:T(1,128)S(1)} collective-permute-done((f32[4,1,1024]{2,1,0:T(1,128)S(1)}, f32[4,1,1024]{2,1,0:T(1,128)S(1)}, u32[]{:S(2)}, u32[]{:S(2)}) %collective-permute-start.2) | collective-permute-done | bytes 16416 | tf_op jit(solution)/shard_map/ppermute | solution.py:33
  17.5 4.6 %all_gather.3 = f32[9,4,1024]{2,0,1:T(8,128)S(1)} all-gather(f32[9,1,1024]{2,0,1:T(8,128)S(1)} %reshape.221), channel_id=1, replica_groups=mesh['mesh'=128,'field'=4] {'field'}, dimensions={1}, use_global_device_ids=true | all-gather | bytes 184320 | tf_op jit(solution)/shard_map/all_gather | solution.py:157
  22.2 0.1 fusion.28
  22.4 1.0 multiply_subtract_fusion.2
  23.4 0.0 copy-start
  23.4 0.0 copy-start.1
  23.4 1.1 %multiply_subtract_fusion.1 = (f32[1,64,4,1024]{3,2,1,0:T(4,128)S(1)}, f32[1,64,4,1024]{3,2,1,0:T(4,128)S(1)}) fusion(f32[1,64,4,1024]{3,2,1,0:T(4,128)S(1)} %get-tuple-element.86, f32[3,64,4,1024]{3,2,1,0:T(4,128)S(1)} %convert_element_type.67, f32[4,1024]{1,0:T(4,128)S(1)} %bitcast.94, f32[4,1024]{1,0:T(4,128)S(1)} %bitcast.95, f32[4,1024]{1,0:T(4,128)S(1)} %bitcast.90, ...), kind=kLoop, calls=%fused_computation.31 | loop fusion | flops 3670016 | bytes 6389760 | tf_op jit(solution)/shard_map/sub | solution.py:99
  24.6 0.3 copy-done
  24.8 0.5 copy-done.1
  25.3 3.0 %fusion.26 = (bf16[3,64,4,1024]{3,2,1,0:T(4,128)(2,1)}, f32[3,64,4,1024]{3,2,1,0:T(4,128)S(1)}) fusion(bf16[3,64,4,1024]{3,2,1,0:T(4,128)(2,1)S(1)} %copy-done.1, f32[1,64,4,1024]{3,2,1,0:T(4,128)S(1)} %get-tuple-element.90, f32[1,64,4,1024]{3,2,1,0:T(4,128)S(1)} %get-tuple-element.89, f32[1,64,4,1024]{3,2,1,0:T(4,128)S(1)} %get-tuple-element.85, ...), kind=kLoop, calls=%fused_computation.87 | loop fusion | flops 7077888 | bytes 11010048 | tf_op jit(solution)/shard_map/convert_element_type | solution.py:109
  28.3 2.0 %fusion.11 = (f32[4,1024]{1,0:T(4,128)S(1)}, f32[4,1024]{1,0:T(4,128)S(1)}, f32[4,1024]{1,0:T(4,128)S(1)}, f32[4,1024]{1,0:T(4,128)S(1)}, f32[4,1024]{1,0:T(4,128)S(1)}, /*index=5*/f32[4,1024]{1,0:T(4,128)S(1)}) fusion(f32[3,64,4,1024]{3,2,1,0:T(4,128)S(1)} %get-tuple-element.84), kind=kLoop, calls=%fused_computation.20 | loop fusion | flops 6004736 | bytes 3244032 | tf_op jit(solution)/shard_map/reduce_sum | solution.py:105
  30.5 0.7 copy.11
  31.2 4.6 %all-to-all-start = ((f32[4,6,1,1024]{3,2,1,0:T(1,128)}), f32[4,6,1,1024]{3,2,1,0:T(1,128)S(1)}, u32[]{:S(2)}, u32[]{:S(2)}) async-start(f32[4,6,1,1024]{3,2,1,0:T(1,128)} %copy.11), calls=%async_computation | async-start | bytes 196608 | tf_op jit(solution)/shard_map/all_to_all | solution.py:52
  35.8 2.4 %all-to-all-done = f32[4,6,1,1024]{3,2,1,0:T(1,128)S(1)} async-done(((f32[4,6,1,1024]{3,2,1,0:T(1,128)}), f32[4,6,1,1024]{3,2,1,0:T(1,128)S(1)}, u32[]{:S(2)}, u32[]{:S(2)}) %all-to-all-start) | async-done | bytes 98336 | tf_op jit(solution)/shard_map/all_to_all | solution.py:52
  38.1 0.1 reduce_sum.69
  38.3 0.1 add_multiply_fusion
  38.4 5.8 %collective-permute-start.5 = (f32[6,1,1024]{2,1,0:T(1,128)S(1)}, f32[6,1,1024]{2,1,0:T(1,128)S(1)}, u32[]{:S(2)}, u32[]{:S(2)}) collective-permute-start(f32[6,1,1024]{2,1,0:T(1,128)S(1)} %add_multiply_fusion), channel_id=1, source_target_pairs={{0,1},{1,2},{2,3},{3,4},{4,5},{5,6},{6,7},{7,8},{8,9},{9,10},{10,1... | collective-permute-start | bytes 73736 | tf_op jit(solution)/shard_map/ppermute | solution.py:32
  44.1 1.9 %collective-permute-start.4 = (f32[6,1,1024]{2,1,0:T(1,128)S(1)}, f32[6,1,1024]{2,1,0:T(1,128)S(1)}, u32[]{:S(2)}, u32[]{:S(2)}) collective-permute-start(f32[6,1,1024]{2,1,0:T(1,128)S(1)} %add_multiply_fusion), channel_id=1, source_target_pairs={{1,0},{2,1},{3,2},{4,3},{5,4},{6,5},{7,6},{8,7},{9,8},{10,9},{11,1... | collective-permute-start | bytes 73736 | tf_op jit(solution)/shard_map/ppermute | solution.py:33
  46.1 0.3 subtract_multiply_fusion.1
  46.4 8.4 %collective-permute-done.4 = f32[6,1,1024]{2,1,0:T(1,128)S(1)} collective-permute-done((f32[6,1,1024]{2,1,0:T(1,128)S(1)}, f32[6,1,1024]{2,1,0:T(1,128)S(1)}, u32[]{:S(2)}, u32[]{:S(2)}) %collective-permute-start.4) | collective-permute-done | bytes 24608 | tf_op jit(solution)/shard_map/ppermute | solution.py:33
  54.8 50.4 %while.13 = (s32[]{:T(128)}, f32[3,1,1024]{2,1,0:T(1,128)S(1)}, f32[3,1,1024]{2,1,0:T(1,128)S(1)}, pred[]{:T(512)}, s32[]{:T(128)}) while((s32[]{:T(128)}, f32[3,1,1024]{2,1,0:T(1,128)S(1)}, f32[3,1,1024]{2,1,0:T(1,128)S(1)}, pred[]{:T(512)}, s32[]{:T(128)}) %tuple.58), condition=%wide.region_8.9_spmd.clone, body=%wide.region_7.8_spmd.clone.sunk | while | flops 60418 | bytes 209038 | solution.py:170
  54.8 1.9 %collective-permute-start.1 = (f32[3,1,1024]{2,1,0:T(1,128)S(1)}, f32[3,1,1024]{2,1,0:T(1,128)S(1)}, u32[]{:S(2)}, u32[]{:S(2)}) collective-permute-start(f32[3,1,1024]{2,1,0:T(1,128)S(1)} %copy.52), channel_id=1, source_target_pairs={{0,1},{1,2},{2,3},{3,4},{4,5},{5,6},{6,7},{7,8},{8,9},{9,10},{10,1... | collective-permute-start | bytes 36872 | tf_op jit(solution)/shard_map/while/body/eval_jaxpr/ppermute | solution.py:32
  56.8 2.4 %collective-permute-start = (f32[3,1,1024]{2,1,0:T(1,128)S(1)}, f32[3,1,1024]{2,1,0:T(1,128)S(1)}, u32[]{:S(2)}, u32[]{:S(2)}) collective-permute-start(f32[3,1,1024]{2,1,0:T(1,128)S(1)} %copy.52), channel_id=1, source_target_pairs={{1,0},{2,1},{3,2},{4,3},{5,4},{6,5},{7,6},{8,7},{9,8},{10,9},{11,1... | collective-permute-start | bytes 36872 | tf_op jit(solution)/shard_map/while/body/eval_jaxpr/ppermute | solution.py:33
  59.2 0.0 collective-permute-done.1
  59.2 8.0 %collective-permute-done = f32[3,1,1024]{2,1,0:T(1,128)S(1)} collective-permute-done((f32[3,1,1024]{2,1,0:T(1,128)S(1)}, f32[3,1,1024]{2,1,0:T(1,128)S(1)}, u32[]{:S(2)}, u32[]{:S(2)}) %collective-permute-start) | collective-permute-done | bytes 12320 | tf_op jit(solution)/shard_map/while/body/eval_jaxpr/ppermute | solution.py:33
  67.2 0.2 multiply_multiply_fusion.3
  67.4 1.9 %collective-permute-start.1 = (f32[3,1,1024]{2,1,0:T(1,128)S(1)}, f32[3,1,1024]{2,1,0:T(1,128)S(1)}, u32[]{:S(2)}, u32[]{:S(2)}) collective-permute-start(f32[3,1,1024]{2,1,0:T(1,128)S(1)} %copy.52), channel_id=1, source_target_pairs={{0,1},{1,2},{2,3},{3,4},{4,5},{5,6},{6,7},{7,8},{8,9},{9,10},{10,1... | collective-permute-start | bytes 36872 | tf_op jit(solution)/shard_map/while/body/eval_jaxpr/ppermute | solution.py:32
  69.4 2.4 %collective-permute-start = (f32[3,1,1024]{2,1,0:T(1,128)S(1)}, f32[3,1,1024]{2,1,0:T(1,128)S(1)}, u32[]{:S(2)}, u32[]{:S(2)}) collective-permute-start(f32[3,1,1024]{2,1,0:T(1,128)S(1)} %copy.52), channel_id=1, source_target_pairs={{1,0},{2,1},{3,2},{4,3},{5,4},{6,5},{7,6},{8,7},{9,8},{10,9},{11,1... | collective-permute-start | bytes 36872 | tf_op jit(solution)/shard_map/while/body/eval_jaxpr/ppermute | solution.py:33
  71.8 8.0 %collective-permute-done = f32[3,1,1024]{2,1,0:T(1,128)S(1)} collective-permute-done((f32[3,1,1024]{2,1,0:T(1,128)S(1)}, f32[3,1,1024]{2,1,0:T(1,128)S(1)}, u32[]{:S(2)}, u32[]{:S(2)}) %collective-permute-start) | collective-permute-done | bytes 12320 | tf_op jit(solution)/shard_map/while/body/eval_jaxpr/ppermute | solution.py:33
  79.8 0.2 multiply_multiply_fusion.3
  80.0 1.9 %collective-permute-start.1 = (f32[3,1,1024]{2,1,0:T(1,128)S(1)}, f32[3,1,1024]{2,1,0:T(1,128)S(1)}, u32[]{:S(2)}, u32[]{:S(2)}) collective-permute-start(f32[3,1,1024]{2,1,0:T(1,128)S(1)} %copy.52), channel_id=1, source_target_pairs={{0,1},{1,2},{2,3},{3,4},{4,5},{5,6},{6,7},{7,8},{8,9},{9,10},{10,1... | collective-permute-start | bytes 36872 | tf_op jit(solution)/shard_map/while/body/eval_jaxpr/ppermute | solution.py:32
  82.0 2.4 %collective-permute-start = (f32[3,1,1024]{2,1,0:T(1,128)S(1)}, f32[3,1,1024]{2,1,0:T(1,128)S(1)}, u32[]{:S(2)}, u32[]{:S(2)}) collective-permute-start(f32[3,1,1024]{2,1,0:T(1,128)S(1)} %copy.52), channel_id=1, source_target_pairs={{1,0},{2,1},{3,2},{4,3},{5,4},{6,5},{7,6},{8,7},{9,8},{10,9},{11,1... | collective-permute-start | bytes 36872 | tf_op jit(solution)/shard_map/while/body/eval_jaxpr/ppermute | solution.py:33
  84.4 0.0 collective-permute-done.1
  84.4 8.0 %collective-permute-done = f32[3,1,1024]{2,1,0:T(1,128)S(1)} collective-permute-done((f32[3,1,1024]{2,1,0:T(1,128)S(1)}, f32[3,1,1024]{2,1,0:T(1,128)S(1)}, u32[]{:S(2)}, u32[]{:S(2)}) %collective-permute-start) | collective-permute-done | bytes 12320 | tf_op jit(solution)/shard_map/while/body/eval_jaxpr/ppermute | solution.py:33
  92.4 0.2 multiply_multiply_fusion.3
  92.6 1.9 %collective-permute-start.1 = (f32[3,1,1024]{2,1,0:T(1,128)S(1)}, f32[3,1,1024]{2,1,0:T(1,128)S(1)}, u32[]{:S(2)}, u32[]{:S(2)}) collective-permute-start(f32[3,1,1024]{2,1,0:T(1,128)S(1)} %copy.52), channel_id=1, source_target_pairs={{0,1},{1,2},{2,3},{3,4},{4,5},{5,6},{6,7},{7,8},{8,9},{9,10},{10,1... | collective-permute-start | bytes 36872 | tf_op jit(solution)/shard_map/while/body/eval_jaxpr/ppermute | solution.py:32
  94.6 2.4 %collective-permute-start = (f32[3,1,1024]{2,1,0:T(1,128)S(1)}, f32[3,1,1024]{2,1,0:T(1,128)S(1)}, u32[]{:S(2)}, u32[]{:S(2)}) collective-permute-start(f32[3,1,1024]{2,1,0:T(1,128)S(1)} %copy.52), channel_id=1, source_target_pairs={{1,0},{2,1},{3,2},{4,3},{5,4},{6,5},{7,6},{8,7},{9,8},{10,9},{11,1... | collective-permute-start | bytes 36872 | tf_op jit(solution)/shard_map/while/body/eval_jaxpr/ppermute | solution.py:33
  97.0 8.0 %collective-permute-done = f32[3,1,1024]{2,1,0:T(1,128)S(1)} collective-permute-done((f32[3,1,1024]{2,1,0:T(1,128)S(1)}, f32[3,1,1024]{2,1,0:T(1,128)S(1)}, u32[]{:S(2)}, u32[]{:S(2)}) %collective-permute-start) | collective-permute-done | bytes 12320 | tf_op jit(solution)/shard_map/while/body/eval_jaxpr/ppermute | solution.py:33
  105.0 0.2 multiply_multiply_fusion.3
  105.2 0.0 copy-start.2
  105.2 0.6 copy-done.2
  (42 shorter events, 0.4 us)
Async XLA Ops:
  2.0 10.3 %collective-permute-start.3 = (f32[4,1,1024]{2,1,0:T(1,128)S(1)}, f32[4,1,1024]{2,1,0:T(1,128)S(1)}, u32[]{:S(2)}, u32[]{:S(2)}) collective-permute-start(f32[4,1,1024]{2,1,0:T(1,128)S(1)} %pad_maximum_fusion.1), channel_id=1, source_target_pairs={{0,1},{1,2},{2,3},{3,4},{4,5},{5,6},{6,7},{7,8},{8,9},{9,10},{10,1... | collective-permute-start | bytes 49160 | tf_op jit(solution)/shard_map/ppermute | solution.py:32
  6.9 10.5 %collective-permute-start.2 = (f32[4,1,1024]{2,1,0:T(1,128)S(1)}, f32[4,1,1024]{2,1,0:T(1,128)S(1)}, u32[]{:S(2)}, u32[]{:S(2)}) collective-permute-start(f32[4,1,1024]{2,1,0:T(1,128)S(1)} %pad_maximum_fusion.1), channel_id=1, source_target_pairs={{1,0},{2,1},{3,2},{4,3},{5,4},{6,5},{7,6},{8,7},{9,8},{10,9},{11,1... | collective-permute-start | bytes 49160 | tf_op jit(solution)/shard_map/ppermute | solution.py:33
  23.4 1.4 %copy-start = (bf16[3,64,4,1024]{3,2,1,0:T(4,128)(2,1)S(1)}, bf16[3,64,4,1024]{3,2,1,0:T(4,128)(2,1)}, u32[]{:S(2)}) copy-start(bf16[3,64,4,1024]{3,2,1,0:T(4,128)(2,1)} %param.9) | copy-start | bytes 4718596
  23.4 1.9 %copy-start.1 = (bf16[3,64,4,1024]{3,2,1,0:T(4,128)(2,1)S(1)}, bf16[3,64,4,1024]{3,2,1,0:T(4,128)(2,1)}, u32[]{:S(2)}) copy-start(bf16[3,64,4,1024]{3,2,1,0:T(4,128)(2,1)} %param.10) | copy-start | bytes 4718596
  28.3 9.9 %copy-start.3 = (f32[6]{0:T(128)S(1)}, f32[6]{0:T(128)}, u32[]{:S(2)}) copy-start(f32[6]{0:T(128)} %constant.161) | copy-start | bytes 76
  31.2 7.0 %all-to-all-start = ((f32[4,6,1,1024]{3,2,1,0:T(1,128)}), f32[4,6,1,1024]{3,2,1,0:T(1,128)S(1)}, u32[]{:S(2)}, u32[]{:S(2)}) async-start(f32[4,6,1,1024]{3,2,1,0:T(1,128)} %copy.11), calls=%async_computation | async-start | bytes 196608 | tf_op jit(solution)/shard_map/all_to_all | solution.py:52
  38.4 8.0 %collective-permute-start.5 = (f32[6,1,1024]{2,1,0:T(1,128)S(1)}, f32[6,1,1024]{2,1,0:T(1,128)S(1)}, u32[]{:S(2)}, u32[]{:S(2)}) collective-permute-start(f32[6,1,1024]{2,1,0:T(1,128)S(1)} %add_multiply_fusion), channel_id=1, source_target_pairs={{0,1},{1,2},{2,3},{3,4},{4,5},{5,6},{6,7},{7,8},{8,9},{9,10},{10,1... | collective-permute-start | bytes 73736 | tf_op jit(solution)/shard_map/ppermute | solution.py:32
  44.1 10.6 %collective-permute-start.4 = (f32[6,1,1024]{2,1,0:T(1,128)S(1)}, f32[6,1,1024]{2,1,0:T(1,128)S(1)}, u32[]{:S(2)}, u32[]{:S(2)}) collective-permute-start(f32[6,1,1024]{2,1,0:T(1,128)S(1)} %add_multiply_fusion), channel_id=1, source_target_pairs={{1,0},{2,1},{3,2},{4,3},{5,4},{6,5},{7,6},{8,7},{9,8},{10,9},{11,1... | collective-permute-start | bytes 73736 | tf_op jit(solution)/shard_map/ppermute | solution.py:33
  54.8 4.4 %collective-permute-start.1 = (f32[3,1,1024]{2,1,0:T(1,128)S(1)}, f32[3,1,1024]{2,1,0:T(1,128)S(1)}, u32[]{:S(2)}, u32[]{:S(2)}) collective-permute-start(f32[3,1,1024]{2,1,0:T(1,128)S(1)} %copy.52), channel_id=1, source_target_pairs={{0,1},{1,2},{2,3},{3,4},{4,5},{5,6},{6,7},{7,8},{8,9},{9,10},{10,1... | collective-permute-start | bytes 36872 | tf_op jit(solution)/shard_map/while/body/eval_jaxpr/ppermute | solution.py:32
  56.8 10.4 %collective-permute-start = (f32[3,1,1024]{2,1,0:T(1,128)S(1)}, f32[3,1,1024]{2,1,0:T(1,128)S(1)}, u32[]{:S(2)}, u32[]{:S(2)}) collective-permute-start(f32[3,1,1024]{2,1,0:T(1,128)S(1)} %copy.52), channel_id=1, source_target_pairs={{1,0},{2,1},{3,2},{4,3},{5,4},{6,5},{7,6},{8,7},{9,8},{10,9},{11,1... | collective-permute-start | bytes 36872 | tf_op jit(solution)/shard_map/while/body/eval_jaxpr/ppermute | solution.py:33
  67.4 4.4 %collective-permute-start.1 = (f32[3,1,1024]{2,1,0:T(1,128)S(1)}, f32[3,1,1024]{2,1,0:T(1,128)S(1)}, u32[]{:S(2)}, u32[]{:S(2)}) collective-permute-start(f32[3,1,1024]{2,1,0:T(1,128)S(1)} %copy.52), channel_id=1, source_target_pairs={{0,1},{1,2},{2,3},{3,4},{4,5},{5,6},{6,7},{7,8},{8,9},{9,10},{10,1... | collective-permute-start | bytes 36872 | tf_op jit(solution)/shard_map/while/body/eval_jaxpr/ppermute | solution.py:32
  69.4 10.4 %collective-permute-start = (f32[3,1,1024]{2,1,0:T(1,128)S(1)}, f32[3,1,1024]{2,1,0:T(1,128)S(1)}, u32[]{:S(2)}, u32[]{:S(2)}) collective-permute-start(f32[3,1,1024]{2,1,0:T(1,128)S(1)} %copy.52), channel_id=1, source_target_pairs={{1,0},{2,1},{3,2},{4,3},{5,4},{6,5},{7,6},{8,7},{9,8},{10,9},{11,1... | collective-permute-start | bytes 36872 | tf_op jit(solution)/shard_map/while/body/eval_jaxpr/ppermute | solution.py:33
  80.0 4.4 %collective-permute-start.1 = (f32[3,1,1024]{2,1,0:T(1,128)S(1)}, f32[3,1,1024]{2,1,0:T(1,128)S(1)}, u32[]{:S(2)}, u32[]{:S(2)}) collective-permute-start(f32[3,1,1024]{2,1,0:T(1,128)S(1)} %copy.52), channel_id=1, source_target_pairs={{0,1},{1,2},{2,3},{3,4},{4,5},{5,6},{6,7},{7,8},{8,9},{9,10},{10,1... | collective-permute-start | bytes 36872 | tf_op jit(solution)/shard_map/while/body/eval_jaxpr/ppermute | solution.py:32
  82.0 10.4 %collective-permute-start = (f32[3,1,1024]{2,1,0:T(1,128)S(1)}, f32[3,1,1024]{2,1,0:T(1,128)S(1)}, u32[]{:S(2)}, u32[]{:S(2)}) collective-permute-start(f32[3,1,1024]{2,1,0:T(1,128)S(1)} %copy.52), channel_id=1, source_target_pairs={{1,0},{2,1},{3,2},{4,3},{5,4},{6,5},{7,6},{8,7},{9,8},{10,9},{11,1... | collective-permute-start | bytes 36872 | tf_op jit(solution)/shard_map/while/body/eval_jaxpr/ppermute | solution.py:33
  92.6 4.4 %collective-permute-start.1 = (f32[3,1,1024]{2,1,0:T(1,128)S(1)}, f32[3,1,1024]{2,1,0:T(1,128)S(1)}, u32[]{:S(2)}, u32[]{:S(2)}) collective-permute-start(f32[3,1,1024]{2,1,0:T(1,128)S(1)} %copy.52), channel_id=1, source_target_pairs={{0,1},{1,2},{2,3},{3,4},{4,5},{5,6},{6,7},{7,8},{8,9},{9,10},{10,1... | collective-permute-start | bytes 36872 | tf_op jit(solution)/shard_map/while/body/eval_jaxpr/ppermute | solution.py:32
  94.6 10.4 %collective-permute-start = (f32[3,1,1024]{2,1,0:T(1,128)S(1)}, f32[3,1,1024]{2,1,0:T(1,128)S(1)}, u32[]{:S(2)}, u32[]{:S(2)}) collective-permute-start(f32[3,1,1024]{2,1,0:T(1,128)S(1)} %copy.52), channel_id=1, source_target_pairs={{1,0},{2,1},{3,2},{4,3},{5,4},{6,5},{7,6},{8,7},{9,8},{10,9},{11,1... | collective-permute-start | bytes 36872 | tf_op jit(solution)/shard_map/while/body/eval_jaxpr/ppermute | solution.py:33
  105.2 0.6 copy-start.2
where the time goes:
time: 107 us; the launch traced here: 106 us
  waiting for transfers between devices  47.8 us (45%)
  starting transfers between devices  36.4 us (34%)
  other arithmetic  12.7 us (12%)
  blocking collectives  4.64 us (4%)
  local copies, waits for them, and re-layouts  3.02 us (3%)
    ppermute x6, waiting for transfers between devices, extended(): lax.ppermute(first, axis, [(b, a) for a, b in up])  45.4 us
    ppermute x6, starting transfers between devices, extended(): lax.ppermute(last, axis, up)  18.4 us
    ppermute x6, starting transfers between devices, extended(): lax.ppermute(first, axis, [(b, a) for a, b in up])  13.4 us
    all_gather x1, blocking collectives, body(): lax.all_gather(velocity_gradient(padded[:3]), 'field', axis=1, tiled=True)  4.64 us
    all_to_all x1, starting transfers between devices, sum_at_owner(): lax.all_to_all(cut_along(array, dim, count), axis, 0, 0, tiled=True)  4.58 us
    convert_element_type x1, other arithmetic, advance(): return (advanced.astype(jnp.bfloat16), partial_value)  3.04 us
    all_to_all x1, waiting for transfers between devices, sum_at_owner(): lax.all_to_all(cut_along(array, dim, count), axis, 0, 0, tiled=True)  2.37 us
    convert_element_type x1, other arithmetic, advance(): current = fields.astype(jnp.float32)  2.32 us
  transfers between devices with their start and end apart: 13, of which 7 were waited for; matrix products, arithmetic and copies ran while one was open for 4% of the time, Pallas kernels for 0%

commit v1 on v0

v1 whole, which is shorter than its diff:
```python
import functools

import jax
import jax.numpy as jnp
from jax import lax
from jax.experimental import pallas as pl
from jax.experimental.pallas import tpu as pltpu
from jax.sharding import PartitionSpec as P

f32 = jnp.float32
bf16 = jnp.bfloat16

NF = 256
TIME_STEP = 0.02
AXIAL = 400.0
TRANSVERSE = 40.0
MAX_STRETCH = 50.0
VISCOSITY = 40.0
WEISSENBERG = 0.5
NOISE = (0.02 / 0.5) ** 0.5
DIAGONAL = 1.0 / 0.02 + 2.0 * 400.0 + 4.0 * 40.0
SWEEPS = 4
INDEX = ((0, 1, 2), (1, 3, 4), (2, 4, 5))
DIAGONAL_PAIRS = (0, 3, 5)

PLANES = 4
CHUNKS = 4
UNROLL = 4
AXES = ("mesh", "field")


def lane_masks():
    lane = lax.broadcasted_iota(jnp.int32, (8, 128), 1)
    row = lax.broadcasted_iota(jnp.int32, (8, 128), 0)
    return dict(
        z_hi=(lane % 32) < 31,
        z_lo=(lane % 32) > 0,
        lane_hi=lane < 96,
        lane_lo=lane >= 32,
        row_hi=row < 7,
        row_lo=row > 0,
        channel=(row >= 2) & (row < 6),
    )


def shift_z(v, masks):
    plus = jnp.where(masks["z_hi"], pltpu.roll(v, 127, 1), 0.0)
    minus = jnp.where(masks["z_lo"], pltpu.roll(v, 1, 1), 0.0)
    return plus, minus


def shift_y(v, masks):
    ahead = pltpu.roll(v, 96, 1)
    behind = pltpu.roll(v, 32, 1)
    next_row = jnp.where(masks["row_hi"], pltpu.roll(ahead, 7, 0), 0.0)
    last_row = jnp.where(masks["row_lo"], pltpu.roll(behind, 1, 0), 0.0)
    return jnp.where(masks["lane_hi"], ahead, next_row), jnp.where(masks["lane_lo"], behind, last_row)


def slope_y(v, masks):
    plus, minus = shift_y(v, masks)
    return (plus - minus) * 0.5


def slope_z(v, masks):
    plus, minus = shift_z(v, masks)
    return (plus - minus) * 0.5


def around(v, masks):
    y_plus, y_minus = shift_y(v, masks)
    z_plus, z_minus = shift_z(v, masks)
    return (y_plus + y_minus) + (z_plus + z_minus)


def advance(f, b, g):
    length_sq = f[0] * f[0] + f[1] * f[1] + f[2] * f[2]
    kept = 1.0 - (TIME_STEP * MAX_STRETCH / (2.0 * WEISSENBERG)) * pl.reciprocal(MAX_STRETCH - length_sq, approx=False)
    a = []
    for o in range(3):
        row = [g[3 * o + c] for c in range(3)]
        row[o] = row[o] + kept
        a.append(row[0] * f[0] + row[1] * f[1] + row[2] * f[2] + NOISE * b[o])
    s = [x * x for x in a]
    r = pl.reciprocal(MAX_STRETCH - (s[0] + s[1] + s[2]), approx=False)
    p0 = r * a[0]
    p1 = r * a[1]
    return a, (r * s[0], p0 * a[1], p0 * a[2], r * s[1], p1 * a[2], r * s[2])


def step_kernel(slabs, around_ref, velocity_ref, pressure_ref, f_hbm, b_hbm, nf_hbm, out_ref,
                f_buf, b_buf, n_buf, grad, sums, in_sem, out_sem):
    pairs = f_buf.shape[1]
    per = pairs // CHUNKS

    def loads(ch):
        some = pl.ds(ch * per, per)
        return [
            pltpu.make_async_copy(src.at[c, some, h], buf.at[c, some, pl.ds(4 * h, 4), :], in_sem.at[ch, 6 * w + 2 * c + h])
            for w, (src, buf) in enumerate(((f_hbm, f_buf), (b_hbm, b_buf)))
            for c in range(3)
            for h in range(2)
        ]

    def stores(ch):
        some = pl.ds(ch * per, per)
        return [
            pltpu.make_async_copy(n_buf.at[c, some, pl.ds(4 * h, 4), :], nf_hbm.at[c, some, h], out_sem.at[ch, 2 * c + h])
            for c in range(3)
            for h in range(2)
        ]

    for ch in range(CHUNKS):
        for copy in loads(ch):
            copy.start()

    slab = lax.axis_index("mesh")
    mine = lax.axis_index("field")
    masks = lane_masks()

    for q in range(PLANES):
        for a in range(3):
            centre = around_ref[q + 1, a]
            slopes = (
                (around_ref[q + 2, a] - around_ref[q, a]) * 0.5,
                slope_y(centre, masks),
                slope_z(centre, masks),
            )
            for c in range(3):
                value = slopes[c] * TIME_STEP
                grad[3 * a + c, pl.ds(q, 8, stride=8), :] = value
                grad[3 * a + c, pl.ds(q + 4, 8, stride=8), :] = value

    for ch in range(CHUNKS):
        for copy in loads(ch):
            copy.wait()

        def block(j, carry):
            rows = pl.ds(pl.multiple_of(8 * j, 8), 8)
            lanes = pl.ds(pl.multiple_of(128 * j, 128), 128)
            g = [grad[k, rows, :] for k in range(9)]

            def some_fields(i, acc):
                for u in range(UNROLL):
                    n = ch * per + i * UNROLL + u
                    f = [f_buf[c, n, :, lanes].astype(f32) for c in range(3)]
                    b = [b_buf[c, n, :, lanes].astype(f32) for c in range(3)]
                    a, products = advance(f, b, g)
                    for c in range(3):
                        n_buf[c, n, :, lanes] = a[c].astype(bf16)
                    acc = tuple(x + y for x, y in zip(acc, products))
                return acc

            if ch:
                acc = tuple(sums[k, rows, :] for k in range(6))
            else:
                acc = tuple(jnp.zeros((8, 128), f32) for _ in range(6))
            acc = lax.fori_loop(0, per // UNROLL, some_fields, acc)
            for k in range(6):
                sums[k, rows, :] = acc[k]
            return carry

        lax.fori_loop(0, 8, block, 0)
        for copy in stores(ch):
            copy.start()

    scale = VISCOSITY / WEISSENBERG / NF * MAX_STRETCH
    stress = []
    for k in range(6):
        rows = []
        for q in range(PLANES):
            total = sums[k, pl.ds(q, 8, stride=8), :] + sums[k, pl.ds(q + 4, 8, stride=8), :]
            total = total * scale
            if k in DIAGONAL_PAIRS:
                total = total - VISCOSITY / WEISSENBERG / 4
            rows.append(total)
        stress.append(rows)

    own = [mine == q for q in range(PLANES)]
    zero = jnp.zeros((8, 128), f32)
    pressure = [jnp.where(own[q], pressure_ref[...], 0.0) for q in range(PLANES)]
    start = [[jnp.where(own[q], velocity_ref[a], 0.0) for q in range(PLANES)] for a in range(3)]

    def at(values, q):
        return values[q] if 0 <= q < PLANES else None

    def add(x, y):
        return y if x is None else x if y is None else x + y

    def halfway(values, q):
        plus, minus = at(values, q + 1), at(values, q - 1)
        if plus is None:
            return None if minus is None else minus * -0.5
        return plus * 0.5 if minus is None else (plus - minus) * 0.5

    first = -(SWEEPS)
    count = PLANES + 2 * SWEEPS
    fluid = []
    for q in range(first, first + count):
        plane = slab * PLANES + q
        inside = (plane >= 0) & (plane < slabs * PLANES)
        wide = plane < slabs * PLANES // 2
        value = jnp.where(masks["channel"] | wide, 1.0 / DIAGONAL, 0.0)
        fluid.append(jnp.where(inside, value, 0.0))

    for a in range(3):
        source = {}
        for q in range(-1, PLANES + 1):
            total = halfway(stress[INDEX[a][0]], q)
            if a == 0:
                total = total - halfway(pressure, q) if total is not None else None
            if 0 <= q < PLANES:
                inner = slope_y(stress[INDEX[a][1]][q], masks) + slope_z(stress[INDEX[a][2]][q], masks)
                if a == 1:
                    inner = inner - slope_y(pressure[q], masks)
                if a == 2:
                    inner = inner - slope_z(pressure[q], masks)
                total = total + inner + start[a][q] * (1.0 / TIME_STEP)
            source[q] = total
        current = {q: start[a][q] for q in range(PLANES)}
        for sweep in range(SWEEPS):
            later = {}
            for q in range(-1 - sweep, PLANES + 1 + sweep):
                total = source.get(q)
                along = add(current.get(q - 1), current.get(q + 1))
                if along is not None:
                    total = add(total, AXIAL * along)
                if q in current:
                    total = add(total, TRANSVERSE * around(current[q], masks))
                later[q] = total * fluid[q - first]
            current = later
        for q in range(first, first + count):
            out_ref[q - first, a] = current[q]

    for ch in range(CHUNKS):
        for copy in stores(ch):
            copy.wait()


def step(planes6, velocity, pressure, fields, brownian):
    n = fields.shape[1] // 2
    split = (3, n, 2, PLANES, 1024)
    slabs = lax.axis_size("mesh")
    vmem = pl.BlockSpec(memory_space=pltpu.VMEM)
    hbm = pl.BlockSpec(memory_space=pl.ANY)
    new_fields, shares = pl.pallas_call(
        functools.partial(step_kernel, slabs),
        out_shape=(
            jax.ShapeDtypeStruct(split, bf16),
            jax.ShapeDtypeStruct((PLANES + 2 * SWEEPS, 3, 8, 128), f32),
        ),
        in_specs=[vmem, vmem, vmem, hbm, hbm],
        out_specs=[hbm, vmem],
        scratch_shapes=[
            pltpu.VMEM((3, n, 8, 1024), bf16),
            pltpu.VMEM((3, n, 8, 1024), bf16),
            pltpu.VMEM((3, n, 8, 1024), bf16),
            pltpu.VMEM((9, 64, 128), f32),
            pltpu.VMEM((6, 64, 128), f32),
            pltpu.SemaphoreType.DMA((CHUNKS, 12)),
            pltpu.SemaphoreType.DMA((CHUNKS, 6)),
        ],
        compiler_params=pltpu.CompilerParams(vmem_limit_bytes=24 << 20),
    )(planes6, velocity, pressure, fields.reshape(split), brownian.reshape(split))
    return new_fields.reshape(fields.shape), shares


def body(velocity, pressure, fields, brownian):
    slabs = lax.axis_size("mesh")
    total = slabs * 4
    slab = lax.axis_index("mesh")
    mine = lax.axis_index("field")
    low = mine < 2
    core = mine % 2
    cores = [[i, i + 1] for i in range(0, total, 2)]
    inner = [[i, i + 2] for s in range(0, total, 4) for i in (s, s + 1)]
    outer = [[i, (i + 2) % total] for s in range(2, total + 2, 4) for i in (s, s + 1)]

    def gather(x, groups):
        return lax.all_gather(x, AXES, axis=0, axis_index_groups=groups)

    def other(x, first):
        return jnp.where(first, x[1], x[0])

    own = velocity.reshape(3, 8, 128)
    near = gather(own, outer)
    near = gather(near, cores)
    left = jnp.where(slab > 0, near[1, 0], 0.0)
    right = jnp.where(slab < slabs - 1, near[0, 1], 0.0)
    send = jnp.where(
        low,
        jnp.stack([left, near[0, 1], near[1, 1]]),
        jnp.stack([near[0, 0], near[1, 0], right]),
    )
    planes6 = gather(send, inner).reshape(6, 3, 8, 128)

    new_fields, shares = step(planes6, own, pressure.reshape(8, 128), fields, brownian)

    both = gather(shares, cores).reshape(2, 3, 2, 2, 3, 8, 128)
    chip = both[0] + both[1]
    chip = jnp.where(core == 0, chip[:, :, 0], chip[:, :, 1])
    low_side = jnp.stack([chip[1, 0], chip[0, 0], chip[0, 1]])
    high_side = jnp.stack([chip[1, 1], chip[2, 0], chip[2, 1]])
    kept = jnp.where(low, low_side, high_side)
    kept = kept + other(gather(jnp.where(low, high_side, low_side), inner), low)
    arrived = other(gather(kept[1:], outer), ~low)
    mine_sum = kept[0] + jnp.where(low, arrived[0], arrived[1])
    passed = jnp.where(low, arrived[1], arrived[0])
    result = mine_sum + other(gather(passed, inner), low)
    return new_fields, result.reshape(velocity.shape)


def solution(mesh):
    placed = (
        P(None, ("mesh", "field"), None),
        P(("mesh", "field"), None),
        P(None, "field", "mesh", None),
        P(None, "field", "mesh", None),
    )
    return jax.shard_map(
        body,
        mesh=mesh,
        in_specs=placed,
        out_specs=(P(None, "field", "mesh", None), P(None, ("mesh", "field"), None)),
        check_vma=False,
    )
```

time: 107 us -> 54.6 us (0.51)
  the two profiles are of different devices: /device:TPU:255 before, /device:TPU:8 now
where the time goes in v1:
time: 54.6 us; the launch traced here: 54.3 us
  blocking collectives  42.6 us (78%)
  Pallas kernels  6.04 us (11%)
  local copies, waits for them, and re-layouts  4.23 us (8%)
  between operations  0.73 us (1%)
  other arithmetic  0.7 us (1%)
    all_gather x7, blocking collectives, gather(): return lax.all_gather(x, AXES, axis=0, axis_index_groups=groups)  42.6 us
    pallas_call x1, Pallas kernels, step(): pl.pallas_call(functools.partial(step_kernel, slabs), out_shape=(jax.Shap...  6.04 us
    unnamed x8, local copies, waits for them, and re-layouts  4.21 us

profile of v1, /device:TPU:8, one launch (start us, length us, event | category | flops | bytes accessed | tf_op | source)
XLA Modules:
  0.0 54.3 jit_solution(6035179155677364613)
XLA Ops:
  0.6 4.6 %all_gather.33 = f32[2,3,8,128]{3,2,1,0:T(8,128)S(1)} all-gather(f32[1,3,8,128]{3,2,1,0:T(8,128)} %bitcast.45), channel_id=1, replica_groups={{2,4},{3,5},{6,8},{7,9},{10,12},{11,13},{14,16},{15,17},{18,20},{19,21}..., dimensions={0}, use_global_device_ids=true | all-gather | bytes 36864 | tf_op jit(solution)/shard_map/all_gather | solution.py:280
  5.2 1.8 %all-gather = f32[4,3,8,128]{3,2,1,0:T(8,128)S(1)} all-gather(f32[2,3,8,128]{3,2,1,0:T(8,128)S(1)} %all_gather.33), channel_id=2, replica_groups={{0,1},{2,3},{4,5},{6,7},{8,9},{10,11},{12,13},{14,15},{16,17},{18,19},{..., dimensions={0}, use_global_device_ids=true | all-gather | bytes 73728 | tf_op jit(solution)/shard_map/all_gather | solution.py:280
  7.1 15.2 %all_gather.36 = f32[2,3,3,8,128]{4,3,2,1,0:T(8,128)S(1)} all-gather(f32[1,3,3,8,128]{4,3,2,1,0:T(8,128)S(1)} %maximum_select_fusion), channel_id=1, replica_groups={{0,2},{1,3},{4,6},{5,7},{8,10},{9,11},{12,14},{13,15},{16,18},{17,19},{..., dimensions={0}, use_global_device_ids=true | all-gather | bytes 110592 | tf_op jit(solution)/shard_map/all_gather | solution.py:280
  22.3 0.0 copy-start
  22.3 1.4 %copy-done = bf16[3,64,4,1024]{3,2,1,0:T(4,128)(2,1)S(1)} copy-done((bf16[3,64,4,1024]{3,2,1,0:T(4,128)(2,1)S(1)}, bf16[3,64,4,1024]{3,2,1,0:T(4,128)(2,1)}, u32[]{:S(2)}) %copy-start) | copy-done | bytes 1572888
  23.7 0.0 copy-start.1
  23.7 1.4 %copy-done.1 = bf16[3,64,4,1024]{3,2,1,0:T(4,128)(2,1)S(1)} copy-done((bf16[3,64,4,1024]{3,2,1,0:T(4,128)(2,1)S(1)}, bf16[3,64,4,1024]{3,2,1,0:T(4,128)(2,1)}, u32[]{:S(2)}) %copy-start.1) | copy-done | bytes 1572888
  25.1 0.0 copy-start.2
  25.1 0.7 %copy-done.2 = f32[3,1,1024]{2,1,0:T(1,128)S(1)} copy-done((f32[3,1,1024]{2,1,0:T(1,128)S(1)}, f32[3,1,1024]{2,1,0:T(1,128)}, u32[]{:S(2)}) %copy-start.2) | copy-done | bytes 12312
  25.8 0.0 copy-start.3
  25.8 0.7 %copy-done.3 = f32[1,1024]{1,0:T(1,128)S(1)} copy-done((f32[1,1024]{1,0:T(1,128)S(1)}, f32[1,1024]{1,0:T(1,128)}, u32[]{:S(2)}) %copy-start.3) | copy-done | bytes 4120
  26.5 6.0 %shard_map.59 = (bf16[3,32,2,4,1024]{4,3,2,1,0:T(4,128)(2,1)}, f32[12,3,8,128]{3,2,1,0:T(8,128)S(1)}) custom-call(f32[6,3,8,128]{3,2,1,0:T(8,128)S(1)} %bitcast.44, f32[3,8,128]{2,1,0:T(8,128)S(1)} %bitcast.46, f32[8,128]{1,0:T(8,128)S(1)} %bitcast.47, bf16[3,32,2,4,1024]{4,3,2,1,0:T(4,128)(2,1)S(1)} %bitcast.42, bf16[3,32,2,4,1024]{4,3,2,1,0:T(4,128)(2,1)S(1)} %bitcast.43), custom_call_target="tpu_custom_call" | custom-call | tf_op jit(solution)/shard_map/pallas_call | solution.py:246
  32.5 2.0 %all-gather.1 = f32[24,3,8,128]{3,2,1,0:T(8,128)S(1)} all-gather(f32[12,3,8,128]{3,2,1,0:T(8,128)S(1)} %get-tuple-element.5), channel_id=3, replica_groups={{0,1},{2,3},{4,5},{6,7},{8,9},{10,11},{12,13},{14,15},{16,17},{18,19},{..., dimensions={0}, use_global_device_ids=true | all-gather | bytes 442368 | tf_op jit(solution)/shard_map/all_gather | solution.py:280
  34.7 4.6 %all_gather.39 = f32[2,3,3,8,128]{4,3,2,1,0:T(8,128)S(1)} all-gather(f32[1,3,3,8,128]{4,3,2,1,0:T(8,128)S(1)} %maximum_select_fusion.2), channel_id=1, replica_groups={{0,2},{1,3},{4,6},{5,7},{8,10},{9,11},{12,14},{13,15},{16,18},{17,19},{..., dimensions={0}, use_global_device_ids=true | all-gather | bytes 110592 | tf_op jit(solution)/shard_map/all_gather | solution.py:280
  39.4 4.5 %all-gather.2 = f32[4,3,8,128]{3,2,1,0:T(8,128)S(1)} all-gather(f32[2,3,8,128]{3,2,1,0:T(8,128)S(1)} %slice.145), channel_id=4, replica_groups={{2,4},{3,5},{6,8},{7,9},{10,12},{11,13},{14,16},{15,17},{18,20},{19,21}..., dimensions={0}, use_global_device_ids=true | all-gather | bytes 73728 | tf_op jit(solution)/shard_map/all_gather | solution.py:280
  43.9 9.8 %all-gather.3 = f32[2,1,3,8,128]{4,3,2,1,0:T(8,128)S(1)} all-gather(f32[1,1,3,8,128]{4,3,2,1,0:T(8,128)S(1)} %slice_select_fusion.4), channel_id=5, replica_groups={{0,2},{1,3},{4,6},{5,7},{8,10},{9,11},{12,14},{13,15},{16,18},{17,19},{..., dimensions={0}, use_global_device_ids=true | all-gather | bytes 36864 | tf_op jit(solution)/shard_map/all_gather | solution.py:280
  53.7 0.6 %fusion.4 = f32[1,3,8,128]{3,2,1,0:T(8,128)} fusion(f32[2,1,3,8,128]{4,3,2,1,0:T(8,128)S(1)} %all-gather.3, f32[3,3,8,128]{3,2,1,0:T(8,128)S(1)} %fusion.1, f32[1,2,3,8,128]{4,3,2,1,0:T(8,128)S(1)} %fusion.2, pred[]{:T(512)S(6)} %lt.12), kind=kLoop, calls=%fused_computation.14 | loop fusion | flops 12288 | bytes 73729 | tf_op jit(solution)/shard_map/add | solution.py:309
  (14 shorter events, 0.1 us)
Async XLA Ops:
  22.3 1.4 %copy-start = (bf16[3,64,4,1024]{3,2,1,0:T(4,128)(2,1)S(1)}, bf16[3,64,4,1024]{3,2,1,0:T(4,128)(2,1)}, u32[]{:S(2)}) copy-start(bf16[3,64,4,1024]{3,2,1,0:T(4,128)(2,1)} %param.6) | copy-start | bytes 4718596
  23.7 1.4 %copy-start.1 = (bf16[3,64,4,1024]{3,2,1,0:T(4,128)(2,1)S(1)}, bf16[3,64,4,1024]{3,2,1,0:T(4,128)(2,1)}, u32[]{:S(2)}) copy-start(bf16[3,64,4,1024]{3,2,1,0:T(4,128)(2,1)} %param.7) | copy-start | bytes 4718596
  25.1 0.7 %copy-start.2 = (f32[3,1,1024]{2,1,0:T(1,128)S(1)}, f32[3,1,1024]{2,1,0:T(1,128)}, u32[]{:S(2)}) copy-start(f32[3,1,1024]{2,1,0:T(1,128)} %param.4) | copy-start | bytes 36868
  25.8 0.7 %copy-start.3 = (f32[1,1024]{1,0:T(1,128)S(1)}, f32[1,1024]{1,0:T(1,128)}, u32[]{:S(2)}) copy-start(f32[1,1024]{1,0:T(1,128)} %param.5) | copy-start | bytes 12292

commit v2 on v1

v2 whole, which is shorter than its diff:
```python
import functools

import jax
import jax.numpy as jnp
from jax import lax
from jax.experimental import pallas as pl
from jax.experimental.pallas import tpu as pltpu
from jax.sharding import PartitionSpec as P

f32 = jnp.float32
bf16 = jnp.bfloat16

NF = 256
TIME_STEP = 0.02
AXIAL = 400.0
TRANSVERSE = 40.0
MAX_STRETCH = 50.0
VISCOSITY = 40.0
WEISSENBERG = 0.5
NOISE = (0.02 / 0.5) ** 0.5
DIAGONAL = 1.0 / 0.02 + 2.0 * 400.0 + 4.0 * 40.0
SWEEPS = 4
INDEX = ((0, 1, 2), (1, 3, 4), (2, 4, 5))
DIAGONAL_PAIRS = (0, 3, 5)

PLANES = 4
CHUNKS = 4
AXES = ("mesh", "field")


def lane_masks():
    lane = lax.broadcasted_iota(jnp.int32, (8, 128), 1)
    row = lax.broadcasted_iota(jnp.int32, (8, 128), 0)
    return dict(
        z_hi=(lane % 32) < 31,
        z_lo=(lane % 32) > 0,
        lane_hi=lane < 96,
        lane_lo=lane >= 32,
        row_hi=row < 7,
        row_lo=row > 0,
        channel=(row >= 2) & (row < 6),
    )


def shift_z(v, masks):
    plus = jnp.where(masks["z_hi"], pltpu.roll(v, 127, 1), 0.0)
    minus = jnp.where(masks["z_lo"], pltpu.roll(v, 1, 1), 0.0)
    return plus, minus


def shift_y(v, masks):
    ahead = pltpu.roll(v, 96, 1)
    behind = pltpu.roll(v, 32, 1)
    next_row = jnp.where(masks["row_hi"], pltpu.roll(ahead, 7, 0), 0.0)
    last_row = jnp.where(masks["row_lo"], pltpu.roll(behind, 1, 0), 0.0)
    return jnp.where(masks["lane_hi"], ahead, next_row), jnp.where(masks["lane_lo"], behind, last_row)


def slope_y(v, masks):
    plus, minus = shift_y(v, masks)
    return (plus - minus) * 0.5


def slope_z(v, masks):
    plus, minus = shift_z(v, masks)
    return (plus - minus) * 0.5


def around(v, masks):
    y_plus, y_minus = shift_y(v, masks)
    z_plus, z_minus = shift_z(v, masks)
    return (y_plus + y_minus) + (z_plus + z_minus)


def chunk(ch, pairs):
    per = pairs // CHUNKS
    return pl.ds(ch * per, per)


def loads(ch, sources, buffers, sem):
    some = chunk(ch, buffers[0].shape[1])
    return [
        pltpu.make_async_copy(src.at[c, some, h], buf.at[c, some, pl.ds(4 * h, 4), :], sem.at[ch, 6 * w + 2 * c + h])
        for w, (src, buf) in enumerate(zip(sources, buffers))
        for c in range(3)
        for h in range(2)
    ]


def stores(ch, buf, dst, sem):
    some = chunk(ch, buf.shape[1])
    return [
        pltpu.make_async_copy(buf.at[c, some, pl.ds(4 * h, 4), :], dst.at[c, some, h], sem.at[ch, 2 * c + h])
        for c in range(3)
        for h in range(2)
    ]


def relax_kernel(velocity_ref, pressure_ref, f_hbm, b_hbm, f_ref, base_ref, local_ref, b_buf, sem):
    pairs = b_buf.shape[1]
    per = pairs // CHUNKS
    for ch in range(CHUNKS):
        for copy in loads(ch, (f_hbm, b_hbm), (f_ref, b_buf), sem):
            copy.start()
    for a in range(3):
        local_ref[a] = velocity_ref[a]
    local_ref[3] = pressure_ref[...]
    for ch in range(CHUNKS):
        for copy in loads(ch, (f_hbm, b_hbm), (f_ref, b_buf), sem):
            copy.wait()

        def block(j, carry):
            lanes = pl.ds(pl.multiple_of(128 * j, 128), 128)
            for u in range(per):
                n = ch * per + u
                f = [f_ref[c, n, :, lanes].astype(f32) for c in range(3)]
                length_sq = f[0] * f[0] + f[1] * f[1] + f[2] * f[2]
                pull = TIME_STEP * MAX_STRETCH / (2.0 * WEISSENBERG) * pltpu.reciprocal(MAX_STRETCH - length_sq)
                kept = 1.0 - pull
                for c in range(3):
                    base_ref[c, n, :, lanes] = kept * f[c] + NOISE * b_buf[c, n, :, lanes].astype(f32)
            return carry

        lax.fori_loop(0, 8, block, 0)


def relax(velocity, pressure, fields, brownian):
    n = fields.shape[1] // 2
    split = (3, n, 2, PLANES, 1024)
    flat = (3, n, 8, 1024)
    vmem = pl.BlockSpec(memory_space=pltpu.VMEM)
    hbm = pl.BlockSpec(memory_space=pl.ANY)
    return pl.pallas_call(
        relax_kernel,
        out_shape=(
            jax.ShapeDtypeStruct(flat, bf16),
            jax.ShapeDtypeStruct(flat, f32),
            jax.ShapeDtypeStruct((4, 8, 128), f32),
        ),
        in_specs=[vmem, vmem, hbm, hbm],
        out_specs=[vmem, vmem, vmem],
        scratch_shapes=[pltpu.VMEM(flat, bf16), pltpu.SemaphoreType.DMA((CHUNKS, 12))],
        compiler_params=pltpu.CompilerParams(vmem_limit_bytes=24 << 20),
        cost_estimate=pl.CostEstimate(flops=10_000_000, bytes_accessed=8_000_000, transcendentals=0),
    )(velocity, pressure, fields.reshape(split), brownian.reshape(split))


def share_kernel(slabs, near_ref, local_ref, f_ref, base_ref, nf_hbm, out_ref, n_buf, grad, sums, sem):
    pairs = n_buf.shape[1]
    per = pairs // CHUNKS
    slab = lax.axis_index("mesh")
    mine = lax.axis_index("field")
    masks = lane_masks()

    planes = [(0, 1), (0, 0), (1, 0), (2, 0), (3, 0), (3, 1)]
    for q in range(PLANES):
        for a in range(3):
            before, centre, after = (near_ref[d, e, a] for d, e in planes[q : q + 3])
            slopes = ((after - before) * 0.5, slope_y(centre, masks), slope_z(centre, masks))
            for c in range(3):
                value = slopes[c] * TIME_STEP
                grad[3 * a + c, pl.ds(q, 8, stride=8), :] = value
                grad[3 * a + c, pl.ds(q + 4, 8, stride=8), :] = value

    for ch in range(CHUNKS):

        def block(j, carry):
            rows = pl.ds(pl.multiple_of(8 * j, 8), 8)
            lanes = pl.ds(pl.multiple_of(128 * j, 128), 128)
            g = [grad[k, rows, :] for k in range(9)]
            if ch:
                acc = [sums[k, rows, :] for k in range(6)]
            else:
                acc = [jnp.zeros((8, 128), f32) for _ in range(6)]
            for u in range(per):
                n = ch * per + u
                f = [f_ref[c, n, :, lanes].astype(f32) for c in range(3)]
                a = [
                    base_ref[o, n, :, lanes] + (g[3 * o] * f[0] + g[3 * o + 1] * f[1] + g[3 * o + 2] * f[2])
                    for o in range(3)
                ]
                for c in range(3):
                    n_buf[c, n, :, lanes] = a[c].astype(bf16)
                s = [x * x for x in a]
                r = pltpu.reciprocal(MAX_STRETCH - (s[0] + s[1] + s[2]))
                p0 = r * a[0]
                p1 = r * a[1]
                products = (r * s[0], p0 * a[1], p0 * a[2], r * s[1], p1 * a[2], r * s[2])
                acc = [x + y for x, y in zip(acc, products)]
            for k in range(6):
                sums[k, rows, :] = acc[k]
            return carry

        lax.fori_loop(0, 8, block, 0)
        for copy in stores(ch, n_buf, nf_hbm, sem):
            copy.start()

    scale = VISCOSITY / WEISSENBERG / NF * MAX_STRETCH
    stress = []
    for k in range(6):
        rows = []
        for q in range(PLANES):
            total = sums[k, pl.ds(q, 8, stride=8), :] + sums[k, pl.ds(q + 4, 8, stride=8), :]
            total = total * scale
            if k in DIAGONAL_PAIRS:
                total = total - VISCOSITY / WEISSENBERG / 4
            rows.append(total)
        stress.append(rows)

    own = [mine == q for q in range(PLANES)]
    zero = jnp.zeros((8, 128), f32)
    pressure = [jnp.where(own[q], local_ref[3], 0.0) for q in range(PLANES)]
    start = [[jnp.where(own[q], local_ref[a], 0.0) for q in range(PLANES)] for a in range(3)]

    def at(values, q):
        return values[q] if 0 <= q < PLANES else None

    def add(x, y):
        return y if x is None else x if y is None else x + y

    def halfway(values, q):
        plus, minus = at(values, q + 1), at(values, q - 1)
        if plus is None:
            return None if minus is None else minus * -0.5
        return plus * 0.5 if minus is None else (plus - minus) * 0.5

    first = -(SWEEPS)
    count = PLANES + 2 * SWEEPS
    fluid = []
    for q in range(first, first + count):
        plane = slab * PLANES + q
        inside = (plane >= 0) & (plane < slabs * PLANES)
        wide = plane < slabs * PLANES // 2
        value = jnp.where(masks["channel"] | wide, 1.0 / DIAGONAL, 0.0)
        fluid.append(jnp.where(inside, value, 0.0))

    for a in range(3):
        source = {}
        for q in range(-1, PLANES + 1):
            total = halfway(stress[INDEX[a][0]], q)
            if a == 0:
                total = total - halfway(pressure, q) if total is not None else None
            if 0 <= q < PLANES:
                inner = slope_y(stress[INDEX[a][1]][q], masks) + slope_z(stress[INDEX[a][2]][q], masks)
                if a == 1:
                    inner = inner - slope_y(pressure[q], masks)
                if a == 2:
                    inner = inner - slope_z(pressure[q], masks)
                total = total + inner + start[a][q] * (1.0 / TIME_STEP)
            source[q] = total
        current = {q: start[a][q] for q in range(PLANES)}
        for sweep in range(SWEEPS):
            later = {}
            for q in range(-1 - sweep, PLANES + 1 + sweep):
                total = source.get(q)
                along = add(current.get(q - 1), current.get(q + 1))
                if along is not None:
                    total = add(total, AXIAL * along)
                if q in current:
                    total = add(total, TRANSVERSE * around(current[q], masks))
                later[q] = total * fluid[q - first]
            current = later
        for q in range(first, first + count):
            out_ref[q - first, a] = current[q]

    for ch in range(CHUNKS):
        for copy in stores(ch, n_buf, nf_hbm, sem):
            copy.wait()


def share(near, local, f_flat, base):
    n = f_flat.shape[1]
    slabs = lax.axis_size("mesh")
    vmem = pl.BlockSpec(memory_space=pltpu.VMEM)
    hbm = pl.BlockSpec(memory_space=pl.ANY)
    return pl.pallas_call(
        functools.partial(share_kernel, slabs),
        out_shape=(
            jax.ShapeDtypeStruct((3, n, 2, PLANES, 1024), bf16),
            jax.ShapeDtypeStruct((PLANES + 2 * SWEEPS, 3, 8, 128), f32),
        ),
        in_specs=[vmem] * 4,
        out_specs=[hbm, vmem],
        scratch_shapes=[
            pltpu.VMEM((3, n, 8, 1024), bf16),
            pltpu.VMEM((9, 64, 128), f32),
            pltpu.VMEM((6, 64, 128), f32),
            pltpu.SemaphoreType.DMA((CHUNKS, 6)),
        ],
        compiler_params=pltpu.CompilerParams(vmem_limit_bytes=24 << 20),
    )(near, local, f_flat, base)


def body(velocity, pressure, fields, brownian):
    total = lax.axis_size("mesh") * 4
    mine = lax.axis_index("field")
    low = mine < 2
    core = mine % 2
    cores = [[i, i + 1] for i in range(0, total, 2)]
    inner = [[i, i + 2] for s in range(0, total, 4) for i in (s, s + 1)]

    def gather(x, groups):
        return lax.all_gather(x, AXES, axis=0, axis_index_groups=groups)

    def other(x, first):
        return jnp.where(first, x[1], x[0])

    own = velocity.reshape(3, 8, 128)
    faces = [(i, i + 1) for i in range(3, total - 1, 4)]
    edge = lax.ppermute(own, AXES, faces + [(b, a) for a, b in faces])
    f_flat, base, local = relax(own, pressure.reshape(8, 128), fields, brownian)
    near = lax.all_gather(jnp.stack([own, edge]), "field", axis=0)
    new_fields, shares = share(near, local, f_flat, base)

    both = gather(shares, cores).reshape(2, 3, 2, 2, 3, 8, 128)
    chip = both[0] + both[1]
    chip = jnp.where(core == 0, chip[:, :, 0], chip[:, :, 1])
    low_side = jnp.stack([chip[1, 0], chip[0, 0], chip[0, 1]])
    high_side = jnp.stack([chip[1, 1], chip[2, 0], chip[2, 1]])
    kept = jnp.where(low, low_side, high_side)
    kept = kept + other(gather(jnp.where(low, high_side, low_side), inner), low)
    far = [(i, i + 4) for i in range(total - 4) if i % 4 > 1] + [(i, i - 4) for i in range(4, total) if i % 4 < 2]
    next_to = [(i, i + 2) for i in range(total - 2) if i % 4 > 1] + [(i, i - 2) for i in range(2, total) if i % 4 < 2]
    from_far = lax.ppermute(jnp.where(low, kept[1], kept[2]), AXES, far)
    from_next = lax.ppermute(jnp.where(low, kept[2], kept[1]), AXES, next_to)
    result = kept[0] + (from_far + from_next)
    return new_fields.reshape(fields.shape), result.reshape(velocity.shape)


def solution(mesh):
    placed = (
        P(None, ("mesh", "field"), None),
        P(("mesh", "field"), None),
        P(None, "field", "mesh", None),
        P(None, "field", "mesh", None),
    )
    return jax.shard_map(
        body,
        mesh=mesh,
        in_specs=placed,
        out_specs=(P(None, "field", "mesh", None), P(None, ("mesh", "field"), None)),
        check_vma=False,
    )
```

time: 54.6 us -> 45.8 us (0.84)
  the two profiles are of different devices: /device:TPU:8 before, /device:TPU:256 now
where the time goes in v2:
time: 45.8 us; the launch traced here: 45.5 us
  starting transfers between devices  16.9 us (37%)
  blocking collectives  12 us (26%)
  Pallas kernels  6.01 us (13%)
  waiting for transfers between devices  4.94 us (11%)
  local copies, waits for them, and re-layouts  4.22 us (9%)
  between operations  0.77 us (2%)
  other arithmetic  0.68 us (1%)
    all_gather x2, blocking collectives, gather(): return lax.all_gather(x, AXES, axis=0, axis_index_groups=groups)  6.65 us
    ppermute x1, starting transfers between devices, body(): edge = lax.ppermute(own, AXES, faces + [(b, a) for a, b in faces])  6.1 us
    ppermute x1, starting transfers between devices, body(): from_next = lax.ppermute(jnp.where(low, kept[2], kept[1]), AXES, next_to)  6.07 us
    all_gather x1, blocking collectives, body(): near = lax.all_gather(jnp.stack([own, edge]), 'field', axis=0)  5.34 us
    ppermute x1, waiting for transfers between devices, body(): from_next = lax.ppermute(jnp.where(low, kept[2], kept[1]), AXES, next_to)  4.93 us
    ppermute x1, starting transfers between devices, body(): from_far = lax.ppermute(jnp.where(low, kept[1], kept[2]), AXES, far)  4.69 us
    unnamed x8, local copies, waits for them, and re-layouts  4.2 us
    pallas_call x1, Pallas kernels, share(): pl.pallas_call(functools.partial(share_kernel, slabs), out_shape=(jax.Sha...  3.18 us
  transfers between devices with their start and end apart: 3, of which 1 were waited for; matrix products, arithmetic and copies ran while one was open for 0% of the time, Pallas kernels for 6%

profile of v2, /device:TPU:256, one launch (start us, length us, event | category | flops | bytes accessed | tf_op | source)
XLA Modules:
  0.0 45.5 jit_solution(6388263623827055592)
XLA Ops:
  0.6 6.1 %collective-permute-start = (f32[3,8,128]{2,1,0:T(8,128)}, f32[3,8,128]{2,1,0:T(8,128)S(1)}, u32[]{:S(2)}, u32[]{:S(2)}) collective-permute-start(f32[3,8,128]{2,1,0:T(8,128)} %bitcast.55), channel_id=1, source_target_pairs={{3,4},{7,8},{11,12},{15,16},{19,20},{23,24},{27,28},{31,32},{35,36... | collective-permute-start | bytes 36872 | tf_op jit(solution)/shard_map/ppermute | solution.py:310
  6.8 0.0 copy-start
  6.8 1.4 %copy-done = bf16[3,64,4,1024]{3,2,1,0:T(4,128)(2,1)S(1)} copy-done((bf16[3,64,4,1024]{3,2,1,0:T(4,128)(2,1)S(1)}, bf16[3,64,4,1024]{3,2,1,0:T(4,128)(2,1)}, u32[]{:S(2)}) %copy-start) | copy-done | bytes 1572888
  8.2 0.0 copy-start.1
  8.2 1.4 %copy-done.1 = bf16[3,64,4,1024]{3,2,1,0:T(4,128)(2,1)S(1)} copy-done((bf16[3,64,4,1024]{3,2,1,0:T(4,128)(2,1)S(1)}, bf16[3,64,4,1024]{3,2,1,0:T(4,128)(2,1)}, u32[]{:S(2)}) %copy-start.1) | copy-done | bytes 1572888
  9.6 0.0 copy-start.2
  9.6 0.7 %copy-done.2 = f32[3,1,1024]{2,1,0:T(1,128)S(1)} copy-done((f32[3,1,1024]{2,1,0:T(1,128)S(1)}, f32[3,1,1024]{2,1,0:T(1,128)}, u32[]{:S(2)}) %copy-start.2) | copy-done | bytes 12312
  10.3 0.0 copy-start.3
  10.3 0.7 %copy-done.3 = f32[1,1024]{1,0:T(1,128)S(1)} copy-done((f32[1,1024]{1,0:T(1,128)S(1)}, f32[1,1024]{1,0:T(1,128)}, u32[]{:S(2)}) %copy-start.3) | copy-done | bytes 4120
  11.0 2.8 %shard_map.59 = (bf16[3,32,8,1024]{3,2,1,0:T(8,128)(2,1)S(1)}, f32[3,32,8,1024]{3,2,1,0:T(8,128)S(1)}, f32[4,8,128]{2,1,0:T(8,128)S(1)}) custom-call(f32[3,8,128]{2,1,0:T(8,128)S(1)} %bitcast.56, f32[8,128]{1,0:T(8,128)S(1)} %bitcast.58, bf16[3,32,2,4,1024]{4,3,2,1,0:T(4,128)(2,1)S(1)} %bitcast.52, bf16[3,32,2,4,1024]{4,3,2,1,0:T(4,128)(2,1)S(1)} %bitcast.53), custom_call_target="tpu_custom_call" | custom-call | flops 10000000 | bytes 8000000 | tf_op jit(solution)/shard_map/pallas_call | solution.py:133
  13.8 0.0 collective-permute-done
  13.8 5.3 %all-gather = f32[8,3,8,128]{3,2,1,0:T(8,128)S(1)} all-gather(f32[2,3,8,128]{3,2,1,0:T(8,128)S(1)} %pad_maximum_fusion), channel_id=2, replica_groups=mesh['mesh'=128,'field'=4] {'field'}, dimensions={0}, use_global_device_ids=true | all-gather | bytes 122880 | tf_op jit(solution)/shard_map/all_gather | solution.py:312
  19.2 3.2 %shard_map.60 = (bf16[3,32,2,4,1024]{4,3,2,1,0:T(4,128)(2,1)}, f32[12,3,8,128]{3,2,1,0:T(8,128)S(1)}) custom-call(f32[4,2,3,8,128]{4,3,2,1,0:T(8,128)S(1)} %bitcast.54, f32[4,8,128]{2,1,0:T(8,128)S(1)} %get-tuple-element.7.local_ref, bf16[3,32,8,1024]{3,2,1,0:T(8,128)(2,1)S(1)} %get-tuple-element.8.f_ref, f32[3,32,8,1024]{3,2,1,0:T(8,128)S(1)} %get-tuple-element.9.base_ref), custom_call_target="tpu_custom_call" | custom-call | tf_op jit(solution)/shard_map/pallas_call | solution.py:276
  22.4 2.0 %all-gather.1 = f32[24,3,8,128]{3,2,1,0:T(8,128)S(1)} all-gather(f32[12,3,8,128]{3,2,1,0:T(8,128)S(1)} %get-tuple-element.11), channel_id=3, replica_groups={{0,1},{2,3},{4,5},{6,7},{8,9},{10,11},{12,13},{14,15},{16,17},{18,19},{..., dimensions={0}, use_global_device_ids=true | all-gather | bytes 442368 | tf_op jit(solution)/shard_map/all_gather | solution.py:303
  24.5 4.6 %all_gather.20 = f32[2,3,3,8,128]{4,3,2,1,0:T(8,128)S(1)} all-gather(f32[1,3,3,8,128]{4,3,2,1,0:T(8,128)S(1)} %maximum_select_fusion.1), channel_id=1, replica_groups={{0,2},{1,3},{4,6},{5,7},{8,10},{9,11},{12,14},{13,15},{16,18},{17,19},{..., dimensions={0}, use_global_device_ids=true | all-gather | bytes 110592 | tf_op jit(solution)/shard_map/all_gather | solution.py:303
  29.1 4.7 %collective-permute-start.1 = (f32[3,8,128]{2,1,0:T(8,128)S(1)}, f32[3,8,128]{2,1,0:T(8,128)S(1)}, u32[]{:S(2)}, u32[]{:S(2)}) collective-permute-start(f32[3,8,128]{2,1,0:T(8,128)S(1)} %get-tuple-element.27), channel_id=1, source_target_pairs={{2,6},{3,7},{6,10},{7,11},{10,14},{11,15},{14,18},{15,19},{18,22},... | collective-permute-start | bytes 36872 | tf_op jit(solution)/shard_map/ppermute | solution.py:324
  33.8 6.1 %collective-permute-start.2 = (f32[3,8,128]{2,1,0:T(8,128)S(1)}, f32[3,8,128]{2,1,0:T(8,128)S(1)}, u32[]{:S(2)}, u32[]{:S(2)}) collective-permute-start(f32[3,8,128]{2,1,0:T(8,128)S(1)} %get-tuple-element.26), channel_id=1, source_target_pairs={{2,4},{3,5},{6,8},{7,9},{10,12},{11,13},{14,16},{15,17},{18,20},{1... | collective-permute-start | bytes 36872 | tf_op jit(solution)/shard_map/ppermute | solution.py:325
  39.9 0.0 collective-permute-done.1
  39.9 4.9 %collective-permute-done.2 = f32[3,8,128]{2,1,0:T(8,128)S(1)} collective-permute-done((f32[3,8,128]{2,1,0:T(8,128)S(1)}, f32[3,8,128]{2,1,0:T(8,128)S(1)}, u32[]{:S(2)}, u32[]{:S(2)}) %collective-permute-start.2) | collective-permute-done | bytes 12320 | tf_op jit(solution)/shard_map/ppermute | solution.py:325
  44.9 0.6 %fusion.3 = f32[3,8,128]{2,1,0:T(8,128)} fusion(f32[3,3,8,128]{3,2,1,0:T(8,128)S(1)} %fusion.2, f32[3,8,128]{2,1,0:T(8,128)S(1)} %collective-permute-done.1, f32[3,8,128]{2,1,0:T(8,128)S(1)} %collective-permute-done.2), kind=kLoop, calls=%fused_computation.13 | loop fusion | flops 6144 | bytes 49152 | tf_op jit(solution)/shard_map/add | solution.py:326
  (9 shorter events, 0.1 us)
Async XLA Ops:
  0.6 13.2 %collective-permute-start = (f32[3,8,128]{2,1,0:T(8,128)}, f32[3,8,128]{2,1,0:T(8,128)S(1)}, u32[]{:S(2)}, u32[]{:S(2)}) collective-permute-start(f32[3,8,128]{2,1,0:T(8,128)} %bitcast.55), channel_id=1, source_target_pairs={{3,4},{7,8},{11,12},{15,16},{19,20},{23,24},{27,28},{31,32},{35,36... | collective-permute-start | bytes 36872 | tf_op jit(solution)/shard_map/ppermute | solution.py:310
  6.8 1.4 %copy-start = (bf16[3,64,4,1024]{3,2,1,0:T(4,128)(2,1)S(1)}, bf16[3,64,4,1024]{3,2,1,0:T(4,128)(2,1)}, u32[]{:S(2)}) copy-start(bf16[3,64,4,1024]{3,2,1,0:T(4,128)(2,1)} %param.6) | copy-start | bytes 4718596
  8.2 1.4 %copy-start.1 = (bf16[3,64,4,1024]{3,2,1,0:T(4,128)(2,1)S(1)}, bf16[3,64,4,1024]{3,2,1,0:T(4,128)(2,1)}, u32[]{:S(2)}) copy-start(bf16[3,64,4,1024]{3,2,1,0:T(4,128)(2,1)} %param.7) | copy-start | bytes 4718596
  9.6 0.7 %copy-start.2 = (f32[3,1,1024]{2,1,0:T(1,128)S(1)}, f32[3,1,1024]{2,1,0:T(1,128)}, u32[]{:S(2)}) copy-start(f32[3,1,1024]{2,1,0:T(1,128)} %param.4) | copy-start | bytes 36868
  10.3 0.7 %copy-start.3 = (f32[1,1024]{1,0:T(1,128)S(1)}, f32[1,1024]{1,0:T(1,128)}, u32[]{:S(2)}) copy-start(f32[1,1024]{1,0:T(1,128)} %param.5) | copy-start | bytes 12292
  29.1 10.8 %collective-permute-start.1 = (f32[3,8,128]{2,1,0:T(8,128)S(1)}, f32[3,8,128]{2,1,0:T(8,128)S(1)}, u32[]{:S(2)}, u32[]{:S(2)}) collective-permute-start(f32[3,8,128]{2,1,0:T(8,128)S(1)} %get-tuple-element.27), channel_id=1, source_target_pairs={{2,6},{3,7},{6,10},{7,11},{10,14},{11,15},{14,18},{15,19},{18,22},... | collective-permute-start | bytes 36872 | tf_op jit(solution)/shard_map/ppermute | solution.py:324
  33.8 11.0 %collective-permute-start.2 = (f32[3,8,128]{2,1,0:T(8,128)S(1)}, f32[3,8,128]{2,1,0:T(8,128)S(1)}, u32[]{:S(2)}, u32[]{:S(2)}) collective-permute-start(f32[3,8,128]{2,1,0:T(8,128)S(1)} %get-tuple-element.26), channel_id=1, source_target_pairs={{2,4},{3,5},{6,8},{7,9},{10,12},{11,13},{14,16},{15,17},{18,20},{1... | collective-permute-start | bytes 36872 | tf_op jit(solution)/shard_map/ppermute | solution.py:325

commit v3 on v2

--- a/solution.py
+++ b/solution.py
@@ -96,15 +96,18 @@
     ]
 
 
-def relax_kernel(velocity_ref, pressure_ref, f_hbm, b_hbm, f_ref, base_ref, local_ref, b_buf, sem):
+def relax_kernel(velocity_hbm, pressure_hbm, f_hbm, b_hbm, f_ref, base_ref, local_ref, b_buf, sem, local_sem):
     pairs = b_buf.shape[1]
     per = pairs // CHUNKS
     for ch in range(CHUNKS):
         for copy in loads(ch, (f_hbm, b_hbm), (f_ref, b_buf), sem):
             copy.start()
-    for a in range(3):
-        local_ref[a] = velocity_ref[a]
-    local_ref[3] = pressure_ref[...]
+    own = (
+        pltpu.make_async_copy(velocity_hbm, local_ref.at[pl.ds(0, 3)], local_sem.at[0]),
+        pltpu.make_async_copy(pressure_hbm, local_ref.at[pl.ds(3, 1)], local_sem.at[1]),
+    )
+    for copy in own:
+        copy.start()
     for ch in range(CHUNKS):
         for copy in loads(ch, (f_hbm, b_hbm), (f_ref, b_buf), sem):
             copy.wait()
@@ -122,6 +125,12 @@
             return carry
 
         lax.fori_loop(0, 8, block, 0)
+    for copy in own:
+        copy.wait()
+
+
+def in_hbm(x):
+    return pltpu.with_memory_space_constraint(x, pltpu.HBM)
 
 
 def relax(velocity, pressure, fields, brownian):
@@ -137,16 +146,24 @@
             jax.ShapeDtypeStruct(flat, f32),
             jax.ShapeDtypeStruct((4, 8, 128), f32),
         ),
-        in_specs=[vmem, vmem, hbm, hbm],
+        in_specs=[hbm] * 4,
         out_specs=[vmem, vmem, vmem],
-        scratch_shapes=[pltpu.VMEM(flat, bf16), pltpu.SemaphoreType.DMA((CHUNKS, 12))],
+        scratch_shapes=[
+            pltpu.VMEM(flat, bf16),
+            pltpu.SemaphoreType.DMA((CHUNKS, 12)),
+            pltpu.SemaphoreType.DMA((2,)),
+        ],
         compiler_params=pltpu.CompilerParams(vmem_limit_bytes=24 << 20),
         cost_estimate=pl.CostEstimate(flops=10_000_000, bytes_accessed=8_000_000, transcendentals=0),
-    )(velocity, pressure, fields.reshape(split), brownian.reshape(split))
-
-
-def share_kernel(slabs, near_ref, local_ref, f_ref, base_ref, nf_hbm, out_ref, n_buf, grad, sums, sem):
-    pairs = n_buf.shape[1]
+    )(*(in_hbm(x) for x in (velocity, pressure, fields.reshape(split), brownian.reshape(split))))
+
+
+def stretch(f, base, g):
+    return [base[o] + (g[3 * o] * f[0] + g[3 * o + 1] * f[1] + g[3 * o + 2] * f[2]) for o in range(3)]
+
+
+def share_kernel(slabs, near_ref, local_ref, f_ref, base_ref, out_ref, grad, sums):
+    pairs = f_ref.shape[1]
     per = pairs // CHUNKS
     slab = lax.axis_index("mesh")
     mine = lax.axis_index("field")
@@ -175,12 +192,7 @@
             for u in range(per):
                 n = ch * per + u
                 f = [f_ref[c, n, :, lanes].astype(f32) for c in range(3)]
-                a = [
-                    base_ref[o, n, :, lanes] + (g[3 * o] * f[0] + g[3 * o + 1] * f[1] + g[3 * o + 2] * f[2])
-                    for o in range(3)
-                ]
-                for c in range(3):
-                    n_buf[c, n, :, lanes] = a[c].astype(bf16)
+                a = stretch(f, [base_ref[o, n, :, lanes] for o in range(3)], g)
                 s = [x * x for x in a]
                 r = pltpu.reciprocal(MAX_STRETCH - (s[0] + s[1] + s[2]))
                 p0 = r * a[0]
@@ -192,8 +204,6 @@
             return carry
 
         lax.fori_loop(0, 8, block, 0)
-        for copy in stores(ch, n_buf, nf_hbm, sem):
-            copy.start()
 
     scale = VISCOSITY / WEISSENBERG / NF * MAX_STRETCH
     stress = []
@@ -263,32 +273,61 @@
         for q in range(first, first + count):
             out_ref[q - first, a] = current[q]
 
-    for ch in range(CHUNKS):
-        for copy in stores(ch, n_buf, nf_hbm, sem):
-            copy.wait()
-
 
 def share(near, local, f_flat, base):
-    n = f_flat.shape[1]
     slabs = lax.axis_size("mesh")
     vmem = pl.BlockSpec(memory_space=pltpu.VMEM)
-    hbm = pl.BlockSpec(memory_space=pl.ANY)
     return pl.pallas_call(
         functools.partial(share_kernel, slabs),
         out_shape=(
-            jax.ShapeDtypeStruct((3, n, 2, PLANES, 1024), bf16),
             jax.ShapeDtypeStruct((PLANES + 2 * SWEEPS, 3, 8, 128), f32),
+            jax.ShapeDtypeStruct((9, 64, 128), f32),
         ),
         in_specs=[vmem] * 4,
-        out_specs=[hbm, vmem],
-        scratch_shapes=[
-            pltpu.VMEM((3, n, 8, 1024), bf16),
-            pltpu.VMEM((9, 64, 128), f32),
-            pltpu.VMEM((6, 64, 128), f32),
-            pltpu.SemaphoreType.DMA((CHUNKS, 6)),
-        ],
-        compiler_params=pltpu.CompilerParams(vmem_limit_bytes=24 << 20),
+        out_specs=[vmem] * 2,
+        scratch_shapes=[pltpu.VMEM((6, 64, 128), f32)],
+        compiler_params=pltpu.CompilerParams(vmem_limit_bytes=16 << 20),
+        cost_estimate=pl.CostEstimate(flops=12_000_000, bytes_accessed=5_000_000, transcendentals=0),
     )(near, local, f_flat, base)
+
+
+def advance_kernel(grad, f_ref, base_ref, nf_hbm, n_buf, sem):
+    pairs = n_buf.shape[1]
+    per = pairs // CHUNKS
+    for ch in range(CHUNKS):
+
+        def block(j, carry):
+            rows = pl.ds(pl.multiple_of(8 * j, 8), 8)
+            lanes = pl.ds(pl.multiple_of(128 * j, 128), 128)
+            g = [grad[k, rows, :] for k in range(9)]
+            for u in range(per):
+                n = ch * per + u
+                f = [f_ref[c, n, :, lanes].astype(f32) for c in range(3)]
+                a = stretch(f, [base_ref[o, n, :, lanes] for o in range(3)], g)
+                for c in range(3):
+                    n_buf[c, n, :, lanes] = a[c].astype(bf16)
+            return carry
+
+        lax.fori_loop(0, 8, block, 0)
+        for copy in stores(ch, n_buf, nf_hbm, sem):
+            copy.start()
+    for ch in range(CHUNKS):
+        for copy in stores(ch, n_buf, nf_hbm, sem):
+            copy.wait()
+
+
+def advance(grad, f_flat, base):
+    n = f_flat.shape[1]
+    vmem = pl.BlockSpec(memory_space=pltpu.VMEM)
+    return pl.pallas_call(
+        advance_kernel,
+        out_shape=jax.ShapeDtypeStruct((3, n, 2, PLANES, 1024), bf16),
+        in_specs=[vmem] * 3,
+        out_specs=pl.BlockSpec(memory_space=pl.ANY),
+        scratch_shapes=[pltpu.VMEM((3, n, 8, 1024), bf16), pltpu.SemaphoreType.DMA((CHUNKS, 6))],
+        compiler_params=pltpu.CompilerParams(vmem_limit_bytes=16 << 20),
+        cost_estimate=pl.CostEstimate(flops=6_000_000, bytes_accessed=6_000_000, transcendentals=0),
+    )(grad, f_flat, base)
 
 
 def body(velocity, pressure, fields, brownian):
@@ -308,9 +347,9 @@
     own = velocity.reshape(3, 8, 128)
     faces = [(i, i + 1) for i in range(3, total - 1, 4)]
     edge = lax.ppermute(own, AXES, faces + [(b, a) for a, b in faces])
-    f_flat, base, local = relax(own, pressure.reshape(8, 128), fields, brownian)
+    f_flat, base, local = relax(own, pressure.reshape(1, 8, 128), fields, brownian)
     near = lax.all_gather(jnp.stack([own, edge]), "field", axis=0)
-    new_fields, shares = share(near, local, f_flat, base)
+    shares, grad = share(near, local, f_flat, base)
 
     both = gather(shares, cores).reshape(2, 3, 2, 2, 3, 8, 128)
     chip = both[0] + both[1]
@@ -319,11 +358,11 @@
     high_side = jnp.stack([chip[1, 1], chip[2, 0], chip[2, 1]])
     kept = jnp.where(low, low_side, high_side)
     kept = kept + other(gather(jnp.where(low, high_side, low_side), inner), low)
-    far = [(i, i + 4) for i in range(total - 4) if i % 4 > 1] + [(i, i - 4) for i in range(4, total) if i % 4 < 2]
-    next_to = [(i, i + 2) for i in range(total - 2) if i % 4 > 1] + [(i, i - 2) for i in range(2, total) if i % 4 < 2]
-    from_far = lax.ppermute(jnp.where(low, kept[1], kept[2]), AXES, far)
-    from_next = lax.ppermute(jnp.where(low, kept[2], kept[1]), AXES, next_to)
-    result = kept[0] + (from_far + from_next)
+    next_to = [(i, i + 2) for i in range(total - 2) if i % 4 > 1]
+    arrived = lax.ppermute(kept[1:], AXES, next_to + [(b, a) for a, b in next_to])
+    new_fields = advance(grad, f_flat, base)
+    passed = jnp.where(low, arrived[1], arrived[0])
+    result = kept[0] + jnp.where(low, arrived[0], arrived[1]) + other(gather(passed, inner), low)
     return new_fields.reshape(fields.shape), result.reshape(velocity.shape)
 
 

time: 45.8 us -> 42.4 us (0.926)
  starting transfers between devices: 16.9 us -> 11.3 us
  blocking collectives: 12 us -> 16.4 us
  local copies, waits for them, and re-layouts: 4.22 us -> 0.03 us
  Pallas kernels: 6.01 us -> 7.76 us
  waiting for transfers between devices: 4.94 us -> 5.4 us
    ppermute x2 -> x1, starting transfers between devices: 10.8 us -> 5.18 us  [body(): lax.ppermute(kept[1:], AXES, next_to + [(b, a) for a, b in next_to])]
    all_gather x2 -> x3, blocking collectives: 6.65 us -> 11 us  [gather(): return lax.all_gather(x, AXES, axis=0, axis_index_groups=groups)]
    unnamed x8 -> x2, local copies, waits for them, and re-layouts: 4.2 us -> 0.01 us
    pallas_call x0 -> x1, Pallas kernels: none -> 2.18 us  [advance(): pl.pallas_call(advance_kernel, out_shape=jax.ShapeDtypeStruct((3, n, 2, P...]
    ppermute x1, waiting for transfers between devices: 0.01 us -> 1.62 us  [body(): edge = lax.ppermute(own, AXES, faces + [(b, a) for a, b in faces])]
    ppermute x2 -> x1, waiting for transfers between devices: 4.93 us -> 3.78 us  [body(): lax.ppermute(kept[1:], AXES, next_to + [(b, a) for a, b in next_to])]
    pallas_call x1, Pallas kernels: 3.18 us -> 2.68 us  [share(): pl.pallas_call(functools.partial(share_kernel, slabs), out_shape=(jax.Sha...]
  transfers between devices with their start and end apart: 3 -> 2, of which waited for: 1 -> 2; matrix products, arithmetic and copies ran while one was open for 0% -> 0% of each run, Pallas kernels for 6% -> 12%
where the time goes in v3:
time: 42.4 us; the launch traced here: 42.2 us
  blocking collectives  16.4 us (39%)
  starting transfers between devices  11.3 us (27%)
  Pallas kernels  7.76 us (18%)
  waiting for transfers between devices  5.4 us (13%)
  between operations  0.74 us (2%)
  other arithmetic  0.67 us (2%)
    all_gather x3, blocking collectives, gather(): return lax.all_gather(x, AXES, axis=0, axis_index_groups=groups)  11 us
    ppermute x1, starting transfers between devices, body(): edge = lax.ppermute(own, AXES, faces + [(b, a) for a, b in faces])  6.1 us
    all_gather x1, blocking collectives, body(): near = lax.all_gather(jnp.stack([own, edge]), 'field', axis=0)  5.32 us
    ppermute x1, starting transfers between devices, body(): lax.ppermute(kept[1:], AXES, next_to + [(b, a) for a, b in next_to])  5.18 us
    ppermute x1, waiting for transfers between devices, body(): lax.ppermute(kept[1:], AXES, next_to + [(b, a) for a, b in next_to])  3.78 us
    pallas_call x1, Pallas kernels, relax(): pl.pallas_call(relax_kernel, out_shape=(jax.ShapeDtypeStruct(flat, bf16),...  2.89 us
    pallas_call x1, Pallas kernels, share(): pl.pallas_call(functools.partial(share_kernel, slabs), out_shape=(jax.Sha...  2.68 us
    pallas_call x1, Pallas kernels, advance(): pl.pallas_call(advance_kernel, out_shape=jax.ShapeDtypeStruct((3, n, 2, P...  2.18 us
  transfers between devices with their start and end apart: 2, of which 2 were waited for; matrix products, arithmetic and copies ran while one was open for 0% of the time, Pallas kernels for 12%

profile of v3, /device:TPU:256, one launch (start us, length us, event | category | flops | bytes accessed | tf_op | source)
XLA Modules:
  0.0 42.2 jit_solution(14977222099144628754)
XLA Ops:
  0.6 6.1 %collective-permute-start = (f32[3,8,128]{2,1,0:T(8,128)}, f32[3,8,128]{2,1,0:T(8,128)S(1)}, u32[]{:S(2)}, u32[]{:S(2)}) collective-permute-start(f32[3,8,128]{2,1,0:T(8,128)} %bitcast.50), channel_id=1, source_target_pairs={{3,4},{7,8},{11,12},{15,16},{19,20},{23,24},{27,28},{31,32},{35,36... | collective-permute-start | bytes 36872 | tf_op jit(solution)/shard_map/ppermute | solution.py:349
  6.8 0.0 copy-start
  6.8 2.9 %shard_map.59 = (bf16[3,32,8,1024]{3,2,1,0:T(8,128)(2,1)S(1)}, f32[3,32,8,1024]{3,2,1,0:T(8,128)S(1)}, f32[4,8,128]{2,1,0:T(8,128)S(1)}) custom-call(f32[3,8,128]{2,1,0:T(8,128)} %bitcast.51, f32[1,8,128]{2,1,0:T(8,128)} %bitcast.55, bf16[3,32,2,4,1024]{4,3,2,1,0:T(4,128)(2,1)} %bitcast.45, bf16[3,32,2,4,1024]{4,3,2,1,0:T(4,128)(2,1)} %bitcast.46), custom_call_target="tpu_custom_call" | custom-call | flops 10000000 | bytes 8000000 | tf_op jit(solution)/shard_map/pallas_call | solution.py:142
  9.7 1.6 %collective-permute-done = f32[3,8,128]{2,1,0:T(8,128)S(1)} collective-permute-done((f32[3,8,128]{2,1,0:T(8,128)}, f32[3,8,128]{2,1,0:T(8,128)S(1)}, u32[]{:S(2)}, u32[]{:S(2)}) %collective-permute-start) | collective-permute-done | bytes 12320 | tf_op jit(solution)/shard_map/ppermute | solution.py:349
  11.3 0.0 copy-done
  11.3 5.3 %all-gather = f32[8,3,8,128]{3,2,1,0:T(8,128)S(1)} all-gather(f32[2,3,8,128]{3,2,1,0:T(8,128)S(1)} %pad_maximum_fusion), channel_id=2, replica_groups=mesh['mesh'=128,'field'=4] {'field'}, dimensions={0}, use_global_device_ids=true | all-gather | bytes 122880 | tf_op jit(solution)/shard_map/all_gather | solution.py:351
  16.6 2.7 %shard_map.60 = (f32[12,3,8,128]{3,2,1,0:T(8,128)S(1)}, f32[9,64,128]{2,1,0:T(8,128)S(1)}) custom-call(f32[4,2,3,8,128]{4,3,2,1,0:T(8,128)S(1)} %bitcast.44, f32[4,8,128]{2,1,0:T(8,128)S(1)} %get-tuple-element.7.local_ref, bf16[3,32,8,1024]{3,2,1,0:T(8,128)(2,1)S(1)} %get-tuple-element.8.f_ref, f32[3,32,8,1024]{3,2,1,0:T(8,128)S(1)} %get-tuple-element.9.base_ref), custom_call_target="tpu_custom_call" | custom-call | flops 12000000 | bytes 5000000 | tf_op jit(solution)/shard_map/pallas_call | solution.py:280
  19.3 2.0 %all-gather.1 = f32[24,3,8,128]{3,2,1,0:T(8,128)S(1)} all-gather(f32[12,3,8,128]{3,2,1,0:T(8,128)S(1)} %get-tuple-element.11), channel_id=3, replica_groups={{0,1},{2,3},{4,5},{6,7},{8,9},{10,11},{12,13},{14,15},{16,17},{18,19},{..., dimensions={0}, use_global_device_ids=true | all-gather | bytes 442368 | tf_op jit(solution)/shard_map/all_gather | solution.py:342
  21.4 4.6 %all_gather.24 = f32[2,3,3,8,128]{4,3,2,1,0:T(8,128)S(1)} all-gather(f32[1,3,3,8,128]{4,3,2,1,0:T(8,128)S(1)} %maximum_select_fusion.1), channel_id=1, replica_groups={{0,2},{1,3},{4,6},{5,7},{8,10},{9,11},{12,14},{13,15},{16,18},{17,19},{..., dimensions={0}, use_global_device_ids=true | all-gather | bytes 110592 | tf_op jit(solution)/shard_map/all_gather | solution.py:342
  26.1 5.2 %collective-permute-start.1 = (f32[2,3,8,128]{3,2,1,0:T(8,128)S(1)}, f32[2,3,8,128]{3,2,1,0:T(8,128)S(1)}, u32[]{:S(2)}, u32[]{:S(2)}) collective-permute-start(f32[2,3,8,128]{3,2,1,0:T(8,128)S(1)} %slice.109), channel_id=1, source_target_pairs={{2,4},{3,5},{6,8},{7,9},{10,12},{11,13},{14,16},{15,17},{18,20},{1... | collective-permute-start | bytes 73736 | tf_op jit(solution)/shard_map/ppermute | solution.py:362
  31.3 2.2 %shard_map.61 = bf16[3,32,2,4,1024]{4,3,2,1,0:T(4,128)(2,1)} custom-call(f32[9,64,128]{2,1,0:T(8,128)S(1)} %get-tuple-element.10.grad, bf16[3,32,8,1024]{3,2,1,0:T(8,128)(2,1)S(1)} %get-tuple-element.8.f_ref, f32[3,32,8,1024]{3,2,1,0:T(8,128)S(1)} %get-tuple-element.9.base_ref), custom_call_target="tpu_custom_call" | custom-call | flops 6000000 | bytes 6000000 | tf_op jit(solution)/shard_map/pallas_call | solution.py:322
  33.5 3.8 %collective-permute-done.1 = f32[2,3,8,128]{3,2,1,0:T(8,128)S(1)} collective-permute-done((f32[2,3,8,128]{3,2,1,0:T(8,128)S(1)}, f32[2,3,8,128]{3,2,1,0:T(8,128)S(1)}, u32[]{:S(2)}, u32[]{:S(2)}) %collective-permute-start.1) | collective-permute-done | bytes 24608 | tf_op jit(solution)/shard_map/ppermute | solution.py:362
  37.2 4.4 %all_gather.25 = f32[2,3,8,128]{3,2,1,0:T(8,128)S(1)} all-gather(f32[1,3,8,128]{3,2,1,0:T(8,128)S(1)} %slice_select_fusion.2), channel_id=1, replica_groups={{0,2},{1,3},{4,6},{5,7},{8,10},{9,11},{12,14},{13,15},{16,18},{17,19},{..., dimensions={0}, use_global_device_ids=true | all-gather | bytes 36864 | tf_op jit(solution)/shard_map/all_gather | solution.py:342
  41.6 0.6 %fusion.3 = f32[1,3,8,128]{3,2,1,0:T(8,128)} fusion(f32[2,3,8,128]{3,2,1,0:T(8,128)S(1)} %all_gather.25, f32[3,3,8,128]{3,2,1,0:T(8,128)S(1)} %fusion.2, f32[2,3,8,128]{3,2,1,0:T(8,128)S(1)} %collective-permute-done.1, pred[]{:T(512)S(6)} %lt.9), kind=kLoop, calls=%fused_computation.13 | loop fusion | flops 12288 | bytes 73729 | tf_op jit(solution)/shard_map/add | solution.py:365
  (10 shorter events, 0.1 us)
Async XLA Ops:
  0.6 10.7 %collective-permute-start = (f32[3,8,128]{2,1,0:T(8,128)}, f32[3,8,128]{2,1,0:T(8,128)S(1)}, u32[]{:S(2)}, u32[]{:S(2)}) collective-permute-start(f32[3,8,128]{2,1,0:T(8,128)} %bitcast.50), channel_id=1, source_target_pairs={{3,4},{7,8},{11,12},{15,16},{19,20},{23,24},{27,28},{31,32},{35,36... | collective-permute-start | bytes 36872 | tf_op jit(solution)/shard_map/ppermute | solution.py:349
  6.8 4.5 %copy-start = (f32[3,1,1024]{2,1,0:T(1,128)S(1)}, f32[3,1,1024]{2,1,0:T(1,128)}, u32[]{:S(2)}) copy-start(f32[3,1,1024]{2,1,0:T(1,128)} %param.4) | copy-start | bytes 36868
  26.1 11.2 %collective-permute-start.1 = (f32[2,3,8,128]{3,2,1,0:T(8,128)S(1)}, f32[2,3,8,128]{3,2,1,0:T(8,128)S(1)}, u32[]{:S(2)}, u32[]{:S(2)}) collective-permute-start(f32[2,3,8,128]{3,2,1,0:T(8,128)S(1)} %slice.109), channel_id=1, source_target_pairs={{2,4},{3,5},{6,8},{7,9},{10,12},{11,13},{14,16},{15,17},{18,20},{1... | collective-permute-start | bytes 73736 | tf_op jit(solution)/shard_map/ppermute | solution.py:362

commit v4 on v3

--- a/solution.py
+++ b/solution.py
@@ -162,7 +162,7 @@
     return [base[o] + (g[3 * o] * f[0] + g[3 * o + 1] * f[1] + g[3 * o + 2] * f[2]) for o in range(3)]
 
 
-def share_kernel(slabs, near_ref, local_ref, f_ref, base_ref, out_ref, grad, sums):
+def share_kernel(slabs, near_ref, local_ref, f_ref, base_ref, own_ref, outer_ref, inner_ref, grad, sums):
     pairs = f_ref.shape[1]
     per = pairs // CHUNKS
     slab = lax.axis_index("mesh")
@@ -270,8 +270,12 @@
                     total = add(total, TRANSVERSE * around(current[q], masks))
                 later[q] = total * fluid[q - first]
             current = later
-        for q in range(first, first + count):
-            out_ref[q - first, a] = current[q]
+        odd = slab % 2 == 1
+        for q in range(PLANES):
+            before, after = current[q - PLANES], current[q + PLANES]
+            own_ref[q, a] = current[q]
+            outer_ref[q, a] = jnp.where(odd, after, before)
+            inner_ref[q, a] = jnp.where(odd, before, after)
 
 
 def share(near, local, f_flat, base):
@@ -280,11 +284,13 @@
     return pl.pallas_call(
         functools.partial(share_kernel, slabs),
         out_shape=(
-            jax.ShapeDtypeStruct((PLANES + 2 * SWEEPS, 3, 8, 128), f32),
+            jax.ShapeDtypeStruct((PLANES, 3, 8, 128), f32),
+            jax.ShapeDtypeStruct((PLANES, 3, 8, 128), f32),
+            jax.ShapeDtypeStruct((PLANES, 3, 8, 128), f32),
             jax.ShapeDtypeStruct((9, 64, 128), f32),
         ),
         in_specs=[vmem] * 4,
-        out_specs=[vmem] * 2,
+        out_specs=[vmem] * 4,
         scratch_shapes=[pltpu.VMEM((6, 64, 128), f32)],
         compiler_params=pltpu.CompilerParams(vmem_limit_bytes=16 << 20),
         cost_estimate=pl.CostEstimate(flops=12_000_000, bytes_accessed=5_000_000, transcendentals=0),
@@ -331,38 +337,23 @@
 
 
 def body(velocity, pressure, fields, brownian):
-    total = lax.axis_size("mesh") * 4
-    mine = lax.axis_index("field")
-    low = mine < 2
-    core = mine % 2
-    cores = [[i, i + 1] for i in range(0, total, 2)]
-    inner = [[i, i + 2] for s in range(0, total, 4) for i in (s, s + 1)]
-
-    def gather(x, groups):
-        return lax.all_gather(x, AXES, axis=0, axis_index_groups=groups)
-
-    def other(x, first):
-        return jnp.where(first, x[1], x[0])
+    total = lax.axis_size("mesh") * PLANES
+
+    def exchange(x, pairs):
+        return lax.ppermute(x, AXES, pairs + [(b, a) for a, b in pairs])
 
     own = velocity.reshape(3, 8, 128)
-    faces = [(i, i + 1) for i in range(3, total - 1, 4)]
-    edge = lax.ppermute(own, AXES, faces + [(b, a) for a, b in faces])
+    edge = exchange(own, [(i, i + 1) for i in range(PLANES - 1, total - 1, PLANES)])
     f_flat, base, local = relax(own, pressure.reshape(1, 8, 128), fields, brownian)
     near = lax.all_gather(jnp.stack([own, edge]), "field", axis=0)
-    shares, grad = share(near, local, f_flat, base)
-
-    both = gather(shares, cores).reshape(2, 3, 2, 2, 3, 8, 128)
-    chip = both[0] + both[1]
-    chip = jnp.where(core == 0, chip[:, :, 0], chip[:, :, 1])
-    low_side = jnp.stack([chip[1, 0], chip[0, 0], chip[0, 1]])
-    high_side = jnp.stack([chip[1, 1], chip[2, 0], chip[2, 1]])
-    kept = jnp.where(low, low_side, high_side)
-    kept = kept + other(gather(jnp.where(low, high_side, low_side), inner), low)
-    next_to = [(i, i + 2) for i in range(total - 2) if i % 4 > 1]
-    arrived = lax.ppermute(kept[1:], AXES, next_to + [(b, a) for a, b in next_to])
-    new_fields = advance(grad, f_flat, base)
-    passed = jnp.where(low, arrived[1], arrived[0])
-    result = kept[0] + jnp.where(low, arrived[0], arrived[1]) + other(gather(passed, inner), low)
+    kept, outer, inner, grad = share(near, local, f_flat, base)
+
+    neighbours = [(i, i + PLANES) for i in range(total - PLANES)]
+    outer = exchange(outer, [p for p in neighbours if p[0] // PLANES % 2 == 1])
+    inner = exchange(inner, [p for p in neighbours if p[0] // PLANES % 2 == 0])
+    kept, new_fields = lax.optimization_barrier((kept, advance(grad, f_flat, base)))
+    parts = lax.all_to_all(kept + (outer + inner), "field", 0, 0, tiled=True)
+    result = (parts[0] + parts[1]) + (parts[2] + parts[3])
     return new_fields.reshape(fields.shape), result.reshape(velocity.shape)
 
 

time: 42.4 us -> 40 us (0.943)
  blocking collectives: 16.4 us -> 11.7 us
  starting transfers between devices: 11.3 us -> 13.9 us
    all_gather x3 -> x0, blocking collectives: 11 us -> none  [gather(): return lax.all_gather(x, AXES, axis=0, axis_index_groups=groups)]
    all_to_all x0 -> x1, blocking collectives: none -> 6.39 us  [body(): parts = lax.all_to_all(kept + (outer + inner), 'field', 0, 0, tiled=True)]
    ppermute x2 -> x3, starting transfers between devices: 11.3 us -> 13.9 us  [exchange(): return lax.ppermute(x, AXES, pairs + [(b, a) for a, b in pairs])]
    ppermute x2 -> x3, waiting for transfers between devices: 5.4 us -> 5.07 us  [exchange(): return lax.ppermute(x, AXES, pairs + [(b, a) for a, b in pairs])]
  transfers between devices with their start and end apart: 2 -> 3, of which waited for: 2 -> 3; matrix products, arithmetic and copies ran while one was open for 0% -> 0% of each run, Pallas kernels for 12% -> 13%
where the time goes in v4:
time: 40 us; the launch traced here: 39.8 us
  starting transfers between devices  13.9 us (35%)
  blocking collectives  11.7 us (29%)
  Pallas kernels  7.76 us (19%)
  waiting for transfers between devices  5.07 us (13%)
  between operations  0.69 us (2%)
  other arithmetic  0.62 us (2%)
    ppermute x3, starting transfers between devices, exchange(): return lax.ppermute(x, AXES, pairs + [(b, a) for a, b in pairs])  13.9 us
    all_to_all x1, blocking collectives, body(): parts = lax.all_to_all(kept + (outer + inner), 'field', 0, 0, tiled=True)  6.39 us
    all_gather x1, blocking collectives, body(): near = lax.all_gather(jnp.stack([own, edge]), 'field', axis=0)  5.32 us
    ppermute x3, waiting for transfers between devices, exchange(): return lax.ppermute(x, AXES, pairs + [(b, a) for a, b in pairs])  5.07 us
    pallas_call x1, Pallas kernels, relax(): pl.pallas_call(relax_kernel, out_shape=(jax.ShapeDtypeStruct(flat, bf16),...  2.89 us
    pallas_call x1, Pallas kernels, share(): pl.pallas_call(functools.partial(share_kernel, slabs), out_shape=(jax.Sha...  2.68 us
    pallas_call x1, Pallas kernels, advance(): pl.pallas_call(advance_kernel, out_shape=jax.ShapeDtypeStruct((3, n, 2, P...  2.18 us
  transfers between devices with their start and end apart: 3, of which 3 were waited for; matrix products, arithmetic and copies ran while one was open for 0% of the time, Pallas kernels for 13%

profile of v4, /device:TPU:256, one launch (start us, length us, event | category | flops | bytes accessed | tf_op | source)
XLA Modules:
  0.0 39.8 jit_solution(11510286270809289813)
XLA Ops:
  0.6 6.1 %collective-permute-start = (f32[3,8,128]{2,1,0:T(8,128)}, f32[3,8,128]{2,1,0:T(8,128)S(1)}, u32[]{:S(2)}, u32[]{:S(2)}) collective-permute-start(f32[3,8,128]{2,1,0:T(8,128)} %bitcast.13), channel_id=1, source_target_pairs={{3,4},{7,8},{11,12},{15,16},{19,20},{23,24},{27,28},{31,32},{35,36... | collective-permute-start | bytes 36872 | tf_op jit(solution)/shard_map/ppermute | solution.py:343
  6.7 0.0 copy-start
  6.7 2.9 %shard_map.59 = (bf16[3,32,8,1024]{3,2,1,0:T(8,128)(2,1)S(1)}, f32[3,32,8,1024]{3,2,1,0:T(8,128)S(1)}, f32[4,8,128]{2,1,0:T(8,128)S(1)}) custom-call(f32[3,8,128]{2,1,0:T(8,128)} %bitcast.14, f32[1,8,128]{2,1,0:T(8,128)} %bitcast.18, bf16[3,32,2,4,1024]{4,3,2,1,0:T(4,128)(2,1)} %bitcast.10, bf16[3,32,2,4,1024]{4,3,2,1,0:T(4,128)(2,1)} %bitcast.11), custom_call_target="tpu_custom_call" | custom-call | flops 10000000 | bytes 8000000 | tf_op jit(solution)/shard_map/pallas_call | solution.py:142
  9.7 1.6 %collective-permute-done = f32[3,8,128]{2,1,0:T(8,128)S(1)} collective-permute-done((f32[3,8,128]{2,1,0:T(8,128)}, f32[3,8,128]{2,1,0:T(8,128)S(1)}, u32[]{:S(2)}, u32[]{:S(2)}) %collective-permute-start) | collective-permute-done | bytes 12320 | tf_op jit(solution)/shard_map/ppermute | solution.py:343
  11.3 0.0 copy-done
  11.3 5.3 %all-gather = f32[8,3,8,128]{3,2,1,0:T(8,128)S(1)} all-gather(f32[2,3,8,128]{3,2,1,0:T(8,128)S(1)} %pad_maximum_fusion), channel_id=2, replica_groups=mesh['mesh'=128,'field'=4] {'field'}, dimensions={0}, use_global_device_ids=true | all-gather | bytes 122880 | tf_op jit(solution)/shard_map/all_gather | solution.py:348
  16.6 2.7 %shard_map.60 = (f32[4,3,8,128]{3,2,1,0:T(8,128)S(1)}, f32[4,3,8,128]{3,2,1,0:T(8,128)S(1)}, f32[4,3,8,128]{3,2,1,0:T(8,128)S(1)}, f32[9,64,128]{2,1,0:T(8,128)S(1)}) custom-call(f32[4,2,3,8,128]{4,3,2,1,0:T(8,128)S(1)} %bitcast.9, f32[4,8,128]{2,1,0:T(8,128)S(1)} %get-tuple-element.11.local_ref, bf16[3,32,8,1024]{3,2,1,0:T(8,128)(2,1)S(1)} %get-tuple-element.12.f_ref, ...), custom_call_target="tpu_custom_call" | custom-call | flops 12000000 | bytes 5000000 | tf_op jit(solution)/shard_map/pallas_call | solution.py:284
  19.3 5.9 %collective-permute-start.1 = (f32[4,3,8,128]{3,2,1,0:T(8,128)S(1)}, f32[4,3,8,128]{3,2,1,0:T(8,128)S(1)}, u32[]{:S(2)}, u32[]{:S(2)}) collective-permute-start(f32[4,3,8,128]{3,2,1,0:T(8,128)S(1)} %get-tuple-element.18), channel_id=1, source_target_pairs={{4,8},{5,9},{6,10},{7,11},{12,16},{13,17},{14,18},{15,19},{20,24},... | collective-permute-start | bytes 147464 | tf_op jit(solution)/shard_map/ppermute | solution.py:343
  25.2 1.9 %collective-permute-start.2 = (f32[4,3,8,128]{3,2,1,0:T(8,128)S(1)}, f32[4,3,8,128]{3,2,1,0:T(8,128)S(1)}, u32[]{:S(2)}, u32[]{:S(2)}) collective-permute-start(f32[4,3,8,128]{3,2,1,0:T(8,128)S(1)} %get-tuple-element.19), channel_id=1, source_target_pairs={{0,4},{1,5},{2,6},{3,7},{8,12},{9,13},{10,14},{11,15},{16,20},{17,... | collective-permute-start | bytes 147464 | tf_op jit(solution)/shard_map/ppermute | solution.py:343
  27.1 2.2 %shard_map.61 = bf16[3,32,2,4,1024]{4,3,2,1,0:T(4,128)(2,1)} custom-call(f32[9,64,128]{2,1,0:T(8,128)S(1)} %get-tuple-element.15.grad, bf16[3,32,8,1024]{3,2,1,0:T(8,128)(2,1)S(1)} %get-tuple-element.12.f_ref, f32[3,32,8,1024]{3,2,1,0:T(8,128)S(1)} %get-tuple-element.13.base_ref), custom_call_target="tpu_custom_call" | custom-call | flops 6000000 | bytes 6000000 | tf_op jit(solution)/shard_map/pallas_call | solution.py:328
  29.3 2.3 %collective-permute-done.1 = f32[4,3,8,128]{3,2,1,0:T(8,128)S(1)} collective-permute-done((f32[4,3,8,128]{3,2,1,0:T(8,128)S(1)}, f32[4,3,8,128]{3,2,1,0:T(8,128)S(1)}, u32[]{:S(2)}, u32[]{:S(2)}) %collective-permute-start.1) | collective-permute-done | bytes 49184 | tf_op jit(solution)/shard_map/ppermute | solution.py:343
  31.6 1.2 %collective-permute-done.2 = f32[4,3,8,128]{3,2,1,0:T(8,128)S(1)} collective-permute-done((f32[4,3,8,128]{3,2,1,0:T(8,128)S(1)}, f32[4,3,8,128]{3,2,1,0:T(8,128)S(1)}, u32[]{:S(2)}, u32[]{:S(2)}) %collective-permute-start.2) | collective-permute-done | bytes 49184 | tf_op jit(solution)/shard_map/ppermute | solution.py:343
  32.8 6.4 %all_to_all.5 = f32[4,3,8,128]{3,2,1,0:T(8,128)S(1)} all-to-all(f32[4,3,8,128]{3,2,1,0:T(8,128)S(1)} %add_add_fusion), channel_id=1, replica_groups=mesh['mesh'=128,'field'=4] {'field'}, dimensions={0} | all-to-all | bytes 98304 | tf_op jit(solution)/shard_map/all_to_all | solution.py:355
  39.2 0.6 %fusion = f32[1,3,8,128]{3,2,1,0:T(8,128)} fusion(f32[4,3,8,128]{3,2,1,0:T(8,128)S(1)} %all_to_all.5), kind=kLoop, calls=%fused_computation.3 | loop fusion | flops 9216 | bytes 61440 | tf_op jit(solution)/shard_map/add | solution.py:356
  (2 shorter events, 0.0 us)
Async XLA Ops:
  0.6 10.7 %collective-permute-start = (f32[3,8,128]{2,1,0:T(8,128)}, f32[3,8,128]{2,1,0:T(8,128)S(1)}, u32[]{:S(2)}, u32[]{:S(2)}) collective-permute-start(f32[3,8,128]{2,1,0:T(8,128)} %bitcast.13), channel_id=1, source_target_pairs={{3,4},{7,8},{11,12},{15,16},{19,20},{23,24},{27,28},{31,32},{35,36... | collective-permute-start | bytes 36872 | tf_op jit(solution)/shard_map/ppermute | solution.py:343
  6.7 4.5 %copy-start = (f32[3,1,1024]{2,1,0:T(1,128)S(1)}, f32[3,1,1024]{2,1,0:T(1,128)}, u32[]{:S(2)}) copy-start(f32[3,1,1024]{2,1,0:T(1,128)} %param.4) | copy-start | bytes 36868
  19.3 12.3 %collective-permute-start.1 = (f32[4,3,8,128]{3,2,1,0:T(8,128)S(1)}, f32[4,3,8,128]{3,2,1,0:T(8,128)S(1)}, u32[]{:S(2)}, u32[]{:S(2)}) collective-permute-start(f32[4,3,8,128]{3,2,1,0:T(8,128)S(1)} %get-tuple-element.18), channel_id=1, source_target_pairs={{4,8},{5,9},{6,10},{7,11},{12,16},{13,17},{14,18},{15,19},{20,24},... | collective-permute-start | bytes 147464 | tf_op jit(solution)/shard_map/ppermute | solution.py:343
  25.2 7.6 %collective-permute-start.2 = (f32[4,3,8,128]{3,2,1,0:T(8,128)S(1)}, f32[4,3,8,128]{3,2,1,0:T(8,128)S(1)}, u32[]{:S(2)}, u32[]{:S(2)}) collective-permute-start(f32[4,3,8,128]{3,2,1,0:T(8,128)S(1)} %get-tuple-element.19), channel_id=1, source_target_pairs={{0,4},{1,5},{2,6},{3,7},{8,12},{9,13},{10,14},{11,15},{16,20},{17,... | collective-permute-start | bytes 147464 | tf_op jit(solution)/shard_map/ppermute | solution.py:343

commit v5 on v4

--- a/solution.py
+++ b/solution.py
@@ -25,6 +25,7 @@
 
 PLANES = 4
 CHUNKS = 4
+PARTS = 2
 AXES = ("mesh", "field")
 
 
@@ -164,7 +165,7 @@
 
 def share_kernel(slabs, near_ref, local_ref, f_ref, base_ref, own_ref, outer_ref, inner_ref, grad, sums):
     pairs = f_ref.shape[1]
-    per = pairs // CHUNKS
+    per = pairs // PARTS
     slab = lax.axis_index("mesh")
     mine = lax.axis_index("field")
     masks = lane_masks()
@@ -179,7 +180,7 @@
                 grad[3 * a + c, pl.ds(q, 8, stride=8), :] = value
                 grad[3 * a + c, pl.ds(q + 4, 8, stride=8), :] = value
 
-    for ch in range(CHUNKS):
+    for ch in range(PARTS):
 
         def block(j, carry):
             rows = pl.ds(pl.multiple_of(8 * j, 8), 8)
@@ -349,8 +350,8 @@
     kept, outer, inner, grad = share(near, local, f_flat, base)
 
     neighbours = [(i, i + PLANES) for i in range(total - PLANES)]
+    inner = exchange(inner, [p for p in neighbours if p[0] // PLANES % 2 == 0])
     outer = exchange(outer, [p for p in neighbours if p[0] // PLANES % 2 == 1])
-    inner = exchange(inner, [p for p in neighbours if p[0] // PLANES % 2 == 0])
     kept, new_fields = lax.optimization_barrier((kept, advance(grad, f_flat, base)))
     parts = lax.all_to_all(kept + (outer + inner), "field", 0, 0, tiled=True)
     result = (parts[0] + parts[1]) + (parts[2] + parts[3])

time: 40 us -> 39.9 us (level)
  no operation moved by 1% of the time
where the time goes in v5:
time: 39.9 us; the launch traced here: 39.7 us
  starting transfers between devices  13.9 us (35%)
  blocking collectives  11.7 us (29%)
  Pallas kernels  7.65 us (19%)
  waiting for transfers between devices  5.07 us (13%)
  between operations  0.69 us (2%)
  other arithmetic  0.62 us (2%)
    ppermute x3, starting transfers between devices, exchange(): return lax.ppermute(x, AXES, pairs + [(b, a) for a, b in pairs])  13.9 us
    all_to_all x1, blocking collectives, body(): parts = lax.all_to_all(kept + (outer + inner), 'field', 0, 0, tiled=True)  6.39 us
    all_gather x1, blocking collectives, body(): near = lax.all_gather(jnp.stack([own, edge]), 'field', axis=0)  5.32 us
    ppermute x3, waiting for transfers between devices, exchange(): return lax.ppermute(x, AXES, pairs + [(b, a) for a, b in pairs])  5.07 us
    pallas_call x1, Pallas kernels, relax(): pl.pallas_call(relax_kernel, out_shape=(jax.ShapeDtypeStruct(flat, bf16),...  2.89 us
    pallas_call x1, Pallas kernels, share(): pl.pallas_call(functools.partial(share_kernel, slabs), out_shape=(jax.Sha...  2.58 us
    pallas_call x1, Pallas kernels, advance(): pl.pallas_call(advance_kernel, out_shape=jax.ShapeDtypeStruct((3, n, 2, P...  2.18 us
  transfers between devices with their start and end apart: 3, of which 3 were waited for; matrix products, arithmetic and copies ran while one was open for 0% of the time, Pallas kernels for 13%

profile of v5, /device:TPU:256, one launch (start us, length us, event | category | flops | bytes accessed | tf_op | source)
XLA Modules:
  0.0 39.7 jit_solution(3673157498862751818)
XLA Ops:
  0.6 6.1 %collective-permute-start = (f32[3,8,128]{2,1,0:T(8,128)}, f32[3,8,128]{2,1,0:T(8,128)S(1)}, u32[]{:S(2)}, u32[]{:S(2)}) collective-permute-start(f32[3,8,128]{2,1,0:T(8,128)} %bitcast.13), channel_id=1, source_target_pairs={{3,4},{7,8},{11,12},{15,16},{19,20},{23,24},{27,28},{31,32},{35,36... | collective-permute-start | bytes 36872 | tf_op jit(solution)/shard_map/ppermute | solution.py:344
  6.7 0.0 copy-start
  6.7 2.9 %shard_map.59 = (bf16[3,32,8,1024]{3,2,1,0:T(8,128)(2,1)S(1)}, f32[3,32,8,1024]{3,2,1,0:T(8,128)S(1)}, f32[4,8,128]{2,1,0:T(8,128)S(1)}) custom-call(f32[3,8,128]{2,1,0:T(8,128)} %bitcast.14, f32[1,8,128]{2,1,0:T(8,128)} %bitcast.18, bf16[3,32,2,4,1024]{4,3,2,1,0:T(4,128)(2,1)} %bitcast.10, bf16[3,32,2,4,1024]{4,3,2,1,0:T(4,128)(2,1)} %bitcast.11), custom_call_target="tpu_custom_call" | custom-call | flops 10000000 | bytes 8000000 | tf_op jit(solution)/shard_map/pallas_call | solution.py:143
  9.7 1.6 %collective-permute-done = f32[3,8,128]{2,1,0:T(8,128)S(1)} collective-permute-done((f32[3,8,128]{2,1,0:T(8,128)}, f32[3,8,128]{2,1,0:T(8,128)S(1)}, u32[]{:S(2)}, u32[]{:S(2)}) %collective-permute-start) | collective-permute-done | bytes 12320 | tf_op jit(solution)/shard_map/ppermute | solution.py:344
  11.3 0.0 copy-done
  11.3 5.3 %all-gather = f32[8,3,8,128]{3,2,1,0:T(8,128)S(1)} all-gather(f32[2,3,8,128]{3,2,1,0:T(8,128)S(1)} %pad_maximum_fusion), channel_id=2, replica_groups=mesh['mesh'=128,'field'=4] {'field'}, dimensions={0}, use_global_device_ids=true | all-gather | bytes 122880 | tf_op jit(solution)/shard_map/all_gather | solution.py:349
  16.6 2.6 %shard_map.60 = (f32[4,3,8,128]{3,2,1,0:T(8,128)S(1)}, f32[4,3,8,128]{3,2,1,0:T(8,128)S(1)}, f32[4,3,8,128]{3,2,1,0:T(8,128)S(1)}, f32[9,64,128]{2,1,0:T(8,128)S(1)}) custom-call(f32[4,2,3,8,128]{4,3,2,1,0:T(8,128)S(1)} %bitcast.9, f32[4,8,128]{2,1,0:T(8,128)S(1)} %get-tuple-element.11.local_ref, bf16[3,32,8,1024]{3,2,1,0:T(8,128)(2,1)S(1)} %get-tuple-element.12.f_ref, ...), custom_call_target="tpu_custom_call" | custom-call | flops 12000000 | bytes 5000000 | tf_op jit(solution)/shard_map/pallas_call | solution.py:285
  19.2 5.9 %collective-permute-start.1 = (f32[4,3,8,128]{3,2,1,0:T(8,128)S(1)}, f32[4,3,8,128]{3,2,1,0:T(8,128)S(1)}, u32[]{:S(2)}, u32[]{:S(2)}) collective-permute-start(f32[4,3,8,128]{3,2,1,0:T(8,128)S(1)} %get-tuple-element.18), channel_id=1, source_target_pairs={{4,8},{5,9},{6,10},{7,11},{12,16},{13,17},{14,18},{15,19},{20,24},... | collective-permute-start | bytes 147464 | tf_op jit(solution)/shard_map/ppermute | solution.py:344
  25.1 1.9 %collective-permute-start.2 = (f32[4,3,8,128]{3,2,1,0:T(8,128)S(1)}, f32[4,3,8,128]{3,2,1,0:T(8,128)S(1)}, u32[]{:S(2)}, u32[]{:S(2)}) collective-permute-start(f32[4,3,8,128]{3,2,1,0:T(8,128)S(1)} %get-tuple-element.19), channel_id=1, source_target_pairs={{0,4},{1,5},{2,6},{3,7},{8,12},{9,13},{10,14},{11,15},{16,20},{17,... | collective-permute-start | bytes 147464 | tf_op jit(solution)/shard_map/ppermute | solution.py:344
  27.0 2.2 %shard_map.61 = bf16[3,32,2,4,1024]{4,3,2,1,0:T(4,128)(2,1)} custom-call(f32[9,64,128]{2,1,0:T(8,128)S(1)} %get-tuple-element.15.grad, bf16[3,32,8,1024]{3,2,1,0:T(8,128)(2,1)S(1)} %get-tuple-element.12.f_ref, f32[3,32,8,1024]{3,2,1,0:T(8,128)S(1)} %get-tuple-element.13.base_ref), custom_call_target="tpu_custom_call" | custom-call | flops 6000000 | bytes 6000000 | tf_op jit(solution)/shard_map/pallas_call | solution.py:329
  29.2 2.3 %collective-permute-done.1 = f32[4,3,8,128]{3,2,1,0:T(8,128)S(1)} collective-permute-done((f32[4,3,8,128]{3,2,1,0:T(8,128)S(1)}, f32[4,3,8,128]{3,2,1,0:T(8,128)S(1)}, u32[]{:S(2)}, u32[]{:S(2)}) %collective-permute-start.1) | collective-permute-done | bytes 49184 | tf_op jit(solution)/shard_map/ppermute | solution.py:344
  31.5 1.2 %collective-permute-done.2 = f32[4,3,8,128]{3,2,1,0:T(8,128)S(1)} collective-permute-done((f32[4,3,8,128]{3,2,1,0:T(8,128)S(1)}, f32[4,3,8,128]{3,2,1,0:T(8,128)S(1)}, u32[]{:S(2)}, u32[]{:S(2)}) %collective-permute-start.2) | collective-permute-done | bytes 49184 | tf_op jit(solution)/shard_map/ppermute | solution.py:344
  32.7 6.4 %all_to_all.5 = f32[4,3,8,128]{3,2,1,0:T(8,128)S(1)} all-to-all(f32[4,3,8,128]{3,2,1,0:T(8,128)S(1)} %add_add_fusion), channel_id=1, replica_groups=mesh['mesh'=128,'field'=4] {'field'}, dimensions={0} | all-to-all | bytes 98304 | tf_op jit(solution)/shard_map/all_to_all | solution.py:356
  39.1 0.6 %fusion = f32[1,3,8,128]{3,2,1,0:T(8,128)} fusion(f32[4,3,8,128]{3,2,1,0:T(8,128)S(1)} %all_to_all.5), kind=kLoop, calls=%fused_computation.3 | loop fusion | flops 9216 | bytes 61440 | tf_op jit(solution)/shard_map/add | solution.py:357
  (2 shorter events, 0.0 us)
Async XLA Ops:
  0.6 10.7 %collective-permute-start = (f32[3,8,128]{2,1,0:T(8,128)}, f32[3,8,128]{2,1,0:T(8,128)S(1)}, u32[]{:S(2)}, u32[]{:S(2)}) collective-permute-start(f32[3,8,128]{2,1,0:T(8,128)} %bitcast.13), channel_id=1, source_target_pairs={{3,4},{7,8},{11,12},{15,16},{19,20},{23,24},{27,28},{31,32},{35,36... | collective-permute-start | bytes 36872 | tf_op jit(solution)/shard_map/ppermute | solution.py:344
  6.7 4.5 %copy-start = (f32[3,1,1024]{2,1,0:T(1,128)S(1)}, f32[3,1,1024]{2,1,0:T(1,128)}, u32[]{:S(2)}) copy-start(f32[3,1,1024]{2,1,0:T(1,128)} %param.4) | copy-start | bytes 36868
  19.2 12.3 %collective-permute-start.1 = (f32[4,3,8,128]{3,2,1,0:T(8,128)S(1)}, f32[4,3,8,128]{3,2,1,0:T(8,128)S(1)}, u32[]{:S(2)}, u32[]{:S(2)}) collective-permute-start(f32[4,3,8,128]{3,2,1,0:T(8,128)S(1)} %get-tuple-element.18), channel_id=1, source_target_pairs={{4,8},{5,9},{6,10},{7,11},{12,16},{13,17},{14,18},{15,19},{20,24},... | collective-permute-start | bytes 147464 | tf_op jit(solution)/shard_map/ppermute | solution.py:344
  25.1 7.6 %collective-permute-start.2 = (f32[4,3,8,128]{3,2,1,0:T(8,128)S(1)}, f32[4,3,8,128]{3,2,1,0:T(8,128)S(1)}, u32[]{:S(2)}, u32[]{:S(2)}) collective-permute-start(f32[4,3,8,128]{3,2,1,0:T(8,128)S(1)} %get-tuple-element.19), channel_id=1, source_target_pairs={{0,4},{1,5},{2,6},{3,7},{8,12},{9,13},{10,14},{11,15},{16,20},{17,... | collective-permute-start | bytes 147464 | tf_op jit(solution)/shard_map/ppermute | solution.py:344

commit v6 on v4

--- a/solution.py
+++ b/solution.py
@@ -162,7 +162,9 @@
     return [base[o] + (g[3 * o] * f[0] + g[3 * o + 1] * f[1] + g[3 * o + 2] * f[2]) for o in range(3)]
 
 
-def share_kernel(slabs, near_ref, local_ref, f_ref, base_ref, own_ref, outer_ref, inner_ref, grad, sums):
+def share_kernel(
+    slabs, near_ref, local_ref, f_ref, base_ref, nf_hbm, own_ref, outer_ref, inner_ref, n_buf, grad, sums, sem
+):
     pairs = f_ref.shape[1]
     per = pairs // CHUNKS
     slab = lax.axis_index("mesh")
@@ -193,6 +195,8 @@
                 n = ch * per + u
                 f = [f_ref[c, n, :, lanes].astype(f32) for c in range(3)]
                 a = stretch(f, [base_ref[o, n, :, lanes] for o in range(3)], g)
+                for c in range(3):
+                    n_buf[c, n, :, lanes] = a[c].astype(bf16)
                 s = [x * x for x in a]
                 r = pltpu.reciprocal(MAX_STRETCH - (s[0] + s[1] + s[2]))
                 p0 = r * a[0]
@@ -204,6 +208,8 @@
             return carry
 
         lax.fori_loop(0, 8, block, 0)
+        for copy in stores(ch, n_buf, nf_hbm, sem):
+            copy.start()
 
     scale = VISCOSITY / WEISSENBERG / NF * MAX_STRETCH
     stress = []
@@ -277,63 +283,30 @@
             outer_ref[q, a] = jnp.where(odd, after, before)
             inner_ref[q, a] = jnp.where(odd, before, after)
 
-
-def share(near, local, f_flat, base):
-    slabs = lax.axis_size("mesh")
-    vmem = pl.BlockSpec(memory_space=pltpu.VMEM)
-    return pl.pallas_call(
-        functools.partial(share_kernel, slabs),
-        out_shape=(
-            jax.ShapeDtypeStruct((PLANES, 3, 8, 128), f32),
-            jax.ShapeDtypeStruct((PLANES, 3, 8, 128), f32),
-            jax.ShapeDtypeStruct((PLANES, 3, 8, 128), f32),
-            jax.ShapeDtypeStruct((9, 64, 128), f32),
-        ),
-        in_specs=[vmem] * 4,
-        out_specs=[vmem] * 4,
-        scratch_shapes=[pltpu.VMEM((6, 64, 128), f32)],
-        compiler_params=pltpu.CompilerParams(vmem_limit_bytes=16 << 20),
-        cost_estimate=pl.CostEstimate(flops=12_000_000, bytes_accessed=5_000_000, transcendentals=0),
-    )(near, local, f_flat, base)
-
-
-def advance_kernel(grad, f_ref, base_ref, nf_hbm, n_buf, sem):
-    pairs = n_buf.shape[1]
-    per = pairs // CHUNKS
-    for ch in range(CHUNKS):
-
-        def block(j, carry):
-            rows = pl.ds(pl.multiple_of(8 * j, 8), 8)
-            lanes = pl.ds(pl.multiple_of(128 * j, 128), 128)
-            g = [grad[k, rows, :] for k in range(9)]
-            for u in range(per):
-                n = ch * per + u
-                f = [f_ref[c, n, :, lanes].astype(f32) for c in range(3)]
-                a = stretch(f, [base_ref[o, n, :, lanes] for o in range(3)], g)
-                for c in range(3):
-                    n_buf[c, n, :, lanes] = a[c].astype(bf16)
-            return carry
-
-        lax.fori_loop(0, 8, block, 0)
-        for copy in stores(ch, n_buf, nf_hbm, sem):
-            copy.start()
     for ch in range(CHUNKS):
         for copy in stores(ch, n_buf, nf_hbm, sem):
             copy.wait()
 
 
-def advance(grad, f_flat, base):
+def share(near, local, f_flat, base):
     n = f_flat.shape[1]
+    slabs = lax.axis_size("mesh")
     vmem = pl.BlockSpec(memory_space=pltpu.VMEM)
+    part = jax.ShapeDtypeStruct((PLANES, 3, 8, 128), f32)
     return pl.pallas_call(
-        advance_kernel,
-        out_shape=jax.ShapeDtypeStruct((3, n, 2, PLANES, 1024), bf16),
-        in_specs=[vmem] * 3,
-        out_specs=pl.BlockSpec(memory_space=pl.ANY),
-        scratch_shapes=[pltpu.VMEM((3, n, 8, 1024), bf16), pltpu.SemaphoreType.DMA((CHUNKS, 6))],
+        functools.partial(share_kernel, slabs),
+        out_shape=(jax.ShapeDtypeStruct((3, n, 2, PLANES, 1024), bf16), part, part, part),
+        in_specs=[vmem] * 4,
+        out_specs=[pl.BlockSpec(memory_space=pl.ANY), vmem, vmem, vmem],
+        scratch_shapes=[
+            pltpu.VMEM((3, n, 8, 1024), bf16),
+            pltpu.VMEM((9, 64, 128), f32),
+            pltpu.VMEM((6, 64, 128), f32),
+            pltpu.SemaphoreType.DMA((CHUNKS, 6)),
+        ],
         compiler_params=pltpu.CompilerParams(vmem_limit_bytes=16 << 20),
-        cost_estimate=pl.CostEstimate(flops=6_000_000, bytes_accessed=6_000_000, transcendentals=0),
-    )(grad, f_flat, base)
+        cost_estimate=pl.CostEstimate(flops=13_000_000, bytes_accessed=7_000_000, transcendentals=0),
+    )(near, local, f_flat, base)
 
 
 def body(velocity, pressure, fields, brownian):
@@ -346,12 +319,12 @@
     edge = exchange(own, [(i, i + 1) for i in range(PLANES - 1, total - 1, PLANES)])
     f_flat, base, local = relax(own, pressure.reshape(1, 8, 128), fields, brownian)
     near = lax.all_gather(jnp.stack([own, edge]), "field", axis=0)
-    kept, outer, inner, grad = share(near, local, f_flat, base)
-
-    neighbours = [(i, i + PLANES) for i in range(total - PLANES)]
-    outer = exchange(outer, [p for p in neighbours if p[0] // PLANES % 2 == 1])
-    inner = exchange(inner, [p for p in neighbours if p[0] // PLANES % 2 == 0])
-    kept, new_fields = lax.optimization_barrier((kept, advance(grad, f_flat, base)))
+    new_fields, kept, outer, inner = share(near, local, f_flat, base)
+
+    outer = exchange(outer, [(i, i + PLANES) for i in range(total - PLANES) if i // PLANES % 2 == 1])
+    couples = [[i, i + PLANES] for i in range(total) if i // PLANES % 2 == 0]
+    both = lax.all_gather(inner, AXES, axis=0, axis_index_groups=couples)
+    inner = jnp.where(lax.axis_index("mesh") % 2 == 1, both[0], both[1])
     parts = lax.all_to_all(kept + (outer + inner), "field", 0, 0, tiled=True)
     result = (parts[0] + parts[1]) + (parts[2] + parts[3])
     return new_fields.reshape(fields.shape), result.reshape(velocity.shape)

time: 40 us -> 39.3 us (0.982)
  blocking collectives: 11.7 us -> 18.1 us
  waiting for transfers between devices: 5.07 us -> 1.68 us
  starting transfers between devices: 13.9 us -> 12 us
  Pallas kernels: 7.76 us -> 6.07 us
    all_gather x0 -> x1, blocking collectives: none -> 6.34 us  [body(): both = lax.all_gather(inner, AXES, axis=0, axis_index_groups=couples)]
    ppermute x3 -> x2, waiting for transfers between devices: 5.07 us -> 1.68 us  [exchange(): return lax.ppermute(x, AXES, pairs + [(b, a) for a, b in pairs])]
    pallas_call x1 -> x0, Pallas kernels: 2.18 us -> none  [advance(): pl.pallas_call(advance_kernel, out_shape=jax.ShapeDtypeStruct((3, n, 2, P...]
    ppermute x3 -> x2, starting transfers between devices: 13.9 us -> 12 us  [exchange(): return lax.ppermute(x, AXES, pairs + [(b, a) for a, b in pairs])]
    pallas_call x1, Pallas kernels: 2.68 us -> 3.18 us  [share(): pl.pallas_call(functools.partial(share_kernel, slabs), out_shape=(jax.Sha...]
  transfers between devices with their start and end apart: 3 -> 2, of which waited for: 3 -> 1; matrix products, arithmetic and copies ran while one was open for 0% -> 0% of each run, Pallas kernels for 13% -> 7%
where the time goes in v6:
time: 39.3 us; the launch traced here: 39.1 us
  blocking collectives  18.1 us (46%)
  starting transfers between devices  12 us (31%)
  Pallas kernels  6.07 us (15%)
  waiting for transfers between devices  1.68 us (4%)
  between operations  0.69 us (2%)
  other arithmetic  0.62 us (2%)
    ppermute x2, starting transfers between devices, exchange(): return lax.ppermute(x, AXES, pairs + [(b, a) for a, b in pairs])  12 us
    all_to_all x1, blocking collectives, body(): parts = lax.all_to_all(kept + (outer + inner), 'field', 0, 0, tiled=True)  6.39 us
    all_gather x1, blocking collectives, body(): both = lax.all_gather(inner, AXES, axis=0, axis_index_groups=couples)  6.34 us
    all_gather x1, blocking collectives, body(): near = lax.all_gather(jnp.stack([own, edge]), 'field', axis=0)  5.32 us
    pallas_call x1, Pallas kernels, share(): pl.pallas_call(functools.partial(share_kernel, slabs), out_shape=(jax.Sha...  3.18 us
    pallas_call x1, Pallas kernels, relax(): pl.pallas_call(relax_kernel, out_shape=(jax.ShapeDtypeStruct(flat, bf16),...  2.89 us
    ppermute x2, waiting for transfers between devices, exchange(): return lax.ppermute(x, AXES, pairs + [(b, a) for a, b in pairs])  1.68 us
  transfers between devices with their start and end apart: 2, of which 1 were waited for; matrix products, arithmetic and copies ran while one was open for 0% of the time, Pallas kernels for 7%

profile of v6, /device:TPU:256, one launch (start us, length us, event | category | flops | bytes accessed | tf_op | source)
XLA Modules:
  0.0 39.1 jit_solution(4065752647753551750)
XLA Ops:
  0.6 6.1 %collective-permute-start = (f32[3,8,128]{2,1,0:T(8,128)}, f32[3,8,128]{2,1,0:T(8,128)S(1)}, u32[]{:S(2)}, u32[]{:S(2)}) collective-permute-start(f32[3,8,128]{2,1,0:T(8,128)} %bitcast.12), channel_id=1, source_target_pairs={{3,4},{7,8},{11,12},{15,16},{19,20},{23,24},{27,28},{31,32},{35,36... | collective-permute-start | bytes 36872 | tf_op jit(solution)/shard_map/ppermute | solution.py:316
  6.7 0.0 copy-start
  6.7 2.9 %shard_map.59 = (bf16[3,32,8,1024]{3,2,1,0:T(8,128)(2,1)S(1)}, f32[3,32,8,1024]{3,2,1,0:T(8,128)S(1)}, f32[4,8,128]{2,1,0:T(8,128)S(1)}) custom-call(f32[3,8,128]{2,1,0:T(8,128)} %bitcast.13, f32[1,8,128]{2,1,0:T(8,128)} %bitcast.17, bf16[3,32,2,4,1024]{4,3,2,1,0:T(4,128)(2,1)} %bitcast.10, bf16[3,32,2,4,1024]{4,3,2,1,0:T(4,128)(2,1)} %bitcast.11), custom_call_target="tpu_custom_call" | custom-call | flops 10000000 | bytes 8000000 | tf_op jit(solution)/shard_map/pallas_call | solution.py:142
  9.7 1.6 %collective-permute-done = f32[3,8,128]{2,1,0:T(8,128)S(1)} collective-permute-done((f32[3,8,128]{2,1,0:T(8,128)}, f32[3,8,128]{2,1,0:T(8,128)S(1)}, u32[]{:S(2)}, u32[]{:S(2)}) %collective-permute-start) | collective-permute-done | bytes 12320 | tf_op jit(solution)/shard_map/ppermute | solution.py:316
  11.3 0.0 copy-done
  11.3 5.3 %all-gather = f32[8,3,8,128]{3,2,1,0:T(8,128)S(1)} all-gather(f32[2,3,8,128]{3,2,1,0:T(8,128)S(1)} %pad_maximum_fusion), channel_id=2, replica_groups=mesh['mesh'=128,'field'=4] {'field'}, dimensions={0}, use_global_device_ids=true | all-gather | bytes 122880 | tf_op jit(solution)/shard_map/all_gather | solution.py:321
  16.6 3.2 %shard_map.60 = (bf16[3,32,2,4,1024]{4,3,2,1,0:T(4,128)(2,1)}, f32[4,3,8,128]{3,2,1,0:T(8,128)S(1)}, f32[4,3,8,128]{3,2,1,0:T(8,128)S(1)}, f32[4,3,8,128]{3,2,1,0:T(8,128)S(1)}) custom-call(f32[4,2,3,8,128]{4,3,2,1,0:T(8,128)S(1)} %bitcast.9, f32[4,8,128]{2,1,0:T(8,128)S(1)} %get-tuple-element.9.local_ref, ...), custom_call_target="tpu_custom_call" | custom-call | flops 13000000 | bytes 7000000 | tf_op jit(solution)/shard_map/pallas_call | solution.py:296
  19.8 5.9 %collective-permute-start.1 = (f32[4,3,8,128]{3,2,1,0:T(8,128)S(1)}, f32[4,3,8,128]{3,2,1,0:T(8,128)S(1)}, u32[]{:S(2)}, u32[]{:S(2)}) collective-permute-start(f32[4,3,8,128]{3,2,1,0:T(8,128)S(1)} %get-tuple-element.14), channel_id=1, source_target_pairs={{4,8},{5,9},{6,10},{7,11},{12,16},{13,17},{14,18},{15,19},{20,24},... | collective-permute-start | bytes 147464 | tf_op jit(solution)/shard_map/ppermute | solution.py:316
  25.7 6.3 %all-gather.1 = f32[8,3,8,128]{3,2,1,0:T(8,128)S(1)} all-gather(f32[4,3,8,128]{3,2,1,0:T(8,128)S(1)} %get-tuple-element.15), channel_id=3, replica_groups={{0,4},{1,5},{2,6},{3,7},{8,12},{9,13},{10,14},{11,15},{16,20},{17,21},{..., dimensions={0}, use_global_device_ids=true | all-gather | bytes 147456 | tf_op jit(solution)/shard_map/all_gather | solution.py:326
  32.1 0.0 collective-permute-done.1
  32.1 6.4 %all_to_all.5 = f32[4,3,8,128]{3,2,1,0:T(8,128)S(1)} all-to-all(f32[4,3,8,128]{3,2,1,0:T(8,128)S(1)} %fusion.1), channel_id=1, replica_groups=mesh['mesh'=128,'field'=4] {'field'}, dimensions={0} | all-to-all | bytes 98304 | tf_op jit(solution)/shard_map/all_to_all | solution.py:328
  38.5 0.6 %fusion.2 = f32[1,3,8,128]{3,2,1,0:T(8,128)} fusion(f32[4,3,8,128]{3,2,1,0:T(8,128)S(1)} %all_to_all.5), kind=kLoop, calls=%fused_computation.5 | loop fusion | flops 9216 | bytes 61440 | tf_op jit(solution)/shard_map/add | solution.py:329
  (2 shorter events, 0.0 us)
Async XLA Ops:
  0.6 10.7 %collective-permute-start = (f32[3,8,128]{2,1,0:T(8,128)}, f32[3,8,128]{2,1,0:T(8,128)S(1)}, u32[]{:S(2)}, u32[]{:S(2)}) collective-permute-start(f32[3,8,128]{2,1,0:T(8,128)} %bitcast.12), channel_id=1, source_target_pairs={{3,4},{7,8},{11,12},{15,16},{19,20},{23,24},{27,28},{31,32},{35,36... | collective-permute-start | bytes 36872 | tf_op jit(solution)/shard_map/ppermute | solution.py:316
  6.7 4.5 %copy-start = (f32[3,1,1024]{2,1,0:T(1,128)S(1)}, f32[3,1,1024]{2,1,0:T(1,128)}, u32[]{:S(2)}) copy-start(f32[3,1,1024]{2,1,0:T(1,128)} %param.4) | copy-start | bytes 36868
  19.8 12.3 %collective-permute-start.1 = (f32[4,3,8,128]{3,2,1,0:T(8,128)S(1)}, f32[4,3,8,128]{3,2,1,0:T(8,128)S(1)}, u32[]{:S(2)}, u32[]{:S(2)}) collective-permute-start(f32[4,3,8,128]{3,2,1,0:T(8,128)S(1)} %get-tuple-element.14), channel_id=1, source_target_pairs={{4,8},{5,9},{6,10},{7,11},{12,16},{13,17},{14,18},{15,19},{20,24},... | collective-permute-start | bytes 147464 | tf_op jit(solution)/shard_map/ppermute | solution.py:316

commit v7 on v6

--- a/solution.py
+++ b/solution.py
@@ -24,7 +24,8 @@
 DIAGONAL_PAIRS = (0, 3, 5)
 
 PLANES = 4
-CHUNKS = 4
+BLOCKS = 8
+UNROLL = 16
 AXES = ("mesh", "field")
 
 
@@ -72,59 +73,62 @@
     return (y_plus + y_minus) + (z_plus + z_minus)
 
 
-def chunk(ch, pairs):
-    per = pairs // CHUNKS
-    return pl.ds(ch * per, per)
-
-
-def loads(ch, sources, buffers, sem):
-    some = chunk(ch, buffers[0].shape[1])
+def lanes_of(j):
+    return pl.ds(pl.multiple_of(128 * j, 128), 128)
+
+
+def loads(j, sources, buffers, sem):
+    lanes = lanes_of(j)
     return [
-        pltpu.make_async_copy(src.at[c, some, h], buf.at[c, some, pl.ds(4 * h, 4), :], sem.at[ch, 6 * w + 2 * c + h])
+        pltpu.make_async_copy(src.at[:, :, h, :, lanes], buf.at[:, :, pl.ds(4 * h, 4), lanes], sem.at[j, 2 * w + h])
         for w, (src, buf) in enumerate(zip(sources, buffers))
-        for c in range(3)
         for h in range(2)
     ]
 
 
-def stores(ch, buf, dst, sem):
-    some = chunk(ch, buf.shape[1])
+def stores(j, buf, dst, sem):
+    lanes = lanes_of(j)
     return [
-        pltpu.make_async_copy(buf.at[c, some, pl.ds(4 * h, 4), :], dst.at[c, some, h], sem.at[ch, 2 * c + h])
-        for c in range(3)
+        pltpu.make_async_copy(buf.at[:, :, pl.ds(4 * h, 4), lanes], dst.at[:, :, h, :, lanes], sem.at[j, h])
         for h in range(2)
     ]
 
 
 def relax_kernel(velocity_hbm, pressure_hbm, f_hbm, b_hbm, f_ref, base_ref, local_ref, b_buf, sem, local_sem):
     pairs = b_buf.shape[1]
-    per = pairs // CHUNKS
-    for ch in range(CHUNKS):
-        for copy in loads(ch, (f_hbm, b_hbm), (f_ref, b_buf), sem):
+
+    def begin(j, carry):
+        for copy in loads(j, (f_hbm, b_hbm), (f_ref, b_buf), sem):
             copy.start()
+        return carry
+
+    lax.fori_loop(0, BLOCKS, begin, 0)
     own = (
         pltpu.make_async_copy(velocity_hbm, local_ref.at[pl.ds(0, 3)], local_sem.at[0]),
         pltpu.make_async_copy(pressure_hbm, local_ref.at[pl.ds(3, 1)], local_sem.at[1]),
     )
     for copy in own:
         copy.start()
-    for ch in range(CHUNKS):
-        for copy in loads(ch, (f_hbm, b_hbm), (f_ref, b_buf), sem):
+
+    def block(j, carry):
+        lanes = lanes_of(j)
+        for copy in loads(j, (f_hbm, b_hbm), (f_ref, b_buf), sem):
             copy.wait()
 
-        def block(j, carry):
-            lanes = pl.ds(pl.multiple_of(128 * j, 128), 128)
-            for u in range(per):
-                n = ch * per + u
+        def some(i, inner):
+            for u in range(UNROLL):
+                n = i * UNROLL + u
                 f = [f_ref[c, n, :, lanes].astype(f32) for c in range(3)]
                 length_sq = f[0] * f[0] + f[1] * f[1] + f[2] * f[2]
                 pull = TIME_STEP * MAX_STRETCH / (2.0 * WEISSENBERG) * pltpu.reciprocal(MAX_STRETCH - length_sq)
                 kept = 1.0 - pull
                 for c in range(3):
                     base_ref[c, n, :, lanes] = kept * f[c] + NOISE * b_buf[c, n, :, lanes].astype(f32)
-            return carry
-
-        lax.fori_loop(0, 8, block, 0)
+            return inner
+
+        return lax.fori_loop(0, pairs // UNROLL, some, carry)
+
+    lax.fori_loop(0, BLOCKS, block, 0)
     for copy in own:
         copy.wait()
 
@@ -150,7 +154,7 @@
         out_specs=[vmem, vmem, vmem],
         scratch_shapes=[
             pltpu.VMEM(flat, bf16),
-            pltpu.SemaphoreType.DMA((CHUNKS, 12)),
+            pltpu.SemaphoreType.DMA((BLOCKS, 4)),
             pltpu.SemaphoreType.DMA((2,)),
         ],
         compiler_params=pltpu.CompilerParams(vmem_limit_bytes=24 << 20),
@@ -166,7 +170,6 @@
     slabs, near_ref, local_ref, f_ref, base_ref, nf_hbm, own_ref, outer_ref, inner_ref, n_buf, grad, sums, sem
 ):
     pairs = f_ref.shape[1]
-    per = pairs // CHUNKS
     slab = lax.axis_index("mesh")
     mine = lax.axis_index("field")
     masks = lane_masks()
@@ -181,18 +184,14 @@
                 grad[3 * a + c, pl.ds(q, 8, stride=8), :] = value
                 grad[3 * a + c, pl.ds(q + 4, 8, stride=8), :] = value
 
-    for ch in range(CHUNKS):
-
-        def block(j, carry):
-            rows = pl.ds(pl.multiple_of(8 * j, 8), 8)
-            lanes = pl.ds(pl.multiple_of(128 * j, 128), 128)
-            g = [grad[k, rows, :] for k in range(9)]
-            if ch:
-                acc = [sums[k, rows, :] for k in range(6)]
-            else:
-                acc = [jnp.zeros((8, 128), f32) for _ in range(6)]
-            for u in range(per):
-                n = ch * per + u
+    def block(j, carry):
+        rows = pl.ds(pl.multiple_of(8 * j, 8), 8)
+        lanes = lanes_of(j)
+        g = [grad[k, rows, :] for k in range(9)]
+
+        def some(i, acc):
+            for u in range(UNROLL):
+                n = i * UNROLL + u
                 f = [f_ref[c, n, :, lanes].astype(f32) for c in range(3)]
                 a = stretch(f, [base_ref[o, n, :, lanes] for o in range(3)], g)
                 for c in range(3):
@@ -202,14 +201,17 @@
                 p0 = r * a[0]
                 p1 = r * a[1]
                 products = (r * s[0], p0 * a[1], p0 * a[2], r * s[1], p1 * a[2], r * s[2])
-                acc = [x + y for x, y in zip(acc, products)]
-            for k in range(6):
-                sums[k, rows, :] = acc[k]
-            return carry
-
-        lax.fori_loop(0, 8, block, 0)
-        for copy in stores(ch, n_buf, nf_hbm, sem):
+                acc = tuple(x + y for x, y in zip(acc, products))
+            return acc
+
+        acc = lax.fori_loop(0, pairs // UNROLL, some, tuple(jnp.zeros((8, 128), f32) for _ in range(6)))
+        for k in range(6):
+            sums[k, rows, :] = acc[k]
+        for copy in stores(j, n_buf, nf_hbm, sem):
             copy.start()
+        return carry
+
+    lax.fori_loop(0, BLOCKS, block, 0)
 
     scale = VISCOSITY / WEISSENBERG / NF * MAX_STRETCH
     stress = []
@@ -283,9 +285,12 @@
             outer_ref[q, a] = jnp.where(odd, after, before)
             inner_ref[q, a] = jnp.where(odd, before, after)
 
-    for ch in range(CHUNKS):
-        for copy in stores(ch, n_buf, nf_hbm, sem):
+    def end(j, carry):
+        for copy in stores(j, n_buf, nf_hbm, sem):
             copy.wait()
+        return carry
+
+    lax.fori_loop(0, BLOCKS, end, 0)
 
 
 def share(near, local, f_flat, base):
@@ -302,7 +307,7 @@
             pltpu.VMEM((3, n, 8, 1024), bf16),
             pltpu.VMEM((9, 64, 128), f32),
             pltpu.VMEM((6, 64, 128), f32),
-            pltpu.SemaphoreType.DMA((CHUNKS, 6)),
+            pltpu.SemaphoreType.DMA((BLOCKS, 2)),
         ],
         compiler_params=pltpu.CompilerParams(vmem_limit_bytes=16 << 20),
         cost_estimate=pl.CostEstimate(flops=13_000_000, bytes_accessed=7_000_000, transcendentals=0),

time: 39.3 us -> 39 us (level)
  Pallas kernels: 6.07 us -> 5.43 us
where the time goes in v7:
time: 39 us; the launch traced here: 38.8 us
  blocking collectives  18.1 us (46%)
  starting transfers between devices  12 us (31%)
  Pallas kernels  5.43 us (14%)
  waiting for transfers between devices  2 us (5%)
  between operations  0.69 us (2%)
  other arithmetic  0.62 us (2%)
    ppermute x2, starting transfers between devices, exchange(): return lax.ppermute(x, AXES, pairs + [(b, a) for a, b in pairs])  12 us
    all_to_all x1, blocking collectives, body(): parts = lax.all_to_all(kept + (outer + inner), 'field', 0, 0, tiled=True)  6.39 us
    all_gather x1, blocking collectives, body(): both = lax.all_gather(inner, AXES, axis=0, axis_index_groups=couples)  6.34 us
    all_gather x1, blocking collectives, body(): near = lax.all_gather(jnp.stack([own, edge]), 'field', axis=0)  5.32 us
    pallas_call x1, Pallas kernels, share(): pl.pallas_call(functools.partial(share_kernel, slabs), out_shape=(jax.Sha...  2.86 us
    pallas_call x1, Pallas kernels, relax(): pl.pallas_call(relax_kernel, out_shape=(jax.ShapeDtypeStruct(flat, bf16),...  2.58 us
    ppermute x2, waiting for transfers between devices, exchange(): return lax.ppermute(x, AXES, pairs + [(b, a) for a, b in pairs])  2 us
  transfers between devices with their start and end apart: 2, of which 1 were waited for; matrix products, arithmetic and copies ran while one was open for 0% of the time, Pallas kernels for 7%

profile of v7, /device:TPU:256, one launch (start us, length us, event | category | flops | bytes accessed | tf_op | source)
XLA Modules:
  0.0 38.8 jit_solution(15490777166829708989)
XLA Ops:
  0.6 6.1 %collective-permute-start = (f32[3,8,128]{2,1,0:T(8,128)}, f32[3,8,128]{2,1,0:T(8,128)S(1)}, u32[]{:S(2)}, u32[]{:S(2)}) collective-permute-start(f32[3,8,128]{2,1,0:T(8,128)} %bitcast.12), channel_id=1, source_target_pairs={{3,4},{7,8},{11,12},{15,16},{19,20},{23,24},{27,28},{31,32},{35,36... | collective-permute-start | bytes 36872 | tf_op jit(solution)/shard_map/ppermute | solution.py:321
  6.7 0.0 copy-start
  6.7 2.6 %shard_map.59 = (bf16[3,32,8,1024]{3,2,1,0:T(8,128)(2,1)S(1)}, f32[3,32,8,1024]{3,2,1,0:T(8,128)S(1)}, f32[4,8,128]{2,1,0:T(8,128)S(1)}) custom-call(f32[3,8,128]{2,1,0:T(8,128)} %bitcast.13, f32[1,8,128]{2,1,0:T(8,128)} %bitcast.17, bf16[3,32,2,4,1024]{4,3,2,1,0:T(4,128)(2,1)} %bitcast.10, bf16[3,32,2,4,1024]{4,3,2,1,0:T(4,128)(2,1)} %bitcast.11), custom_call_target="tpu_custom_call" | custom-call | flops 10000000 | bytes 8000000 | tf_op jit(solution)/shard_map/pallas_call | solution.py:146
  9.3 2.0 %collective-permute-done = f32[3,8,128]{2,1,0:T(8,128)S(1)} collective-permute-done((f32[3,8,128]{2,1,0:T(8,128)}, f32[3,8,128]{2,1,0:T(8,128)S(1)}, u32[]{:S(2)}, u32[]{:S(2)}) %collective-permute-start) | collective-permute-done | bytes 12320 | tf_op jit(solution)/shard_map/ppermute | solution.py:321
  11.3 0.0 copy-done
  11.3 5.3 %all-gather = f32[8,3,8,128]{3,2,1,0:T(8,128)S(1)} all-gather(f32[2,3,8,128]{3,2,1,0:T(8,128)S(1)} %pad_maximum_fusion), channel_id=2, replica_groups=mesh['mesh'=128,'field'=4] {'field'}, dimensions={0}, use_global_device_ids=true | all-gather | bytes 122880 | tf_op jit(solution)/shard_map/all_gather | solution.py:326
  16.6 2.9 %shard_map.60 = (bf16[3,32,2,4,1024]{4,3,2,1,0:T(4,128)(2,1)}, f32[4,3,8,128]{3,2,1,0:T(8,128)S(1)}, f32[4,3,8,128]{3,2,1,0:T(8,128)S(1)}, f32[4,3,8,128]{3,2,1,0:T(8,128)S(1)}) custom-call(f32[4,2,3,8,128]{4,3,2,1,0:T(8,128)S(1)} %bitcast.9, f32[4,8,128]{2,1,0:T(8,128)S(1)} %get-tuple-element.9.local_ref, ...), custom_call_target="tpu_custom_call" | custom-call | flops 13000000 | bytes 7000000 | tf_op jit(solution)/shard_map/pallas_call | solution.py:301
  19.5 5.9 %collective-permute-start.1 = (f32[4,3,8,128]{3,2,1,0:T(8,128)S(1)}, f32[4,3,8,128]{3,2,1,0:T(8,128)S(1)}, u32[]{:S(2)}, u32[]{:S(2)}) collective-permute-start(f32[4,3,8,128]{3,2,1,0:T(8,128)S(1)} %get-tuple-element.14), channel_id=1, source_target_pairs={{4,8},{5,9},{6,10},{7,11},{12,16},{13,17},{14,18},{15,19},{20,24},... | collective-permute-start | bytes 147464 | tf_op jit(solution)/shard_map/ppermute | solution.py:321
  25.4 6.3 %all-gather.1 = f32[8,3,8,128]{3,2,1,0:T(8,128)S(1)} all-gather(f32[4,3,8,128]{3,2,1,0:T(8,128)S(1)} %get-tuple-element.15), channel_id=3, replica_groups={{0,4},{1,5},{2,6},{3,7},{8,12},{9,13},{10,14},{11,15},{16,20},{17,21},{..., dimensions={0}, use_global_device_ids=true | all-gather | bytes 147456 | tf_op jit(solution)/shard_map/all_gather | solution.py:331
  31.7 0.0 collective-permute-done.1
  31.8 6.4 %all_to_all.5 = f32[4,3,8,128]{3,2,1,0:T(8,128)S(1)} all-to-all(f32[4,3,8,128]{3,2,1,0:T(8,128)S(1)} %fusion.1), channel_id=1, replica_groups=mesh['mesh'=128,'field'=4] {'field'}, dimensions={0} | all-to-all | bytes 98304 | tf_op jit(solution)/shard_map/all_to_all | solution.py:333
  38.2 0.6 %fusion.2 = f32[1,3,8,128]{3,2,1,0:T(8,128)} fusion(f32[4,3,8,128]{3,2,1,0:T(8,128)S(1)} %all_to_all.5), kind=kLoop, calls=%fused_computation.5 | loop fusion | flops 9216 | bytes 61440 | tf_op jit(solution)/shard_map/add | solution.py:334
  (2 shorter events, 0.0 us)
Async XLA Ops:
  0.6 10.7 %collective-permute-start = (f32[3,8,128]{2,1,0:T(8,128)}, f32[3,8,128]{2,1,0:T(8,128)S(1)}, u32[]{:S(2)}, u32[]{:S(2)}) collective-permute-start(f32[3,8,128]{2,1,0:T(8,128)} %bitcast.12), channel_id=1, source_target_pairs={{3,4},{7,8},{11,12},{15,16},{19,20},{23,24},{27,28},{31,32},{35,36... | collective-permute-start | bytes 36872 | tf_op jit(solution)/shard_map/ppermute | solution.py:321
  6.7 4.5 %copy-start = (f32[3,1,1024]{2,1,0:T(1,128)S(1)}, f32[3,1,1024]{2,1,0:T(1,128)}, u32[]{:S(2)}) copy-start(f32[3,1,1024]{2,1,0:T(1,128)} %param.4) | copy-start | bytes 36868
  19.5 12.3 %collective-permute-start.1 = (f32[4,3,8,128]{3,2,1,0:T(8,128)S(1)}, f32[4,3,8,128]{3,2,1,0:T(8,128)S(1)}, u32[]{:S(2)}, u32[]{:S(2)}) collective-permute-start(f32[4,3,8,128]{3,2,1,0:T(8,128)S(1)} %get-tuple-element.14), channel_id=1, source_target_pairs={{4,8},{5,9},{6,10},{7,11},{12,16},{13,17},{14,18},{15,19},{20,24},... | collective-permute-start | bytes 147464 | tf_op jit(solution)/shard_map/ppermute | solution.py:321

commit v8 on v7

--- a/solution.py
+++ b/solution.py
@@ -94,11 +94,11 @@
     ]
 
 
-def relax_kernel(velocity_hbm, pressure_hbm, f_hbm, b_hbm, f_ref, base_ref, local_ref, b_buf, sem, local_sem):
+def relax_kernel(velocity_hbm, pressure_hbm, f_hbm, b_hbm, f_ref, base_ref, local_ref, f_buf, b_buf, sem, local_sem):
     pairs = b_buf.shape[1]
 
     def begin(j, carry):
-        for copy in loads(j, (f_hbm, b_hbm), (f_ref, b_buf), sem):
+        for copy in loads(j, (f_hbm, b_hbm), (f_buf, b_buf), sem):
             copy.start()
         return carry
 
@@ -112,17 +112,18 @@
 
     def block(j, carry):
         lanes = lanes_of(j)
-        for copy in loads(j, (f_hbm, b_hbm), (f_ref, b_buf), sem):
+        for copy in loads(j, (f_hbm, b_hbm), (f_buf, b_buf), sem):
             copy.wait()
 
         def some(i, inner):
             for u in range(UNROLL):
                 n = i * UNROLL + u
-                f = [f_ref[c, n, :, lanes].astype(f32) for c in range(3)]
+                f = [f_buf[c, n, :, lanes].astype(f32) for c in range(3)]
                 length_sq = f[0] * f[0] + f[1] * f[1] + f[2] * f[2]
                 pull = TIME_STEP * MAX_STRETCH / (2.0 * WEISSENBERG) * pltpu.reciprocal(MAX_STRETCH - length_sq)
                 kept = 1.0 - pull
                 for c in range(3):
+                    f_ref[c, n, :, lanes] = f[c]
                     base_ref[c, n, :, lanes] = kept * f[c] + NOISE * b_buf[c, n, :, lanes].astype(f32)
             return inner
 
@@ -146,13 +147,14 @@
     return pl.pallas_call(
         relax_kernel,
         out_shape=(
-            jax.ShapeDtypeStruct(flat, bf16),
+            jax.ShapeDtypeStruct(flat, f32),
             jax.ShapeDtypeStruct(flat, f32),
             jax.ShapeDtypeStruct((4, 8, 128), f32),
         ),
         in_specs=[hbm] * 4,
         out_specs=[vmem, vmem, vmem],
         scratch_shapes=[
+            pltpu.VMEM(flat, bf16),
             pltpu.VMEM(flat, bf16),
             pltpu.SemaphoreType.DMA((BLOCKS, 4)),
             pltpu.SemaphoreType.DMA((2,)),
@@ -192,7 +194,7 @@
         def some(i, acc):
             for u in range(UNROLL):
                 n = i * UNROLL + u
-                f = [f_ref[c, n, :, lanes].astype(f32) for c in range(3)]
+                f = [f_ref[c, n, :, lanes] for c in range(3)]
                 a = stretch(f, [base_ref[o, n, :, lanes] for o in range(3)], g)
                 for c in range(3):
                     n_buf[c, n, :, lanes] = a[c].astype(bf16)
@@ -252,6 +254,7 @@
         value = jnp.where(masks["channel"] | wide, 1.0 / DIAGONAL, 0.0)
         fluid.append(jnp.where(inside, value, 0.0))
 
+    sources, currents = [], [{q: start[a][q] for q in range(PLANES)} for a in range(3)]
     for a in range(3):
         source = {}
         for q in range(-1, PLANES + 1):
@@ -266,22 +269,25 @@
                     inner = inner - slope_z(pressure[q], masks)
                 total = total + inner + start[a][q] * (1.0 / TIME_STEP)
             source[q] = total
-        current = {q: start[a][q] for q in range(PLANES)}
-        for sweep in range(SWEEPS):
+        sources.append(source)
+    for sweep in range(SWEEPS):
+        for a in range(3):
+            current = currents[a]
             later = {}
             for q in range(-1 - sweep, PLANES + 1 + sweep):
-                total = source.get(q)
+                total = sources[a].get(q)
                 along = add(current.get(q - 1), current.get(q + 1))
                 if along is not None:
                     total = add(total, AXIAL * along)
                 if q in current:
                     total = add(total, TRANSVERSE * around(current[q], masks))
                 later[q] = total * fluid[q - first]
-            current = later
-        odd = slab % 2 == 1
+            currents[a] = later
+    odd = slab % 2 == 1
+    for a in range(3):
         for q in range(PLANES):
-            before, after = current[q - PLANES], current[q + PLANES]
-            own_ref[q, a] = current[q]
+            before, after = currents[a][q - PLANES], currents[a][q + PLANES]
+            own_ref[q, a] = currents[a][q]
             outer_ref[q, a] = jnp.where(odd, after, before)
             inner_ref[q, a] = jnp.where(odd, before, after)
 

time: 39 us -> 38.7 us (level)
  no operation moved by 1% of the time
where the time goes in v8:
time: 38.7 us; the launch traced here: 38.5 us
  blocking collectives  18.1 us (47%)
  starting transfers between devices  12 us (31%)
  Pallas kernels  5.18 us (13%)
  waiting for transfers between devices  1.97 us (5%)
  between operations  0.69 us (2%)
  other arithmetic  0.62 us (2%)
    ppermute x2, starting transfers between devices, exchange(): return lax.ppermute(x, AXES, pairs + [(b, a) for a, b in pairs])  12 us
    all_to_all x1, blocking collectives, body(): parts = lax.all_to_all(kept + (outer + inner), 'field', 0, 0, tiled=True)  6.39 us
    all_gather x1, blocking collectives, body(): both = lax.all_gather(inner, AXES, axis=0, axis_index_groups=couples)  6.34 us
    all_gather x1, blocking collectives, body(): near = lax.all_gather(jnp.stack([own, edge]), 'field', axis=0)  5.32 us
    pallas_call x1, Pallas kernels, relax(): pl.pallas_call(relax_kernel, out_shape=(jax.ShapeDtypeStruct(flat, f32),...  2.61 us
    pallas_call x1, Pallas kernels, share(): pl.pallas_call(functools.partial(share_kernel, slabs), out_shape=(jax.Sha...  2.58 us
    ppermute x2, waiting for transfers between devices, exchange(): return lax.ppermute(x, AXES, pairs + [(b, a) for a, b in pairs])  1.97 us
  transfers between devices with their start and end apart: 2, of which 1 were waited for; matrix products, arithmetic and copies ran while one was open for 0% of the time, Pallas kernels for 7%

profile of v8, /device:TPU:256, one launch (start us, length us, event | category | flops | bytes accessed | tf_op | source)
XLA Modules:
  0.0 38.5 jit_solution(17451149545542090664)
XLA Ops:
  0.6 6.1 %collective-permute-start = (f32[3,8,128]{2,1,0:T(8,128)}, f32[3,8,128]{2,1,0:T(8,128)S(1)}, u32[]{:S(2)}, u32[]{:S(2)}) collective-permute-start(f32[3,8,128]{2,1,0:T(8,128)} %bitcast.12), channel_id=1, source_target_pairs={{3,4},{7,8},{11,12},{15,16},{19,20},{23,24},{27,28},{31,32},{35,36... | collective-permute-start | bytes 36872 | tf_op jit(solution)/shard_map/ppermute | solution.py:327
  6.7 0.0 copy-start
  6.7 2.6 %shard_map.59 = (f32[3,32,8,1024]{3,2,1,0:T(8,128)S(1)}, f32[3,32,8,1024]{3,2,1,0:T(8,128)S(1)}, f32[4,8,128]{2,1,0:T(8,128)S(1)}) custom-call(f32[3,8,128]{2,1,0:T(8,128)} %bitcast.13, f32[1,8,128]{2,1,0:T(8,128)} %bitcast.17, bf16[3,32,2,4,1024]{4,3,2,1,0:T(4,128)(2,1)} %bitcast.10, bf16[3,32,2,4,1024]{4,3,2,1,0:T(4,128)(2,1)} %bitcast.11), custom_call_target="tpu_custom_call" | custom-call | flops 10000000 | bytes 8000000 | tf_op jit(solution)/shard_map/pallas_call | solution.py:147
  9.4 1.9 %collective-permute-done = f32[3,8,128]{2,1,0:T(8,128)S(1)} collective-permute-done((f32[3,8,128]{2,1,0:T(8,128)}, f32[3,8,128]{2,1,0:T(8,128)S(1)}, u32[]{:S(2)}, u32[]{:S(2)}) %collective-permute-start) | collective-permute-done | bytes 12320 | tf_op jit(solution)/shard_map/ppermute | solution.py:327
  11.3 0.0 copy-done
  11.3 5.3 %all-gather = f32[8,3,8,128]{3,2,1,0:T(8,128)S(1)} all-gather(f32[2,3,8,128]{3,2,1,0:T(8,128)S(1)} %pad_maximum_fusion), channel_id=2, replica_groups=mesh['mesh'=128,'field'=4] {'field'}, dimensions={0}, use_global_device_ids=true | all-gather | bytes 122880 | tf_op jit(solution)/shard_map/all_gather | solution.py:332
  16.6 2.6 %shard_map.60 = (bf16[3,32,2,4,1024]{4,3,2,1,0:T(4,128)(2,1)}, f32[4,3,8,128]{3,2,1,0:T(8,128)S(1)}, f32[4,3,8,128]{3,2,1,0:T(8,128)S(1)}, f32[4,3,8,128]{3,2,1,0:T(8,128)S(1)}) custom-call(f32[4,2,3,8,128]{4,3,2,1,0:T(8,128)S(1)} %bitcast.9, f32[4,8,128]{2,1,0:T(8,128)S(1)} %get-tuple-element.9.local_ref, f32[3,32,8,1024]{3,2,1,0:T(8,128)S(1)} %get-tuple-element.10.f_ref, ...), custom_call_target="tpu_custom_call" | custom-call | flops 13000000 | bytes 7000000 | tf_op jit(solution)/shard_map/pallas_call | solution.py:307
  19.2 5.9 %collective-permute-start.1 = (f32[4,3,8,128]{3,2,1,0:T(8,128)S(1)}, f32[4,3,8,128]{3,2,1,0:T(8,128)S(1)}, u32[]{:S(2)}, u32[]{:S(2)}) collective-permute-start(f32[4,3,8,128]{3,2,1,0:T(8,128)S(1)} %get-tuple-element.14), channel_id=1, source_target_pairs={{4,8},{5,9},{6,10},{7,11},{12,16},{13,17},{14,18},{15,19},{20,24},... | collective-permute-start | bytes 147464 | tf_op jit(solution)/shard_map/ppermute | solution.py:327
  25.1 6.3 %all-gather.1 = f32[8,3,8,128]{3,2,1,0:T(8,128)S(1)} all-gather(f32[4,3,8,128]{3,2,1,0:T(8,128)S(1)} %get-tuple-element.15), channel_id=3, replica_groups={{0,4},{1,5},{2,6},{3,7},{8,12},{9,13},{10,14},{11,15},{16,20},{17,21},{..., dimensions={0}, use_global_device_ids=true | all-gather | bytes 147456 | tf_op jit(solution)/shard_map/all_gather | solution.py:337
  31.5 0.0 collective-permute-done.1
  31.5 6.4 %all_to_all.5 = f32[4,3,8,128]{3,2,1,0:T(8,128)S(1)} all-to-all(f32[4,3,8,128]{3,2,1,0:T(8,128)S(1)} %fusion.1), channel_id=1, replica_groups=mesh['mesh'=128,'field'=4] {'field'}, dimensions={0} | all-to-all | bytes 98304 | tf_op jit(solution)/shard_map/all_to_all | solution.py:339
  37.9 0.6 %fusion.2 = f32[1,3,8,128]{3,2,1,0:T(8,128)} fusion(f32[4,3,8,128]{3,2,1,0:T(8,128)S(1)} %all_to_all.5), kind=kLoop, calls=%fused_computation.5 | loop fusion | flops 9216 | bytes 61440 | tf_op jit(solution)/shard_map/add | solution.py:340
  (2 shorter events, 0.0 us)
Async XLA Ops:
  0.6 10.7 %collective-permute-start = (f32[3,8,128]{2,1,0:T(8,128)}, f32[3,8,128]{2,1,0:T(8,128)S(1)}, u32[]{:S(2)}, u32[]{:S(2)}) collective-permute-start(f32[3,8,128]{2,1,0:T(8,128)} %bitcast.12), channel_id=1, source_target_pairs={{3,4},{7,8},{11,12},{15,16},{19,20},{23,24},{27,28},{31,32},{35,36... | collective-permute-start | bytes 36872 | tf_op jit(solution)/shard_map/ppermute | solution.py:327
  6.7 4.5 %copy-start = (f32[3,1,1024]{2,1,0:T(1,128)S(1)}, f32[3,1,1024]{2,1,0:T(1,128)}, u32[]{:S(2)}) copy-start(f32[3,1,1024]{2,1,0:T(1,128)} %param.4) | copy-start | bytes 36868
  19.2 12.3 %collective-permute-start.1 = (f32[4,3,8,128]{3,2,1,0:T(8,128)S(1)}, f32[4,3,8,128]{3,2,1,0:T(8,128)S(1)}, u32[]{:S(2)}, u32[]{:S(2)}) collective-permute-start(f32[4,3,8,128]{3,2,1,0:T(8,128)S(1)} %get-tuple-element.14), channel_id=1, source_target_pairs={{4,8},{5,9},{6,10},{7,11},{12,16},{13,17},{14,18},{15,19},{20,24},... | collective-permute-start | bytes 147464 | tf_op jit(solution)/shard_map/ppermute | solution.py:327

commit v9 on v8

--- a/solution.py
+++ b/solution.py
@@ -336,7 +336,8 @@
     couples = [[i, i + PLANES] for i in range(total) if i // PLANES % 2 == 0]
     both = lax.all_gather(inner, AXES, axis=0, axis_index_groups=couples)
     inner = jnp.where(lax.axis_index("mesh") % 2 == 1, both[0], both[1])
-    parts = lax.all_to_all(kept + (outer + inner), "field", 0, 0, tiled=True)
+    parts = lax.all_gather(kept + (outer + inner), "field", axis=0)
+    parts = lax.dynamic_index_in_dim(parts, lax.axis_index("field"), 1, keepdims=False)
     result = (parts[0] + parts[1]) + (parts[2] + parts[3])
     return new_fields.reshape(fields.shape), result.reshape(velocity.shape)
 

time: 38.7 us -> 38.4 us (level); the launches traced: 38.5 us -> 37.7 us
  blocking collectives: 18.1 us -> 17.3 us
    all_to_all x1 -> x0, blocking collectives: 6.39 us -> none  [body(): parts = lax.all_to_all(kept + (outer + inner), 'field', 0, 0, tiled=True)]
    all_gather x0 -> x1, blocking collectives: none -> 5.61 us  [body(): parts = lax.all_gather(kept + (outer + inner), 'field', axis=0)]
where the time goes in v9:
time: 38.4 us; the launch traced here: 37.7 us
  blocking collectives  17.3 us (45%)
  starting transfers between devices  12 us (31%)
  Pallas kernels  5.18 us (13%)
  waiting for transfers between devices  1.97 us (5%)
  between operations  0.69 us (2%)
  other arithmetic  0.62 us (2%)
    ppermute x2, starting transfers between devices, exchange(): return lax.ppermute(x, AXES, pairs + [(b, a) for a, b in pairs])  12 us
    all_gather x1, blocking collectives, body(): both = lax.all_gather(inner, AXES, axis=0, axis_index_groups=couples)  6.34 us
    all_gather x1, blocking collectives, body(): parts = lax.all_gather(kept + (outer + inner), 'field', axis=0)  5.61 us
    all_gather x1, blocking collectives, body(): near = lax.all_gather(jnp.stack([own, edge]), 'field', axis=0)  5.32 us
    pallas_call x1, Pallas kernels, relax(): pl.pallas_call(relax_kernel, out_shape=(jax.ShapeDtypeStruct(flat, f32),...  2.61 us
    pallas_call x1, Pallas kernels, share(): pl.pallas_call(functools.partial(share_kernel, slabs), out_shape=(jax.Sha...  2.58 us
    ppermute x2, waiting for transfers between devices, exchange(): return lax.ppermute(x, AXES, pairs + [(b, a) for a, b in pairs])  1.97 us
  transfers between devices with their start and end apart: 2, of which 1 were waited for; matrix products, arithmetic and copies ran while one was open for 0% of the time, Pallas kernels for 7%

profile of v9, /device:TPU:256, one launch (start us, length us, event | category | flops | bytes accessed | tf_op | source)
XLA Modules:
  0.0 37.7 jit_solution(7549225947064396838)
XLA Ops:
  0.6 6.1 %collective-permute-start = (f32[3,8,128]{2,1,0:T(8,128)}, f32[3,8,128]{2,1,0:T(8,128)S(1)}, u32[]{:S(2)}, u32[]{:S(2)}) collective-permute-start(f32[3,8,128]{2,1,0:T(8,128)} %bitcast.14), channel_id=1, source_target_pairs={{3,4},{7,8},{11,12},{15,16},{19,20},{23,24},{27,28},{31,32},{35,36... | collective-permute-start | bytes 36872 | tf_op jit(solution)/shard_map/ppermute | solution.py:327
  6.7 0.0 copy-start
  6.7 2.6 %shard_map.59 = (f32[3,32,8,1024]{3,2,1,0:T(8,128)S(1)}, f32[3,32,8,1024]{3,2,1,0:T(8,128)S(1)}, f32[4,8,128]{2,1,0:T(8,128)S(1)}) custom-call(f32[3,8,128]{2,1,0:T(8,128)} %bitcast.15, f32[1,8,128]{2,1,0:T(8,128)} %bitcast.19, bf16[3,32,2,4,1024]{4,3,2,1,0:T(4,128)(2,1)} %bitcast.11, bf16[3,32,2,4,1024]{4,3,2,1,0:T(4,128)(2,1)} %bitcast.12), custom_call_target="tpu_custom_call" | custom-call | flops 10000000 | bytes 8000000 | tf_op jit(solution)/shard_map/pallas_call | solution.py:147
  9.4 1.9 %collective-permute-done = f32[3,8,128]{2,1,0:T(8,128)S(1)} collective-permute-done((f32[3,8,128]{2,1,0:T(8,128)}, f32[3,8,128]{2,1,0:T(8,128)S(1)}, u32[]{:S(2)}, u32[]{:S(2)}) %collective-permute-start) | collective-permute-done | bytes 12320 | tf_op jit(solution)/shard_map/ppermute | solution.py:327
  11.3 0.0 copy-done
  11.3 5.3 %all-gather = f32[8,3,8,128]{3,2,1,0:T(8,128)S(1)} all-gather(f32[2,3,8,128]{3,2,1,0:T(8,128)S(1)} %pad_maximum_fusion), channel_id=2, replica_groups=mesh['mesh'=128,'field'=4] {'field'}, dimensions={0}, use_global_device_ids=true | all-gather | bytes 122880 | tf_op jit(solution)/shard_map/all_gather | solution.py:332
  16.6 2.6 %shard_map.60 = (bf16[3,32,2,4,1024]{4,3,2,1,0:T(4,128)(2,1)}, f32[4,3,8,128]{3,2,1,0:T(8,128)S(1)}, f32[4,3,8,128]{3,2,1,0:T(8,128)S(1)}, f32[4,3,8,128]{3,2,1,0:T(8,128)S(1)}) custom-call(f32[4,2,3,8,128]{4,3,2,1,0:T(8,128)S(1)} %bitcast.10, f32[4,8,128]{2,1,0:T(8,128)S(1)} %get-tuple-element.9.local_ref, f32[3,32,8,1024]{3,2,1,0:T(8,128)S(1)} %get-tuple-element.10.f_ref, ...), custom_call_target="tpu_custom_call" | custom-call | flops 13000000 | bytes 7000000 | tf_op jit(solution)/shard_map/pallas_call | solution.py:307
  19.2 5.9 %collective-permute-start.1 = (f32[4,3,8,128]{3,2,1,0:T(8,128)S(1)}, f32[4,3,8,128]{3,2,1,0:T(8,128)S(1)}, u32[]{:S(2)}, u32[]{:S(2)}) collective-permute-start(f32[4,3,8,128]{3,2,1,0:T(8,128)S(1)} %get-tuple-element.14), channel_id=1, source_target_pairs={{4,8},{5,9},{6,10},{7,11},{12,16},{13,17},{14,18},{15,19},{20,24},... | collective-permute-start | bytes 147464 | tf_op jit(solution)/shard_map/ppermute | solution.py:327
  25.1 6.3 %all-gather.1 = f32[8,3,8,128]{3,2,1,0:T(8,128)S(1)} all-gather(f32[4,3,8,128]{3,2,1,0:T(8,128)S(1)} %get-tuple-element.15), channel_id=3, replica_groups={{0,4},{1,5},{2,6},{3,7},{8,12},{9,13},{10,14},{11,15},{16,20},{17,21},{..., dimensions={0}, use_global_device_ids=true | all-gather | bytes 147456 | tf_op jit(solution)/shard_map/all_gather | solution.py:337
  31.5 0.0 collective-permute-done.1
  31.5 5.6 %all-gather.2 = f32[16,3,8,128]{3,2,1,0:T(8,128)S(1)} all-gather(f32[4,3,8,128]{3,2,1,0:T(8,128)S(1)} %fusion.1), channel_id=4, replica_groups=mesh['mesh'=128,'field'=4] {'field'}, dimensions={0}, use_global_device_ids=true | all-gather | bytes 245760 | tf_op jit(solution)/shard_map/all_gather | solution.py:339
  37.1 0.6 %fusion.2 = f32[1,1,3,8,128]{4,3,2,1,0:T(8,128)} fusion(f32[4,4,3,8,128]{4,3,2,1,0:T(8,128)S(1)} %bitcast.13, s32[]{:T(128)S(6)} %add.59, s32[]{:T(128)S(6)} %select_n.26, s32[]{:T(128)S(6)} %add.58, s32[]{:T(128)S(6)} %add.57), kind=kLoop, calls=%fused_computation.5 | loop fusion | flops 9216 | bytes 61456 | tf_op jit(solution)/shard_map/add | solution.py:341
  (2 shorter events, 0.0 us)
Async XLA Ops:
  0.6 10.7 %collective-permute-start = (f32[3,8,128]{2,1,0:T(8,128)}, f32[3,8,128]{2,1,0:T(8,128)S(1)}, u32[]{:S(2)}, u32[]{:S(2)}) collective-permute-start(f32[3,8,128]{2,1,0:T(8,128)} %bitcast.14), channel_id=1, source_target_pairs={{3,4},{7,8},{11,12},{15,16},{19,20},{23,24},{27,28},{31,32},{35,36... | collective-permute-start | bytes 36872 | tf_op jit(solution)/shard_map/ppermute | solution.py:327
  6.7 4.5 %copy-start = (f32[3,1,1024]{2,1,0:T(1,128)S(1)}, f32[3,1,1024]{2,1,0:T(1,128)}, u32[]{:S(2)}) copy-start(f32[3,1,1024]{2,1,0:T(1,128)} %param.4) | copy-start | bytes 36868
  19.2 12.3 %collective-permute-start.1 = (f32[4,3,8,128]{3,2,1,0:T(8,128)S(1)}, f32[4,3,8,128]{3,2,1,0:T(8,128)S(1)}, u32[]{:S(2)}, u32[]{:S(2)}) collective-permute-start(f32[4,3,8,128]{3,2,1,0:T(8,128)S(1)} %get-tuple-element.14), channel_id=1, source_target_pairs={{4,8},{5,9},{6,10},{7,11},{12,16},{13,17},{14,18},{15,19},{20,24},... | collective-permute-start | bytes 147464 | tf_op jit(solution)/shard_map/ppermute | solution.py:327

commit v10 on v9

--- a/solution.py
+++ b/solution.py
@@ -176,7 +176,7 @@
     mine = lax.axis_index("field")
     masks = lane_masks()
 
-    planes = [(0, 1), (0, 0), (1, 0), (2, 0), (3, 0), (3, 1)]
+    planes = [(1, 1), (0, 0), (1, 0), (2, 0), (3, 0), (3, 1)]
     for q in range(PLANES):
         for a in range(3):
             before, centre, after = (near_ref[d, e, a] for d, e in planes[q : q + 3])
@@ -327,7 +327,8 @@
         return lax.ppermute(x, AXES, pairs + [(b, a) for a, b in pairs])
 
     own = velocity.reshape(3, 8, 128)
-    edge = exchange(own, [(i, i + 1) for i in range(PLANES - 1, total - 1, PLANES)])
+    ends = range(PLANES - 1, total - 1, PLANES)
+    edge = lax.ppermute(own, AXES, [(i, i + 2) for i in ends] + [(i + 1, i) for i in ends])
     f_flat, base, local = relax(own, pressure.reshape(1, 8, 128), fields, brownian)
     near = lax.all_gather(jnp.stack([own, edge]), "field", axis=0)
     new_fields, kept, outer, inner = share(near, local, f_flat, base)

time: 38.4 us -> 38.4 us (level)
  waiting for transfers between devices: 1.97 us -> 0.01 us
  starting transfers between devices: 12 us -> 13.8 us
    ppermute x0 -> x1, starting transfers between devices: none -> 6.1 us  [body(): lax.ppermute(own, AXES, [(i, i + 2) for i in ends] + [(i + 1, i) for i in...]
    ppermute x2 -> x1, starting transfers between devices: 12 us -> 7.7 us  [exchange(): return lax.ppermute(x, AXES, pairs + [(b, a) for a, b in pairs])]
    ppermute x2 -> x1, waiting for transfers between devices: 1.97 us -> 0.01 us  [exchange(): return lax.ppermute(x, AXES, pairs + [(b, a) for a, b in pairs])]
  transfers between devices with their start and end apart: 2 -> 2, of which waited for: 1 -> 0; matrix products, arithmetic and copies ran while one was open for 0% -> 0% of each run, Pallas kernels for 7% -> 7%
where the time goes in v10:
time: 38.4 us; the launch traced here: 37.7 us
  blocking collectives  17.4 us (45%)
  starting transfers between devices  13.8 us (36%)
  Pallas kernels  5.18 us (13%)
  between operations  0.71 us (2%)
  other arithmetic  0.62 us (2%)
    ppermute x1, starting transfers between devices, exchange(): return lax.ppermute(x, AXES, pairs + [(b, a) for a, b in pairs])  7.7 us
    all_gather x1, blocking collectives, body(): both = lax.all_gather(inner, AXES, axis=0, axis_index_groups=couples)  6.34 us
    ppermute x1, starting transfers between devices, body(): lax.ppermute(own, AXES, [(i, i + 2) for i in ends] + [(i + 1, i) for i in...  6.1 us
    all_gather x1, blocking collectives, body(): parts = lax.all_gather(kept + (outer + inner), 'field', axis=0)  5.61 us
    all_gather x1, blocking collectives, body(): near = lax.all_gather(jnp.stack([own, edge]), 'field', axis=0)  5.42 us
    pallas_call x1, Pallas kernels, relax(): pl.pallas_call(relax_kernel, out_shape=(jax.ShapeDtypeStruct(flat, f32),...  2.61 us
    pallas_call x1, Pallas kernels, share(): pl.pallas_call(functools.partial(share_kernel, slabs), out_shape=(jax.Sha...  2.58 us
  transfers between devices with their start and end apart: 2, of which 0 were waited for; matrix products, arithmetic and copies ran while one was open for 0% of the time, Pallas kernels for 7%

profile of v10, /device:TPU:256, one launch (start us, length us, event | category | flops | bytes accessed | tf_op | source)
XLA Modules:
  0.0 37.7 jit_solution(6812653902504867883)
XLA Ops:
  0.6 6.1 %collective-permute-start = (f32[3,8,128]{2,1,0:T(8,128)}, f32[3,8,128]{2,1,0:T(8,128)S(1)}, u32[]{:S(2)}, u32[]{:S(2)}) collective-permute-start(f32[3,8,128]{2,1,0:T(8,128)} %bitcast.14), channel_id=1, source_target_pairs={{3,5},{7,9},{11,13},{15,17},{19,21},{23,25},{27,29},{31,33},{35,37... | collective-permute-start | bytes 36872 | tf_op jit(solution)/shard_map/ppermute | solution.py:331
  6.7 0.0 copy-start
  6.7 2.6 %shard_map.59 = (f32[3,32,8,1024]{3,2,1,0:T(8,128)S(1)}, f32[3,32,8,1024]{3,2,1,0:T(8,128)S(1)}, f32[4,8,128]{2,1,0:T(8,128)S(1)}) custom-call(f32[3,8,128]{2,1,0:T(8,128)} %bitcast.15, f32[1,8,128]{2,1,0:T(8,128)} %bitcast.19, bf16[3,32,2,4,1024]{4,3,2,1,0:T(4,128)(2,1)} %bitcast.11, bf16[3,32,2,4,1024]{4,3,2,1,0:T(4,128)(2,1)} %bitcast.12), custom_call_target="tpu_custom_call" | custom-call | flops 10000000 | bytes 8000000 | tf_op jit(solution)/shard_map/pallas_call | solution.py:147
  9.4 0.0 collective-permute-done
  9.4 0.0 copy-done
  9.4 5.4 %all-gather = f32[8,3,8,128]{3,2,1,0:T(8,128)S(1)} all-gather(f32[2,3,8,128]{3,2,1,0:T(8,128)S(1)} %pad_maximum_fusion), channel_id=2, replica_groups=mesh['mesh'=128,'field'=4] {'field'}, dimensions={0}, use_global_device_ids=true | all-gather | bytes 122880 | tf_op jit(solution)/shard_map/all_gather | solution.py:333
  14.8 2.6 %shard_map.60 = (bf16[3,32,2,4,1024]{4,3,2,1,0:T(4,128)(2,1)}, f32[4,3,8,128]{3,2,1,0:T(8,128)S(1)}, f32[4,3,8,128]{3,2,1,0:T(8,128)S(1)}, f32[4,3,8,128]{3,2,1,0:T(8,128)S(1)}) custom-call(f32[4,2,3,8,128]{4,3,2,1,0:T(8,128)S(1)} %bitcast.10, f32[4,8,128]{2,1,0:T(8,128)S(1)} %get-tuple-element.9.local_ref, f32[3,32,8,1024]{3,2,1,0:T(8,128)S(1)} %get-tuple-element.10.f_ref, ...), custom_call_target="tpu_custom_call" | custom-call | flops 13000000 | bytes 7000000 | tf_op jit(solution)/shard_map/pallas_call | solution.py:307
  17.4 7.7 %collective-permute-start.1 = (f32[4,3,8,128]{3,2,1,0:T(8,128)S(1)}, f32[4,3,8,128]{3,2,1,0:T(8,128)S(1)}, u32[]{:S(2)}, u32[]{:S(2)}) collective-permute-start(f32[4,3,8,128]{3,2,1,0:T(8,128)S(1)} %get-tuple-element.14), channel_id=1, source_target_pairs={{4,8},{5,9},{6,10},{7,11},{12,16},{13,17},{14,18},{15,19},{20,24},... | collective-permute-start | bytes 147464 | tf_op jit(solution)/shard_map/ppermute | solution.py:327
  25.1 6.3 %all-gather.1 = f32[8,3,8,128]{3,2,1,0:T(8,128)S(1)} all-gather(f32[4,3,8,128]{3,2,1,0:T(8,128)S(1)} %get-tuple-element.15), channel_id=3, replica_groups={{0,4},{1,5},{2,6},{3,7},{8,12},{9,13},{10,14},{11,15},{16,20},{17,21},{..., dimensions={0}, use_global_device_ids=true | all-gather | bytes 147456 | tf_op jit(solution)/shard_map/all_gather | solution.py:338
  31.5 0.0 collective-permute-done.1
  31.5 5.6 %all-gather.2 = f32[16,3,8,128]{3,2,1,0:T(8,128)S(1)} all-gather(f32[4,3,8,128]{3,2,1,0:T(8,128)S(1)} %fusion.1), channel_id=4, replica_groups=mesh['mesh'=128,'field'=4] {'field'}, dimensions={0}, use_global_device_ids=true | all-gather | bytes 245760 | tf_op jit(solution)/shard_map/all_gather | solution.py:340
  37.1 0.6 %fusion.2 = f32[1,1,3,8,128]{4,3,2,1,0:T(8,128)} fusion(f32[4,4,3,8,128]{4,3,2,1,0:T(8,128)S(1)} %bitcast.13, s32[]{:T(128)S(6)} %add.59, s32[]{:T(128)S(6)} %select_n.26, s32[]{:T(128)S(6)} %add.58, s32[]{:T(128)S(6)} %add.57), kind=kLoop, calls=%fused_computation.5 | loop fusion | flops 9216 | bytes 61456 | tf_op jit(solution)/shard_map/add | solution.py:342
  (2 shorter events, 0.0 us)
Async XLA Ops:
  0.6 8.7 %collective-permute-start = (f32[3,8,128]{2,1,0:T(8,128)}, f32[3,8,128]{2,1,0:T(8,128)S(1)}, u32[]{:S(2)}, u32[]{:S(2)}) collective-permute-start(f32[3,8,128]{2,1,0:T(8,128)} %bitcast.14), channel_id=1, source_target_pairs={{3,5},{7,9},{11,13},{15,17},{19,21},{23,25},{27,29},{31,33},{35,37... | collective-permute-start | bytes 36872 | tf_op jit(solution)/shard_map/ppermute | solution.py:331
  6.7 2.6 %copy-start = (f32[3,1,1024]{2,1,0:T(1,128)S(1)}, f32[3,1,1024]{2,1,0:T(1,128)}, u32[]{:S(2)}) copy-start(f32[3,1,1024]{2,1,0:T(1,128)} %param.4) | copy-start | bytes 36868
  17.4 14.1 %collective-permute-start.1 = (f32[4,3,8,128]{3,2,1,0:T(8,128)S(1)}, f32[4,3,8,128]{3,2,1,0:T(8,128)S(1)}, u32[]{:S(2)}, u32[]{:S(2)}) collective-permute-start(f32[4,3,8,128]{3,2,1,0:T(8,128)S(1)} %get-tuple-element.14), channel_id=1, source_target_pairs={{4,8},{5,9},{6,10},{7,11},{12,16},{13,17},{14,18},{15,19},{20,24},... | collective-permute-start | bytes 147464 | tf_op jit(solution)/shard_map/ppermute | solution.py:327

commit v11 on v10

--- a/solution.py
+++ b/solution.py
@@ -333,7 +333,7 @@
     near = lax.all_gather(jnp.stack([own, edge]), "field", axis=0)
     new_fields, kept, outer, inner = share(near, local, f_flat, base)
 
-    outer = exchange(outer, [(i, i + PLANES) for i in range(total - PLANES) if i // PLANES % 2 == 1])
+    outer = exchange(outer, [(i, (i + PLANES) ^ 1) for i in range(total - PLANES) if i // PLANES % 2 == 1])
     couples = [[i, i + PLANES] for i in range(total) if i // PLANES % 2 == 0]
     both = lax.all_gather(inner, AXES, axis=0, axis_index_groups=couples)
     inner = jnp.where(lax.axis_index("mesh") % 2 == 1, both[0], both[1])

time: 38.4 us -> 38.5 us (level)
  no operation moved by 1% of the time
where the time goes in v11:
time: 38.5 us; the launch traced here: 37.7 us
  blocking collectives  17.5 us (45%)
  starting transfers between devices  13.7 us (36%)
  Pallas kernels  5.18 us (13%)
  between operations  0.71 us (2%)
  other arithmetic  0.62 us (2%)
    ppermute x1, starting transfers between devices, exchange(): return lax.ppermute(x, AXES, pairs + [(b, a) for a, b in pairs])  7.65 us
    all_gather x1, blocking collectives, body(): both = lax.all_gather(inner, AXES, axis=0, axis_index_groups=couples)  6.44 us
    ppermute x1, starting transfers between devices, body(): lax.ppermute(own, AXES, [(i, i + 2) for i in ends] + [(i + 1, i) for i in...  6.1 us
    all_gather x1, blocking collectives, body(): parts = lax.all_gather(kept + (outer + inner), 'field', axis=0)  5.61 us
    all_gather x1, blocking collectives, body(): near = lax.all_gather(jnp.stack([own, edge]), 'field', axis=0)  5.42 us
    pallas_call x1, Pallas kernels, relax(): pl.pallas_call(relax_kernel, out_shape=(jax.ShapeDtypeStruct(flat, f32),...  2.61 us
    pallas_call x1, Pallas kernels, share(): pl.pallas_call(functools.partial(share_kernel, slabs), out_shape=(jax.Sha...  2.58 us
  transfers between devices with their start and end apart: 2, of which 0 were waited for; matrix products, arithmetic and copies ran while one was open for 0% of the time, Pallas kernels for 7%

profile of v11, /device:TPU:256, one launch (start us, length us, event | category | flops | bytes accessed | tf_op | source)
XLA Modules:
  0.0 37.7 jit_solution(4896744245823902416)
XLA Ops:
  0.6 6.1 %collective-permute-start = (f32[3,8,128]{2,1,0:T(8,128)}, f32[3,8,128]{2,1,0:T(8,128)S(1)}, u32[]{:S(2)}, u32[]{:S(2)}) collective-permute-start(f32[3,8,128]{2,1,0:T(8,128)} %bitcast.14), channel_id=1, source_target_pairs={{3,5},{7,9},{11,13},{15,17},{19,21},{23,25},{27,29},{31,33},{35,37... | collective-permute-start | bytes 36872 | tf_op jit(solution)/shard_map/ppermute | solution.py:331
  6.7 0.0 copy-start
  6.7 2.6 %shard_map.59 = (f32[3,32,8,1024]{3,2,1,0:T(8,128)S(1)}, f32[3,32,8,1024]{3,2,1,0:T(8,128)S(1)}, f32[4,8,128]{2,1,0:T(8,128)S(1)}) custom-call(f32[3,8,128]{2,1,0:T(8,128)} %bitcast.15, f32[1,8,128]{2,1,0:T(8,128)} %bitcast.19, bf16[3,32,2,4,1024]{4,3,2,1,0:T(4,128)(2,1)} %bitcast.11, bf16[3,32,2,4,1024]{4,3,2,1,0:T(4,128)(2,1)} %bitcast.12), custom_call_target="tpu_custom_call" | custom-call | flops 10000000 | bytes 8000000 | tf_op jit(solution)/shard_map/pallas_call | solution.py:147
  9.4 0.0 collective-permute-done
  9.4 0.0 copy-done
  9.4 5.4 %all-gather = f32[8,3,8,128]{3,2,1,0:T(8,128)S(1)} all-gather(f32[2,3,8,128]{3,2,1,0:T(8,128)S(1)} %pad_maximum_fusion), channel_id=2, replica_groups=mesh['mesh'=128,'field'=4] {'field'}, dimensions={0}, use_global_device_ids=true | all-gather | bytes 122880 | tf_op jit(solution)/shard_map/all_gather | solution.py:333
  14.8 2.6 %shard_map.60 = (bf16[3,32,2,4,1024]{4,3,2,1,0:T(4,128)(2,1)}, f32[4,3,8,128]{3,2,1,0:T(8,128)S(1)}, f32[4,3,8,128]{3,2,1,0:T(8,128)S(1)}, f32[4,3,8,128]{3,2,1,0:T(8,128)S(1)}) custom-call(f32[4,2,3,8,128]{4,3,2,1,0:T(8,128)S(1)} %bitcast.10, f32[4,8,128]{2,1,0:T(8,128)S(1)} %get-tuple-element.9.local_ref, f32[3,32,8,1024]{3,2,1,0:T(8,128)S(1)} %get-tuple-element.10.f_ref, ...), custom_call_target="tpu_custom_call" | custom-call | flops 13000000 | bytes 7000000 | tf_op jit(solution)/shard_map/pallas_call | solution.py:307
  17.4 7.6 %collective-permute-start.1 = (f32[4,3,8,128]{3,2,1,0:T(8,128)S(1)}, f32[4,3,8,128]{3,2,1,0:T(8,128)S(1)}, u32[]{:S(2)}, u32[]{:S(2)}) collective-permute-start(f32[4,3,8,128]{3,2,1,0:T(8,128)S(1)} %get-tuple-element.14), channel_id=1, source_target_pairs={{4,9},{5,8},{6,11},{7,10},{12,17},{13,16},{14,19},{15,18},{20,25},... | collective-permute-start | bytes 147464 | tf_op jit(solution)/shard_map/ppermute | solution.py:327
  25.1 6.4 %all-gather.1 = f32[8,3,8,128]{3,2,1,0:T(8,128)S(1)} all-gather(f32[4,3,8,128]{3,2,1,0:T(8,128)S(1)} %get-tuple-element.15), channel_id=3, replica_groups={{0,4},{1,5},{2,6},{3,7},{8,12},{9,13},{10,14},{11,15},{16,20},{17,21},{..., dimensions={0}, use_global_device_ids=true | all-gather | bytes 147456 | tf_op jit(solution)/shard_map/all_gather | solution.py:338
  31.5 0.0 collective-permute-done.1
  31.5 5.6 %all-gather.2 = f32[16,3,8,128]{3,2,1,0:T(8,128)S(1)} all-gather(f32[4,3,8,128]{3,2,1,0:T(8,128)S(1)} %fusion.1), channel_id=4, replica_groups=mesh['mesh'=128,'field'=4] {'field'}, dimensions={0}, use_global_device_ids=true | all-gather | bytes 245760 | tf_op jit(solution)/shard_map/all_gather | solution.py:340
  37.1 0.6 %fusion.2 = f32[1,1,3,8,128]{4,3,2,1,0:T(8,128)} fusion(f32[4,4,3,8,128]{4,3,2,1,0:T(8,128)S(1)} %bitcast.13, s32[]{:T(128)S(6)} %add.59, s32[]{:T(128)S(6)} %select_n.26, s32[]{:T(128)S(6)} %add.58, s32[]{:T(128)S(6)} %add.57), kind=kLoop, calls=%fused_computation.5 | loop fusion | flops 9216 | bytes 61456 | tf_op jit(solution)/shard_map/add | solution.py:342
  (2 shorter events, 0.0 us)
Async XLA Ops:
  0.6 8.7 %collective-permute-start = (f32[3,8,128]{2,1,0:T(8,128)}, f32[3,8,128]{2,1,0:T(8,128)S(1)}, u32[]{:S(2)}, u32[]{:S(2)}) collective-permute-start(f32[3,8,128]{2,1,0:T(8,128)} %bitcast.14), channel_id=1, source_target_pairs={{3,5},{7,9},{11,13},{15,17},{19,21},{23,25},{27,29},{31,33},{35,37... | collective-permute-start | bytes 36872 | tf_op jit(solution)/shard_map/ppermute | solution.py:331
  6.7 2.6 %copy-start = (f32[3,1,1024]{2,1,0:T(1,128)S(1)}, f32[3,1,1024]{2,1,0:T(1,128)}, u32[]{:S(2)}) copy-start(f32[3,1,1024]{2,1,0:T(1,128)} %param.4) | copy-start | bytes 36868
  17.4 14.1 %collective-permute-start.1 = (f32[4,3,8,128]{3,2,1,0:T(8,128)S(1)}, f32[4,3,8,128]{3,2,1,0:T(8,128)S(1)}, u32[]{:S(2)}, u32[]{:S(2)}) collective-permute-start(f32[4,3,8,128]{3,2,1,0:T(8,128)S(1)} %get-tuple-element.14), channel_id=1, source_target_pairs={{4,9},{5,8},{6,11},{7,10},{12,17},{13,16},{14,19},{15,18},{20,25},... | collective-permute-start | bytes 147464 | tf_op jit(solution)/shard_map/ppermute | solution.py:327

commit v12 on v11

--- a/solution.py
+++ b/solution.py
@@ -337,9 +337,13 @@
     couples = [[i, i + PLANES] for i in range(total) if i // PLANES % 2 == 0]
     both = lax.all_gather(inner, AXES, axis=0, axis_index_groups=couples)
     inner = jnp.where(lax.axis_index("mesh") % 2 == 1, both[0], both[1])
-    parts = lax.all_gather(kept + (outer + inner), "field", axis=0)
-    parts = lax.dynamic_index_in_dim(parts, lax.axis_index("field"), 1, keepdims=False)
-    result = (parts[0] + parts[1]) + (parts[2] + parts[3])
+    mine = lax.axis_index("field")
+    shares = kept + (outer + inner)
+    others = lax.dynamic_slice_in_dim(jnp.concatenate([shares, shares]), mine + 1, PLANES - 1, 0)
+    parts = lax.all_gather(others, "field", axis=0)
+    result = lax.dynamic_index_in_dim(shares, mine, 0, keepdims=False)
+    for d in range(1, PLANES):
+        result = result + lax.dynamic_index_in_dim(parts[:, PLANES - 1 - d], (mine + d) % PLANES, 0, keepdims=False)
     return new_fields.reshape(fields.shape), result.reshape(velocity.shape)
 
 

time: 38.5 us -> 38.5 us (level)
  no operation moved by 1% of the time
where the time goes in v12:
time: 38.5 us; the launch traced here: 37.8 us
  blocking collectives  17.3 us (45%)
  starting transfers between devices  13.7 us (36%)
  Pallas kernels  5.18 us (13%)
  between operations  0.79 us (2%)
  other arithmetic  0.67 us (2%)
    ppermute x1, starting transfers between devices, exchange(): return lax.ppermute(x, AXES, pairs + [(b, a) for a, b in pairs])  7.65 us
    all_gather x1, blocking collectives, body(): both = lax.all_gather(inner, AXES, axis=0, axis_index_groups=couples)  6.44 us
    ppermute x1, starting transfers between devices, body(): lax.ppermute(own, AXES, [(i, i + 2) for i in ends] + [(i + 1, i) for i in...  6.1 us
    all_gather x1, blocking collectives, body(): parts = lax.all_gather(others, 'field', axis=0)  5.47 us
    all_gather x1, blocking collectives, body(): near = lax.all_gather(jnp.stack([own, edge]), 'field', axis=0)  5.42 us
    pallas_call x1, Pallas kernels, relax(): pl.pallas_call(relax_kernel, out_shape=(jax.ShapeDtypeStruct(flat, f32),...  2.61 us
    pallas_call x1, Pallas kernels, share(): pl.pallas_call(functools.partial(share_kernel, slabs), out_shape=(jax.Sha...  2.58 us
  transfers between devices with their start and end apart: 2, of which 0 were waited for; matrix products, arithmetic and copies ran while one was open for 0% of the time, Pallas kernels for 7%

profile of v12, /device:TPU:256, one launch (start us, length us, event | category | flops | bytes accessed | tf_op | source)
XLA Modules:
  0.0 37.8 jit_solution(6937039082327268978)
XLA Ops:
  0.6 6.1 %collective-permute-start = (f32[3,8,128]{2,1,0:T(8,128)}, f32[3,8,128]{2,1,0:T(8,128)S(1)}, u32[]{:S(2)}, u32[]{:S(2)}) collective-permute-start(f32[3,8,128]{2,1,0:T(8,128)} %bitcast.17), channel_id=1, source_target_pairs={{3,5},{7,9},{11,13},{15,17},{19,21},{23,25},{27,29},{31,33},{35,37... | collective-permute-start | bytes 36872 | tf_op jit(solution)/shard_map/ppermute | solution.py:331
  6.7 0.0 copy-start
  6.7 2.6 %shard_map.59 = (f32[3,32,8,1024]{3,2,1,0:T(8,128)S(1)}, f32[3,32,8,1024]{3,2,1,0:T(8,128)S(1)}, f32[4,8,128]{2,1,0:T(8,128)S(1)}) custom-call(f32[3,8,128]{2,1,0:T(8,128)} %bitcast.18, f32[1,8,128]{2,1,0:T(8,128)} %bitcast.25, bf16[3,32,2,4,1024]{4,3,2,1,0:T(4,128)(2,1)} %bitcast.14, bf16[3,32,2,4,1024]{4,3,2,1,0:T(4,128)(2,1)} %bitcast.15), custom_call_target="tpu_custom_call" | custom-call | flops 10000000 | bytes 8000000 | tf_op jit(solution)/shard_map/pallas_call | solution.py:147
  9.4 0.0 collective-permute-done
  9.4 0.0 copy-done
  9.4 5.4 %all-gather = f32[8,3,8,128]{3,2,1,0:T(8,128)S(1)} all-gather(f32[2,3,8,128]{3,2,1,0:T(8,128)S(1)} %pad_maximum_fusion), channel_id=2, replica_groups=mesh['mesh'=128,'field'=4] {'field'}, dimensions={0}, use_global_device_ids=true | all-gather | bytes 122880 | tf_op jit(solution)/shard_map/all_gather | solution.py:333
  14.8 2.6 %shard_map.60 = (bf16[3,32,2,4,1024]{4,3,2,1,0:T(4,128)(2,1)}, f32[4,3,8,128]{3,2,1,0:T(8,128)S(1)}, f32[4,3,8,128]{3,2,1,0:T(8,128)S(1)}, f32[4,3,8,128]{3,2,1,0:T(8,128)S(1)}) custom-call(f32[4,2,3,8,128]{4,3,2,1,0:T(8,128)S(1)} %bitcast.13, f32[4,8,128]{2,1,0:T(8,128)S(1)} %get-tuple-element.9.local_ref, f32[3,32,8,1024]{3,2,1,0:T(8,128)S(1)} %get-tuple-element.10.f_ref, ...), custom_call_target="tpu_custom_call" | custom-call | flops 13000000 | bytes 7000000 | tf_op jit(solution)/shard_map/pallas_call | solution.py:307
  17.4 7.6 %collective-permute-start.1 = (f32[4,3,8,128]{3,2,1,0:T(8,128)S(1)}, f32[4,3,8,128]{3,2,1,0:T(8,128)S(1)}, u32[]{:S(2)}, u32[]{:S(2)}) collective-permute-start(f32[4,3,8,128]{3,2,1,0:T(8,128)S(1)} %get-tuple-element.14), channel_id=1, source_target_pairs={{4,9},{5,8},{6,11},{7,10},{12,17},{13,16},{14,19},{15,18},{20,25},... | collective-permute-start | bytes 147464 | tf_op jit(solution)/shard_map/ppermute | solution.py:327
  25.1 6.4 %all-gather.1 = f32[8,3,8,128]{3,2,1,0:T(8,128)S(1)} all-gather(f32[4,3,8,128]{3,2,1,0:T(8,128)S(1)} %get-tuple-element.15), channel_id=3, replica_groups={{0,4},{1,5},{2,6},{3,7},{8,12},{9,13},{10,14},{11,15},{16,20},{17,21},{..., dimensions={0}, use_global_device_ids=true | all-gather | bytes 147456 | tf_op jit(solution)/shard_map/all_gather | solution.py:338
  31.6 0.0 collective-permute-done.1
  31.6 5.5 %all-gather.2 = f32[12,3,8,128]{3,2,1,0:T(8,128)S(1)} all-gather(f32[3,3,8,128]{3,2,1,0:T(8,128)S(1)} %fusion.2), channel_id=4, replica_groups=mesh['mesh'=128,'field'=4] {'field'}, dimensions={0}, use_global_device_ids=true | all-gather | bytes 184320 | tf_op jit(solution)/shard_map/all_gather | solution.py:343
  37.1 0.6 %add_add_fusion = f32[3,1,1024]{2,1,0:T(1,128)} fusion(f32[3,1,1024]{2,1,0:T(1,128)S(1)} %bitcast.22, f32[3,1,1024]{2,1,0:T(1,128)S(1)} %bitcast.23, f32[3,1,1024]{2,1,0:T(1,128)S(1)} %bitcast.20, f32[3,1,1024]{2,1,0:T(1,128)S(1)} %bitcast.21), kind=kLoop, calls=%fused_computation.7 | loop fusion | flops 9216 | bytes 61440 | tf_op jit(solution)/shard_map/add | solution.py:346
  (7 shorter events, 0.1 us)
Async XLA Ops:
  0.6 8.7 %collective-permute-start = (f32[3,8,128]{2,1,0:T(8,128)}, f32[3,8,128]{2,1,0:T(8,128)S(1)}, u32[]{:S(2)}, u32[]{:S(2)}) collective-permute-start(f32[3,8,128]{2,1,0:T(8,128)} %bitcast.17), channel_id=1, source_target_pairs={{3,5},{7,9},{11,13},{15,17},{19,21},{23,25},{27,29},{31,33},{35,37... | collective-permute-start | bytes 36872 | tf_op jit(solution)/shard_map/ppermute | solution.py:331
  6.7 2.6 %copy-start = (f32[3,1,1024]{2,1,0:T(1,128)S(1)}, f32[3,1,1024]{2,1,0:T(1,128)}, u32[]{:S(2)}) copy-start(f32[3,1,1024]{2,1,0:T(1,128)} %param.4) | copy-start | bytes 36868
  17.4 14.2 %collective-permute-start.1 = (f32[4,3,8,128]{3,2,1,0:T(8,128)S(1)}, f32[4,3,8,128]{3,2,1,0:T(8,128)S(1)}, u32[]{:S(2)}, u32[]{:S(2)}) collective-permute-start(f32[4,3,8,128]{3,2,1,0:T(8,128)S(1)} %get-tuple-element.14), channel_id=1, source_target_pairs={{4,9},{5,8},{6,11},{7,10},{12,17},{13,16},{14,19},{15,18},{20,25},... | collective-permute-start | bytes 147464 | tf_op jit(solution)/shard_map/ppermute | solution.py:327
